TPU v7x, 32 devices: a whole 2x2x4 slice. The times are simulated.
32 devices in a mesh: seq: 16 (over z, y, core), head: 2 (over x).
Axes of the slice: x: 2, y: 2, z: 4, core: 2. Of those that a mesh axis runs over, the one named last changes fastest.
Arguments:
- prefill_input: bfloat16 [4096, 8192], P('seq', 'head'), may hold values from -6 to 6
- prefill_step: float32 [4096, 128], P('seq', 'head'), may hold values from 0 to 4096, as said below
- write_proj: bfloat16 [4096, 1024], P('seq', 'head'), may hold values from -2.5 to 2.5
- read_proj: bfloat16 [4096, 1024], P('seq', 'head'), may hold values from -0.5 to 0.5
- decay_rate: float32 [128], P('head'), may hold values from 0 to 1, as said below
- skip_gain: float32 [128], P('head'), may hold values from 0.5 to 2
- resident_state: bfloat16 [16, 128, 64, 128], P('seq', 'head'), may hold values from -6 to 6
- owner_slot: int32 [16], replicated, may hold values from 0 to 15, each once
- draft_ids: int32 [16, 8], replicated, may hold values from 0 to 15
- accepted_len: int32 [16], replicated, may hold values from 0 to 8
- draft_input: bfloat16 [256, 8192], P('seq', 'head'), may hold values from -6 to 6
- draft_gate: bfloat16 [256, 8192], P('seq', 'head'), may hold values from -6 to 6
- draft_write: bfloat16 [256, 1024], P('seq', 'head'), may hold values from -2.5 to 2.5
- draft_read: bfloat16 [256, 1024], P('seq', 'head'), may hold values from -0.5 to 0.5
- draft_step: float32 [256, 128], P('seq', 'head'), may hold values from 0.05 to 1
- norm_gain: float32 [8192], P('head'), may hold values from 0.5 to 1.5
- out_weight: bfloat16 [8192, 8192], P('head', 'seq'), may hold values from -0.0625 to 0.0625
Outputs:
- prefill_out: bfloat16 [4096, 8192], P('seq', 'head')
- new_state: bfloat16 [16, 128, 64, 128], P('seq', 'head')
- verify_out: bfloat16 [128, 8192], P('head', 'seq')
- prompt_state: bfloat16 [128, 8192], P('head', 'seq')
Inputs may be any that keep to these rules, and one draw needn't show every extreme that they name: owner_slot holds every slot once. `decay_rate`: positive. `prefill_step`: positive.
All inputs are finite; a program needn't handle non-finite values.
Results may differ from a plain program's by a relative error of at most 0.005.
Values may be sent and summed in bfloat16 or wider, within the bound.
No kernel may reach another device: no remote copies, remote signals or barrier semaphores. Data moves between devices by JAX's collectives and lax.ppermute only.
A program may use at most 128 MiB of HBM per device.

v0:
```python
import jax
import jax.numpy as jnp
from jax import lax
from jax.sharding import PartitionSpec as P

HEAD_DIM = 64
STATE_SIZE = 128
BLOCK_LEN = 256


PRECISE = lax.Precision.HIGHEST
EPSILON = 1e-05


def carried_in(value, axis, combine, identity):
    peers, here = (lax.axis_size(axis), lax.axis_index(axis))
    everything = jax.tree.map(lambda part: lax.all_gather(part, axis), value)
    start = jax.tree.map(
        lambda part, zero: jnp.broadcast_to(jnp.asarray(zero, part.dtype), part.shape),
        value,
        identity,
    )

    def turn(k, before):
        reached = k < here
        new = combine(before, jax.tree.map(lambda part: part[k], everything))
        return jax.tree.map(lambda a, b: jnp.where(reached, a, b), new, before)

    return lax.fori_loop(0, peers, turn, start)


def from_root(block, axis, source):
    block = jnp.where(lax.axis_index(axis) == source, block, jnp.zeros_like(block))
    return lax.psum(block, axis)


def local_block(block_input, block_step, block_write, block_read, rate, groups):
    span_len = block_input.shape[0]
    head_total = rate.shape[0]
    per_group = head_total // groups
    log_decay = -block_step * rate[None, :]
    running = jnp.cumsum(log_decay, axis=0)
    write_rows = block_write.reshape(span_len, groups, STATE_SIZE)
    read_rows = block_read.reshape(span_len, groups, STATE_SIZE)
    scores = jnp.einsum("tgn,jgn->gtj", read_rows, write_rows, preferred_element_type=jnp.float32)
    position = jnp.arange(span_len, dtype=jnp.int32)
    causal = position[:, None] >= position[None, :]
    running_t = running.T.reshape(groups, per_group, span_len)
    log_gap = running_t[:, :, :, None] - running_t[:, :, None, :]
    decayed = jnp.exp(jnp.where(causal[None, None], log_gap, -jnp.inf))
    step_t = block_step.T.reshape(groups, per_group, 1, span_len)
    mixing = (scores[:, None] * decayed * step_t).astype(jnp.bfloat16)
    incoming_vectors = block_input.reshape(span_len, groups, per_group, HEAD_DIM)
    intra_part = jnp.einsum(
        "gktj,jgkp->tgkp", mixing, incoming_vectors, preferred_element_type=jnp.float32
    )
    intra_part = intra_part.reshape(span_len, head_total, HEAD_DIM)
    to_end = jnp.exp(running[-1][None, :] - running) * block_step
    weighted = (
        incoming_vectors.astype(jnp.float32)
        * to_end.reshape(span_len, groups, per_group)[..., None]
    ).astype(jnp.bfloat16)
    local_state = jnp.einsum(
        "tgkp,tgn->gkpn", weighted, write_rows, preferred_element_type=jnp.float32
    )
    return (intra_part, local_state.reshape(head_total, HEAD_DIM, STATE_SIZE), running)


def read_state(block_read, state_now, running, groups):
    span_len = block_read.shape[0]
    head_total = state_now.shape[0]
    per_group = head_total // groups
    grouped = state_now.astype(jnp.bfloat16).reshape(groups, per_group, HEAD_DIM, STATE_SIZE)
    read_rows = block_read.reshape(span_len, groups, STATE_SIZE)
    inter_part = jnp.einsum(
        "tgn,gkpn->tgkp", read_rows, grouped, preferred_element_type=jnp.float32
    )
    return inter_part.reshape(span_len, head_total, HEAD_DIM) * jnp.exp(running)[:, :, None]


def verify_slot(
    start_state,
    rows_input,
    rows_gate,
    rows_write,
    rows_read,
    rows_step,
    kept_len,
    rate,
    skip,
    gain,
    groups,
):
    span_len = rows_input.shape[0]
    head_total = start_state.shape[0]
    per_group = head_total // groups
    log_decay = -rows_step * rate[None, :]
    running = jnp.cumsum(log_decay, axis=0)
    incoming_vectors = rows_input.astype(jnp.float32).reshape(span_len, groups, per_group, HEAD_DIM)
    write_rows = rows_write.astype(jnp.float32).reshape(span_len, groups, STATE_SIZE)
    read_rows = rows_read.astype(jnp.float32).reshape(span_len, groups, STATE_SIZE)
    scores = jnp.einsum("tgn,jgn->gtj", read_rows, write_rows, precision=PRECISE)
    position = jnp.arange(span_len, dtype=jnp.int32)
    causal = position[:, None] >= position[None, :]
    running_t = running.T.reshape(groups, per_group, span_len)
    log_gap = running_t[:, :, :, None] - running_t[:, :, None, :]
    decayed = jnp.exp(jnp.where(causal[None, None], log_gap, -jnp.inf))
    mixing = scores[:, None] * decayed * rows_step.T.reshape(groups, per_group, 1, span_len)
    intra_part = jnp.einsum("gktj,jgkp->tgkp", mixing, incoming_vectors, precision=PRECISE)
    grouped = start_state.reshape(groups, per_group, HEAD_DIM, STATE_SIZE)
    inter_part = jnp.einsum("tgn,gkpn->tgkp", read_rows, grouped, precision=PRECISE)
    inter_part = inter_part * jnp.exp(running).reshape(span_len, groups, per_group)[..., None]
    direct = (
        intra_part
        + inter_part
        + skip.reshape(groups, per_group)[None, :, :, None] * incoming_vectors
    )
    gates = rows_gate.astype(jnp.float32).reshape(span_len, groups, per_group, HEAD_DIM)
    gated = direct * jax.nn.silu(gates)
    flattened = gated.reshape(span_len, groups, per_group * HEAD_DIM)
    mean_square = jnp.mean(flattened * flattened, axis=2, keepdims=True)
    hidden = (
        flattened
        * lax.rsqrt(mean_square + EPSILON)
        * gain.reshape(groups, per_group * HEAD_DIM)[None]
    )
    hidden = hidden.astype(jnp.bfloat16).reshape(span_len, head_total * HEAD_DIM)
    is_live = position < kept_len
    reach_log = jnp.sum(jnp.where(is_live[:, None], log_decay, 0.0), axis=0)
    tail_weight = (
        jnp.exp(jnp.where(is_live[:, None], reach_log[None, :] - running, -jnp.inf)) * rows_step
    )
    weighted = incoming_vectors * tail_weight.reshape(span_len, groups, per_group)[..., None]
    added = jnp.einsum("tgkp,tgn->gkpn", weighted, write_rows, precision=PRECISE)
    added = added.reshape(head_total, HEAD_DIM, STATE_SIZE)
    new_state = (start_state * jnp.exp(reach_log)[:, None, None] + added).astype(jnp.bfloat16)
    return (hidden, new_state)


def combine(earlier, later):
    return (earlier[0] + later[0], earlier[1] * jnp.exp(later[0])[:, None, None] + later[1])


def on_device(
    prefill_input,
    prefill_step,
    write_proj,
    read_proj,
    decay_rate,
    skip_gain,
    resident_state,
    owner_slot,
    draft_ids,
    accepted_len,
    draft_input,
    draft_gate,
    draft_write,
    draft_read,
    draft_step,
    norm_gain,
    out_weight,
):
    local_heads = decay_rate.shape[0]
    local_groups = write_proj.shape[1] // STATE_SIZE
    blocks = prefill_input.shape[0] // BLOCK_LEN
    incoming_vectors = prefill_input.reshape(blocks, BLOCK_LEN, local_heads * HEAD_DIM)
    steps = prefill_step.reshape(blocks, BLOCK_LEN, local_heads)
    writes = write_proj.reshape(blocks, BLOCK_LEN, local_groups * STATE_SIZE)
    reads = read_proj.reshape(blocks, BLOCK_LEN, local_groups * STATE_SIZE)
    zero_state = jnp.zeros((local_heads, HEAD_DIM, STATE_SIZE), jnp.float32)
    zero_log = jnp.zeros((local_heads,), jnp.float32)

    def first_pass(carry_pair, block_data):
        total_log, aggregate_memory_tensor = carry_pair
        block_input, block_step, block_write, block_read = block_data
        intra_part, local_state, running = local_block(
            block_input, block_step, block_write, block_read, decay_rate, local_groups
        )
        aggregate_memory_tensor = (
            aggregate_memory_tensor * jnp.exp(running[-1])[:, None, None] + local_state
        )
        return (
            (total_log + running[-1], aggregate_memory_tensor),
            (intra_part, local_state, running),
        )

    (device_log, device_state), (intra_all, local_all, running_all) = lax.scan(
        first_pass, (zero_log, zero_state), (incoming_vectors, steps, writes, reads)
    )
    enter_log, entering = carried_in(
        (device_log, device_state), "seq", combine, (zero_log, zero_state)
    )

    def finish_block(state_now, block_data):
        intra_part, local_state, running, block_input, block_read = block_data
        inter_part = read_state(block_read, state_now, running, local_groups)
        skip_part = skip_gain[None, :, None] * block_input.reshape(
            BLOCK_LEN, local_heads, HEAD_DIM
        ).astype(jnp.float32)
        output = (intra_part + inter_part + skip_part).astype(jnp.bfloat16)
        state_now = state_now * jnp.exp(running[-1])[:, None, None] + local_state
        return (state_now, output.reshape(BLOCK_LEN, local_heads * HEAD_DIM))

    leaving, output_blocks = lax.scan(
        finish_block, entering, (intra_all, local_all, running_all, incoming_vectors, reads)
    )
    prefill_out = output_blocks.reshape(blocks * BLOCK_LEN, local_heads * HEAD_DIM)
    seq_count = lax.axis_size("seq")
    sequence_index = lax.axis_index("seq")
    prompt_state = from_root(leaving.astype(jnp.bfloat16), "seq", seq_count - 1)
    slice_width = HEAD_DIM * STATE_SIZE // seq_count
    flat_state = prompt_state.reshape(local_heads, HEAD_DIM * STATE_SIZE)
    state_slice = lax.dynamic_slice_in_dim(flat_state, sequence_index * slice_width, slice_width, 1)
    slot_index = jnp.arange(owner_slot.shape[0], dtype=jnp.int32)
    request = jnp.sum(jnp.where(owner_slot == sequence_index, slot_index, 0))
    picked = slot_index == request
    chosen = jnp.sum(jnp.where(picked[:, None], draft_ids, 0), axis=0)
    kept_len = jnp.sum(jnp.where(picked, accepted_len, 0))
    start_state = jnp.where(
        owner_slot[0] == sequence_index, prompt_state, resident_state[0]
    ).astype(jnp.float32)
    selector = chosen[:, None] == jnp.arange(draft_input.shape[0], dtype=jnp.int32)[None, :]
    pick_low = selector.astype(jnp.bfloat16)
    pick_high = selector.astype(jnp.float32)
    rows_input = jnp.dot(pick_low, draft_input, preferred_element_type=jnp.float32).astype(
        jnp.bfloat16
    )
    rows_gate = jnp.dot(pick_low, draft_gate, preferred_element_type=jnp.float32).astype(
        jnp.bfloat16
    )
    rows_write = jnp.dot(pick_low, draft_write, preferred_element_type=jnp.float32).astype(
        jnp.bfloat16
    )
    rows_read = jnp.dot(pick_low, draft_read, preferred_element_type=jnp.float32).astype(
        jnp.bfloat16
    )
    rows_step = jnp.dot(pick_high, draft_step, precision=PRECISE)
    hidden, new_state = verify_slot(
        start_state,
        rows_input,
        rows_gate,
        rows_write,
        rows_read,
        rows_step,
        kept_len,
        decay_rate,
        skip_gain,
        norm_gain,
        local_groups,
    )
    partial_out = jnp.dot(
        lax.all_gather(hidden, "seq", axis=0, tiled=True),
        out_weight,
        preferred_element_type=jnp.float32,
    )
    verify_out = lax.psum_scatter(partial_out, "head", scatter_dimension=0, tiled=True).astype(
        jnp.bfloat16
    )
    return (prefill_out, new_state[None], verify_out, state_slice)


def solution(mesh):
    return jax.shard_map(
        on_device,
        mesh=mesh,
        in_specs=(
            P("seq", "head"),
            P("seq", "head"),
            P("seq", "head"),
            P("seq", "head"),
            P("head"),
            P("head"),
            P("seq", "head", None, None),
            P(),
            P(),
            P(),
            P("seq", "head"),
            P("seq", "head"),
            P("seq", "head"),
            P("seq", "head"),
            P("seq", "head"),
            P("head"),
            P("head", "seq"),
        ),
        out_specs=(
            P("seq", "head"),
            P("seq", "head", None, None),
            P("head", "seq"),
            P("head", "seq"),
        ),
        check_vma=False,
    )
```

profile of v0, /device:TPU:0, one launch (start us, length us, event | category | flops | bytes accessed | tf_op | source)
XLA Modules:
  0.0 391.7 jit_solution(461719430640332738)
XLA Ops:
  10.8 3.3 copy.58
  22.8 23.0 %all-gather = f32[16,1,64]{2,1,0:T(1,128)S(1)} all-gather(f32[1,1,64]{2,1,0:T(1,128)S(1)} %bitcast.165), channel_id=1, replica_groups=mesh['seq'=16,'head'=2] {'seq'}, dimensions={0}, use_global_device_ids=true | all-gather | bytes 4352 | tf_op jit(solution)/shard_map/all_gather | solution.py:17
  46.7 142.7 %all-gather.4.cloned.1.call-done = f32[16,64,64,128]{3,2,1,0:T(8,128)} async-done(((f32[1,64,64,128]{3,2,1,0:T(8,128)}), f32[16,64,64,128]{3,2,1,0:T(8,128)}) %all-gather.4.cloned.1.call-update) | async-done | bytes 33554448 | tf_op jit(solution)/shard_map/all_gather | solution.py:17
  189.5 34.0 %while.9 = (s32[]{:T(128)}, f32[64,64,128]{2,1,0:T(8,128)S(1)}, s32[]{:T(128)}, f32[16,64]{1,0:T(8,128)S(1)}, f32[16,64,64,128]{3,2,1,0:T(8,128)}, /*index=5*/s32[]{:T(128)}, s32[]{:T(128)}) while((s32[]{:T(128)}, f32[64,64,128]{2,1,0:T(8,128)S(1)}, s32[]{:T(128)}, f32[16,64]{1,0:T(8,128)S(1)}, f32[16,64,64,128]{3,2,1,0:T(8,128)}, ...), condition=%wide.region_3.4_spmd.clone, body=%wide.region_2.3_spmd.clone.sunk | while | flops 2097156 | bytes 6292329 | solution.py:29
  189.5 2.1 fusion.78
  191.6 2.1 fusion.78
  193.7 2.1 fusion.78
  195.8 2.1 fusion.78
  198.0 2.1 fusion.78
  200.1 2.1 fusion.78
  202.2 2.1 fusion.78
  204.3 2.1 fusion.78
  206.5 2.1 fusion.78
  208.6 2.1 fusion.78
  215.0 2.1 fusion.78
  217.1 2.1 fusion.78
  223.4 2.9 fusion.20
  229.1 3.2 fusion.21
  232.4 87.5 %all-reduce.2.cloned.1.call-done = bf16[64,64,128]{2,1,0:T(8,128)(2,1)} async-done(((bf16[64,64,128]{2,1,0:T(8,128)(2,1)}), bf16[64,64,128]{2,1,0:T(8,128)(2,1)}) %all-reduce.2.cloned.1.call-update) | async-done | bytes 1048592 | tf_op jit(solution)/shard_map/psum | solution.py:34
  319.9 3.3 fusion.13
  328.8 34.7 %all-gather.6.cloned.1.call-done = bf16[128,4096]{1,0:T(8,128)(2,1)} async-done(((bf16[8,4096]{1,0:T(8,128)(2,1)}), bf16[128,4096]{1,0:T(8,128)(2,1)}) %all-gather.6.cloned.1.call-update) | async-done | bytes 1048592 | tf_op jit(solution)/shard_map/all_gather | solution.py:252
  363.5 4.0 %fusion.61 = f32[128,512]{1,0:T(8,128)} fusion(bf16[128,4096]{1,0:T(8,128)(2,1)} %all-gather.6.cloned.1.call-done, bf16[4096,512]{1,0:T(8,128)(2,1)} %param.35), kind=kOutput, calls=%fused_computation.102 | convolution fusion | flops 536870912 | bytes 5505024 | tf_op jit(solution)/shard_map/dot_general | solution.py:251
  367.5 7.2 %fusion.1 = f32[4,16,256,64]{2,3,1,0:T(8,128)} fusion(bf16[256,4,16,64]{0,3,2,1:T(8,128)(2,1)} %bitcast.147, f32[4,16,256]{2,1,0:T(8,128)S(1)} %bitcast.157, f32[4,16,256]{2,1,0:T(8,128)S(1)} %copy-done.12, f32[4,256,256]{2,1,0:T(8,128)S(1)} %fusion.22, pred[256,256]{1,0:T(8,128)(4,1)} %iota_compare_fusion), kind=kOutput, calls=%fused_computation.4 | convolution fusion | flops 557842432 | bytes 7536640 | tf_op jit(solution)/shard_map/while/body/eval_jaxpr/gktj,jgkp->tgkp/dot_general | solution.py:54
  379.4 2.9 copy.73
  (137 shorter events, 37.3 us)
Async XLA Ops:
  7.2 39.1 %copy-start = (bf16[16,4096]{1,0:T(8,128)(2,1)S(1)}, bf16[16,4096]{1,0:T(8,128)(2,1)}, u32[]{:S(2)}) copy-start(bf16[16,4096]{1,0:T(8,128)(2,1)} %param.29) | copy-start | bytes 393220
  7.2 182.3 %all-gather.4.cloned.1.call-start = ((), (), s32[]{:S(2)}) async-start(), calls=%async_computation.1 | async-start | bytes 35651584 | tf_op jit(solution)/shard_map/all_gather | solution.py:17
  10.8 3.3 copy-start.7
  18.4 4.0 %copy-start.16 = (s32[16,8]{0,1:T(8,128)S(1)}, s32[16,8]{0,1:T(8,128)}, u32[]{:S(2)}) copy-start(s32[16,8]{0,1:T(8,128)} %param.27) | copy-start | bytes 1540
  18.4 4.1 %copy-start.19 = (f32[64]{0:T(128)S(1)}, f32[64]{0:T(128)}, u32[]{:S(2)}) copy-start(f32[64]{0:T(128)} %param.23) | copy-start | bytes 772
  18.4 4.1 %copy-start.22 = (f32[16,64]{1,0:T(8,128)S(1)}, f32[16,64]{1,0:T(8,128)}, u32[]{:S(2)}) copy-start(f32[16,64]{1,0:T(8,128)} %param.33) | copy-start | bytes 12292
  18.5 27.4 %copy-start.20 = (bf16[16,512]{1,0:T(8,128)(2,1)S(1)}, bf16[16,512]{1,0:T(8,128)(2,1)}, u32[]{:S(2)}) copy-start(bf16[16,512]{1,0:T(8,128)(2,1)} %param.31) | copy-start | bytes 49156
  18.5 27.6 %copy-start.21 = (bf16[16,512]{1,0:T(8,128)(2,1)S(1)}, bf16[16,512]{1,0:T(8,128)(2,1)}, u32[]{:S(2)}) copy-start(bf16[16,512]{1,0:T(8,128)(2,1)} %param.32) | copy-start | bytes 49156
  18.5 28.0 %copy-start.11 = (bf16[16,4096]{1,0:T(8,128)(2,1)S(1)}, bf16[16,4096]{1,0:T(8,128)(2,1)}, u32[]{:S(2)}) copy-start(bf16[16,4096]{1,0:T(8,128)(2,1)} %param.30) | copy-start | bytes 393220
  18.5 301.4 %all-reduce.2.cloned.1.call-start = ((), (), s32[]{:S(2)}) async-start(), calls=%async_computation.2 | async-start | bytes 2097152 | tf_op jit(solution)/shard_map/psum | solution.py:34
  223.4 5.5 %copy-start.17 = (f32[64]{0:T(128)S(1)}, f32[64]{0:T(128)}, u32[]{:S(2)}) copy-start(f32[64]{0:T(128)} %param.24) | copy-start | bytes 772
  226.4 137.1 %all-gather.6.cloned.1.call-start = ((), (), s32[]{:S(2)}) async-start(), calls=%async_computation.3 | async-start | bytes 1114112 | tf_op jit(solution)/shard_map/all_gather | solution.py:252
  232.4 91.7 %copy-start.13 = (f32[64,8]{1,0:T(8,128)S(1)}, f32[64,8]{1,0:T(8,128)}, u32[]{:S(2)}) copy-start(f32[64,8]{1,0:T(8,128)} %copy.85) | copy-start | bytes 6148
  232.4 91.7 %copy-start.14 = (f32[64,8]{1,0:T(8,128)S(1)}, f32[64,8]{1,0:T(8,128)}, u32[]{:S(2)}) copy-start(f32[64,8]{1,0:T(8,128)} %copy.83) | copy-start | bytes 6148
  232.4 91.8 %copy-start.25 = (pred[8,8]{1,0:T(8,128)(4,1)S(1)}, pred[8,8]{1,0:T(8,128)(4,1)}, u32[]{:S(2)}) copy-start(pred[8,8]{1,0:T(8,128)(4,1)} %iota_compare_fusion.1) | copy-start | bytes 196
  325.8 57.8 %reduce-scatter.2.cloned.1.call-start = ((), (), s32[]{:S(2)}) async-start(), calls=%async_computation.4 | async-start | bytes 393216 | tf_op jit(solution)/shard_map/reduce_scatter | solution.py:256
  328.8 38.7 %copy-start.10 = (f32[256,64]{0,1:T(8,128)S(1)}, f32[256,64]{0,1:T(8,128)}, u32[]{:S(2)}) copy-start(f32[256,64]{0,1:T(8,128)} %param.20) | copy-start | bytes 196612
  328.8 38.7 %copy-start.12 = (f32[4,16,256]{2,1,0:T(8,128)S(1)}, f32[4,16,256]{2,1,0:T(8,128)}, u32[]{:S(2)}) copy-start(f32[4,16,256]{2,1,0:T(8,128)} %reduce_window_sum.39) | copy-start | bytes 196612
  367.5 7.2 %copy-start.8 = (bf16[256,512]{1,0:T(8,128)(2,1)S(1)}, bf16[256,512]{1,0:T(8,128)(2,1)}, u32[]{:S(2)}) copy-start(bf16[256,512]{1,0:T(8,128)(2,1)} %param.22) | copy-start | bytes 786436
  367.5 7.3 %copy-start.18 = (f32[64]{0:T(128)S(1)}, f32[64]{0:T(128)}, u32[]{:S(2)}) copy-start(f32[64]{0:T(128)} %param.24) | copy-start | bytes 772
  375.1 2.8 copy-start.4
  375.1 2.7 copy-start.9
  379.4 2.9 copy-start.6
  379.4 5.8 %copy-start.1 = (bf16[16,4096]{1,0:T(8,128)(2,1)S(1)}, bf16[16,4096]{1,0:T(8,128)(2,1)}, u32[]{:S(2)}) copy-start(bf16[16,4096]{1,0:T(8,128)(2,1)} %param.29) | copy-start | bytes 393220
  (6 other events, 9.5 us)
Sparse Core Ops, SparseCore 0:
  18.6 170.7 all-gather.3
  226.5 93.3 all-reduce.1
  325.9 37.4 all-gather.5
  367.6 10.5 reduce-scatter.1
where the time goes:
time: 393 us; the launch traced here: 392 us
  waiting for transfers between devices  265 us (67%)
  other arithmetic  53 us (13%)
  blocking collectives  23 us (6%)
  matrix products  19.8 us (5%)
  local copies, waits for them, and re-layouts  15.8 us (4%)
  between operations  14.2 us (4%)
    all_gather x1, waiting for transfers between devices, carried_in(): everything = jax.tree.map(lambda part: lax.all_gather(part, axis), value)  143 us
    psum x1, waiting for transfers between devices, from_root(): return lax.psum(block, axis)  87.5 us
    all_gather x1, waiting for transfers between devices, on_device(): lax.all_gather(hidden, 'seq', axis=0, tiled=True)  34.7 us
    select_n x16, other arithmetic, turn(): return jax.tree.map(lambda a, b: jnp.where(reached, a, b), new, before)  33.2 us
    all_gather x1, blocking collectives, carried_in(): everything = jax.tree.map(lambda part: lax.all_gather(part, axis), value)  23 us
    unnamed x55, local copies, waits for them, and re-layouts  11.5 us
  transfers between devices with their start and end apart: 4, of which 3 were waited for; matrix products, arithmetic and copies ran while one was open for 7% of the time, Pallas kernels for 0%

commit v1 on v0

--- a/solution.py
+++ b/solution.py
@@ -12,26 +12,130 @@
 EPSILON = 1e-05
 
 
-def carried_in(value, axis, combine, identity):
-    peers, here = (lax.axis_size(axis), lax.axis_index(axis))
-    everything = jax.tree.map(lambda part: lax.all_gather(part, axis), value)
-    start = jax.tree.map(
-        lambda part, zero: jnp.broadcast_to(jnp.asarray(zero, part.dtype), part.shape),
-        value,
-        identity,
-    )
-
-    def turn(k, before):
-        reached = k < here
-        new = combine(before, jax.tree.map(lambda part: part[k], everything))
-        return jax.tree.map(lambda a, b: jnp.where(reached, a, b), new, before)
-
-    return lax.fori_loop(0, peers, turn, start)
-
-
-def from_root(block, axis, source):
-    block = jnp.where(lax.axis_index(axis) == source, block, jnp.zeros_like(block))
-    return lax.psum(block, axis)
+def tree_factors(count):
+    factors = []
+    if count > 1:
+        factors.append(2)
+        count //= 2
+    inner = 1
+    while inner * inner * 4 <= count:
+        inner *= 2
+    for factor in (inner, count // inner):
+        if factor > 1:
+            factors.append(factor)
+    return factors
+
+
+def tree_stages(count):
+    stages, stride = [], 1
+    for factor in tree_factors(count):
+        stages.append((factor, stride))
+        stride *= factor
+    assert stride == count
+    return stages
+
+
+def partner(index, stage, offset):
+    factor, stride = stage
+    return index ^ (offset * stride)
+
+
+def swap(value, axis, stage, offset):
+    count = lax.axis_size(axis)
+    return lax.ppermute(
+        value, axis, [(source, partner(source, stage, offset)) for source in range(count)]
+    )
+
+
+def in_order(parts, place):
+    if len(parts) == 2:
+        first = jnp.where(place == 0, parts[0], parts[1])
+        second = jnp.where(place == 0, parts[1], parts[0])
+        return jnp.stack([first, second])
+    stacked = jnp.stack(parts)
+    order = place ^ jnp.arange(len(parts), dtype=jnp.int32)
+    return jnp.take(stacked, order, axis=0)
+
+
+def gather_slots(part, axis):
+    here = lax.axis_index(axis)
+    stages = tree_stages(lax.axis_size(axis))
+    ndim = part.ndim
+    for level, stage in enumerate(reversed(stages)):
+        factor, stride = stage
+        place = (here // stride) % factor
+        parts = [part] + [swap(part, axis, stage, k) for k in range(1, factor)]
+        part = jnp.moveaxis(in_order(parts, place), 0, level)
+    return part.reshape((-1,) + part.shape[part.ndim - ndim:])
+
+
+def spread_rows(weights, start, length):
+    rows = jnp.repeat(weights, HEAD_DIM, axis=-1)
+    return lax.dynamic_slice_in_dim(rows, start, length, rows.ndim - 1)[..., None]
+
+
+def scan_states(local_rows, device_log, axis):
+    count, here = lax.axis_size(axis), lax.axis_index(axis)
+    logs = gather_slots(device_log, axis)
+    stages = tree_stages(count)
+    device = jnp.arange(count, dtype=jnp.int32)
+    total, start, held = local_rows, 0, []
+    for factor, stride in stages:
+        stage = (factor, stride)
+        place = (here // stride) % factor
+        base = here // (stride * factor) * (stride * factor)
+        length = total.shape[0] // factor
+        pieces = total.astype(jnp.bfloat16).reshape(factor, length, STATE_SIZE)
+        parts = [lax.dynamic_index_in_dim(total.reshape(factor, length, STATE_SIZE), place, 0, keepdims=False)]
+        for k in range(1, factor):
+            sent = lax.dynamic_index_in_dim(pieces, place ^ k, 0, keepdims=False)
+            parts.append(swap(sent, axis, stage, k).astype(jnp.float32))
+        start = start + place * length
+        segment = (device - base) // stride
+        inside = (device >= base) & (device < base + stride * factor)
+        spots = place ^ jnp.arange(factor, dtype=jnp.int32)
+        targets = jnp.concatenate([spots, jnp.full((1,), factor, jnp.int32)])
+        between = (
+            inside[None, None, :]
+            & (segment[None, None, :] > spots[None, :, None])
+            & (segment[None, None, :] < targets[:, None, None])
+        )
+        reach = jnp.sum(jnp.where(between[..., None], logs[None, None], 0.0), axis=2)
+        earlier = spots[None, :] < targets[:, None]
+        weights = jnp.where(earlier[..., None], jnp.exp(reach), 0.0)
+        ahead = inside[None, :] & (segment[None, :] < targets[:, None])
+        carry = jnp.exp(jnp.sum(jnp.where(ahead[..., None], logs[None], 0.0), axis=1))
+        weights = spread_rows(weights, start, length)
+        carry = spread_rows(carry, start, length)
+        sums = [
+            sum(weights[target, k] * parts[k] for k in range(factor)) for target in range(factor + 1)
+        ]
+        total = sums[factor]
+        held.append((stage, place, sums[:factor], carry))
+    final = total.astype(jnp.bfloat16)
+    entering = None
+    for stage, place, sums, carry in reversed(held):
+        factor, stride = stage
+        if entering is not None:
+            sums = [carry[k] * entering.astype(jnp.float32) + sums[k] for k in range(factor)]
+        sums = [part.astype(jnp.bfloat16) for part in sums]
+        parts = [sums[0]] + [swap(sums[k], axis, stage, k) for k in range(1, factor)]
+        entering = in_order(parts, place).reshape(-1, STATE_SIZE)
+    for stage, place, _, _ in reversed(held):
+        factor, stride = stage
+        parts = [final] + [swap(final, axis, stage, k) for k in range(1, factor)]
+        final = in_order(parts, place).reshape(-1, STATE_SIZE)
+    return (entering, final)
+
+
+def scatter_sum(whole, axis):
+    count, here = lax.axis_size(axis), lax.axis_index(axis)
+    blocks = whole.reshape((count, -1) + whole.shape[1:])
+    total = lax.dynamic_index_in_dim(blocks, here, 0, keepdims=False)
+    for k in range(1, count):
+        sent = lax.dynamic_index_in_dim(blocks, here ^ k, 0, keepdims=False)
+        total = total + swap(sent, axis, (count, 1), k)
+    return total
 
 
 def local_block(block_input, block_step, block_write, block_read, rate, groups):
@@ -137,10 +241,6 @@
     return (hidden, new_state)
 
 
-def combine(earlier, later):
-    return (earlier[0] + later[0], earlier[1] * jnp.exp(later[0])[:, None, None] + later[1])
-
-
 def on_device(
     prefill_input,
     prefill_step,
@@ -162,52 +262,23 @@
 ):
     local_heads = decay_rate.shape[0]
     local_groups = write_proj.shape[1] // STATE_SIZE
-    blocks = prefill_input.shape[0] // BLOCK_LEN
-    incoming_vectors = prefill_input.reshape(blocks, BLOCK_LEN, local_heads * HEAD_DIM)
-    steps = prefill_step.reshape(blocks, BLOCK_LEN, local_heads)
-    writes = write_proj.reshape(blocks, BLOCK_LEN, local_groups * STATE_SIZE)
-    reads = read_proj.reshape(blocks, BLOCK_LEN, local_groups * STATE_SIZE)
-    zero_state = jnp.zeros((local_heads, HEAD_DIM, STATE_SIZE), jnp.float32)
-    zero_log = jnp.zeros((local_heads,), jnp.float32)
-
-    def first_pass(carry_pair, block_data):
-        total_log, aggregate_memory_tensor = carry_pair
-        block_input, block_step, block_write, block_read = block_data
-        intra_part, local_state, running = local_block(
-            block_input, block_step, block_write, block_read, decay_rate, local_groups
-        )
-        aggregate_memory_tensor = (
-            aggregate_memory_tensor * jnp.exp(running[-1])[:, None, None] + local_state
-        )
-        return (
-            (total_log + running[-1], aggregate_memory_tensor),
-            (intra_part, local_state, running),
-        )
-
-    (device_log, device_state), (intra_all, local_all, running_all) = lax.scan(
-        first_pass, (zero_log, zero_state), (incoming_vectors, steps, writes, reads)
-    )
-    enter_log, entering = carried_in(
-        (device_log, device_state), "seq", combine, (zero_log, zero_state)
-    )
-
-    def finish_block(state_now, block_data):
-        intra_part, local_state, running, block_input, block_read = block_data
-        inter_part = read_state(block_read, state_now, running, local_groups)
-        skip_part = skip_gain[None, :, None] * block_input.reshape(
-            BLOCK_LEN, local_heads, HEAD_DIM
-        ).astype(jnp.float32)
-        output = (intra_part + inter_part + skip_part).astype(jnp.bfloat16)
-        state_now = state_now * jnp.exp(running[-1])[:, None, None] + local_state
-        return (state_now, output.reshape(BLOCK_LEN, local_heads * HEAD_DIM))
-
-    leaving, output_blocks = lax.scan(
-        finish_block, entering, (intra_all, local_all, running_all, incoming_vectors, reads)
-    )
-    prefill_out = output_blocks.reshape(blocks * BLOCK_LEN, local_heads * HEAD_DIM)
+    assert prefill_input.shape[0] == BLOCK_LEN
+    intra_part, local_state, running = local_block(
+        prefill_input, prefill_step, write_proj, read_proj, decay_rate, local_groups
+    )
+    entering, final = scan_states(
+        local_state.reshape(local_heads * HEAD_DIM, STATE_SIZE), running[-1], "seq"
+    )
+    state_shape = (local_heads, HEAD_DIM, STATE_SIZE)
+    inter_part = read_state(read_proj, entering.reshape(state_shape), running, local_groups)
+    skip_part = skip_gain[None, :, None] * prefill_input.reshape(
+        BLOCK_LEN, local_heads, HEAD_DIM
+    ).astype(jnp.float32)
+    prefill_out = (intra_part + inter_part + skip_part).astype(jnp.bfloat16)
+    prefill_out = prefill_out.reshape(BLOCK_LEN, local_heads * HEAD_DIM)
     seq_count = lax.axis_size("seq")
     sequence_index = lax.axis_index("seq")
-    prompt_state = from_root(leaving.astype(jnp.bfloat16), "seq", seq_count - 1)
+    prompt_state = final.reshape(state_shape)
     slice_width = HEAD_DIM * STATE_SIZE // seq_count
     flat_state = prompt_state.reshape(local_heads, HEAD_DIM * STATE_SIZE)
     state_slice = lax.dynamic_slice_in_dim(flat_state, sequence_index * slice_width, slice_width, 1)
@@ -248,14 +319,11 @@
         norm_gain,
         local_groups,
     )
+    gathered = gather_slots(hidden, "seq")
     partial_out = jnp.dot(
-        lax.all_gather(hidden, "seq", axis=0, tiled=True),
-        out_weight,
-        preferred_element_type=jnp.float32,
-    )
-    verify_out = lax.psum_scatter(partial_out, "head", scatter_dimension=0, tiled=True).astype(
-        jnp.bfloat16
-    )
+        gathered.reshape(-1, gathered.shape[-1]), out_weight, preferred_element_type=jnp.float32
+    )
+    verify_out = scatter_sum(partial_out, "head").astype(jnp.bfloat16)
     return (prefill_out, new_state[None], verify_out, state_slice)
 
 

time: 393 us -> 186 us (0.47)
  waiting for transfers between devices: 265 us -> 18.1 us
  local copies, waits for them, and re-layouts: 15.8 us -> 50.3 us
  starting transfers between devices: 0.34 us -> 31.9 us
  blocking collectives: 23 us -> 0 us
  between operations: 14.2 us -> 1.67 us
  other arithmetic: 53 us -> 59.9 us
    all_gather x2 -> x0, waiting for transfers between devices: 177 us -> none  [the longest x1 143 us: carried_in(): everything = jax.tree.map(lambda part: lax.all_gather(part, axis), value)]
    psum x1 -> x0, waiting for transfers between devices: 87.5 us -> none  [from_root(): return lax.psum(block, axis)]
    select_n x17 -> x9, other arithmetic: 36.2 us -> 3.44 us  [the longest x5 3.21 us: in_order(): return jnp.take(stacked, order, axis=0)]
    ppermute x0 -> x26, starting transfers between devices: none -> 31.9 us  [swap(): lax.ppermute(value, axis, [(source, partner(source, stage, offset)) for s...]
    all_gather x1 -> x0, blocking collectives: 23 us -> none  [carried_in(): everything = jax.tree.map(lambda part: lax.all_gather(part, axis), value)]
    ppermute x0 -> x26, waiting for transfers between devices: none -> 18.1 us  [swap(): lax.ppermute(value, axis, [(source, partner(source, stage, offset)) for s...]
    another operation x5 -> x23, other arithmetic: 1.75 us -> 13.5 us  [the longest x5 6.76 us: in_order(): stacked = jnp.stack(parts)]
    convert_element_type x3 -> x7, other arithmetic: 3.28 us -> 14.7 us  [the longest x1 4.93 us: on_device(): prefill_out = (intra_part + inter_part + skip_part).astype(jnp.bfloat16)]
  transfers between devices with their start and end apart: 4 -> 26, of which waited for: 3 -> 8; matrix products, arithmetic and copies ran while one was open for 7% -> 57% of each run, Pallas kernels for 0% -> 0%
where the time goes in v1:
time: 186 us; the launch traced here: 184 us
  other arithmetic  59.9 us (32%)
  local copies, waits for them, and re-layouts  50.3 us (27%)
  starting transfers between devices  31.9 us (17%)
  matrix products  22.5 us (12%)
  waiting for transfers between devices  18.1 us (10%)
    ppermute x26, starting transfers between devices, swap(): lax.ppermute(value, axis, [(source, partner(source, stage, offset)) for s...  31.9 us
    ppermute x26, waiting for transfers between devices, swap(): lax.ppermute(value, axis, [(source, partner(source, stage, offset)) for s...  18.1 us
    unnamed x94, local copies, waits for them, and re-layouts  12.8 us
    gather x4, local copies, waits for them, and re-layouts, in_order(): return jnp.take(stacked, order, axis=0)  6.89 us
    dot_general x1, matrix products, local_block(): jnp.einsum('gktj,jgkp->tgkp', mixing, incoming_vectors, preferred_element...  6.8 us
    another operation x5, other arithmetic, in_order(): stacked = jnp.stack(parts)  6.76 us
    another operation x14, other arithmetic, in_order(): return jnp.stack([first, second])  5.89 us
    and x6, other arithmetic, scan_states(): inside[None, None, :] & (segment[None, None, :] > spots[None, :, None])  5.66 us
  transfers between devices with their start and end apart: 26, of which 8 were waited for; matrix products, arithmetic and copies ran while one was open for 57% of the time, Pallas kernels for 0%

profile of v1, /device:TPU:0, one launch (start us, length us, event | category | flops | bytes accessed | tf_op | source)
XLA Modules:
  0.0 184.4 jit_solution(15566575954793788133)
XLA Ops:
  3.3 5.0 %collective-permute-start.2 = (f32[64]{0:T(128)}, f32[64]{0:T(128)}, u32[]{:S(2)}, u32[]{:S(2)}) collective-permute-start(f32[64]{0:T(128)} %get-tuple-element.66), channel_id=1, source_target_pairs={{0,24},{2,26},{4,28},{6,30},{8,16},{10,18},{12,20},{14,22},{16,8},... | collective-permute-start | bytes 776 | tf_op jit(solution)/shard_map/ppermute | solution.py:45
  10.5 3.3 %copy.149 = bf16[256,4096]{0,1:T(8,128)(2,1)S(1)} copy(bf16[256,4096]{1,0:T(8,128)(2,1)} %param.19) | data formatting | bytes 4194304 | tf_op args[0]
  33.5 2.0 %select_reduce_fusion.7 = s32[]{:T(128)} fusion(s32[16]{0:T(128)} %param.28, s32[]{:T(128)} %fusion.93), kind=kLoop, calls=%fused_computation.251 | loop fusion | flops 47 | bytes 72 | tf_op jit(solution)/shard_map/reduce_sum | solution.py:289
  44.5 3.2 %fusion.37 = f32[4,16,64,128]{3,2,1,0:T(8,128)} fusion(f32[8,4,16]{0,2,1:T(8,128)S(1)} %bitcast.345, bf16[8,4,16,64]{3,2,1,0:T(8,128)(2,1)S(1)} %reshape.866, bf16[8,512]{1,0:T(8,128)(2,1)S(1)} %convolution_convert_fusion.3), kind=kOutput, calls=%fused_computation.82 | convolution fusion | flops 50397184 | bytes 2172928 | tf_op jit(solution)/shard_map/tgkp,tgn->gkpn/dot_general | solution.py:238
  47.9 6.8 %fusion = f32[4,16,256,64]{2,3,1,0:T(8,128)} fusion(bf16[256,4,16,64]{0,3,2,1:T(8,128)(2,1)S(1)} %bitcast.318, f32[4,16,256]{2,1,0:T(8,128)S(1)} %bitcast.343, f32[4,16,256]{2,1,0:T(8,128)S(1)} %reduce_window_sum.38, f32[4,256,256]{2,1,0:T(8,128)} %fusion.38, pred[256,256]{1,0:T(8,128)(4,1)S(1)} %copy-done.20), kind=kOutput, calls=%fused_computation.5 | convolution fusion | flops 557842432 | bytes 7536640 | tf_op jit(solution)/shard_map/gktj,jgkp->tgkp/dot_general | solution.py:158
  56.0 1.7 collective-permute-start.3
  71.3 2.0 %fusion.102 = (bf16[2048,128]{1,0:T(8,128)(2,1)S(1)}, f32[2048,128]{1,0:T(8,128)S(1)}) fusion(bf16[2048,128]{1,0:T(8,128)(2,1)} %copy-done.6, f32[2048]{0:T(1024)S(1)} %bitcast.357, f32[2,2048,128]{2,1,0:T(8,128)} %bitcast.320, s32[]{:T(128)S(6)} %select_n.340, f32[2048]{0:T(1024)S(1)} %bitcast.358), kind=kLoop, calls=%fused_computation.263 | loop fusion | flops 1310720 | bytes 3162116 | tf_op jit(solution)/shard_map/convert_element_type | solution.py:88
  80.9 2.0 %collective-permute-done.6 = bf16[1024,128]{1,0:T(8,128)(2,1)S(1)} collective-permute-done((bf16[1024,128]{1,0:T(8,128)(2,1)}, bf16[1024,128]{1,0:T(8,128)(2,1)S(1)}, u32[]{:S(2)}, u32[]{:S(2)}) %collective-permute-start.6) | collective-permute-done | bytes 262176 | tf_op jit(solution)/shard_map/ppermute | solution.py:45
  86.2 2.9 %collective-permute-start.8 = (bf16[256,128]{1,0:T(8,128)(2,1)}, bf16[256,128]{1,0:T(8,128)(2,1)}, u32[]{:S(2)}, u32[]{:S(2)}) collective-permute-start(bf16[256,128]{1,0:T(8,128)(2,1)} %get-tuple-element.57), channel_id=1, source_target_pairs={{0,16},{2,18},{4,20},{6,22},{8,24},{10,26},{12,28},{14,30},{16,0},... | collective-permute-start | bytes 196616 | tf_op jit(solution)/shard_map/ppermute | solution.py:45
  95.5 2.1 %fusion.70 = (bf16[256,128]{1,0:T(8,128)(2,1)S(1)}, bf16[256,128]{1,0:T(8,128)(2,1)}, bf16[256,128]{1,0:T(8,128)(2,1)}) fusion(bf16[256,128]{1,0:T(8,128)(2,1)} %collective-permute-done.7, bf16[256,128]{1,0:T(8,128)(2,1)} %collective-permute-done.8, bf16[256,128]{1,0:T(8,128)(2,1)} %collective-permute-done.9, f32[4,256,128]{2,1,0:T(8,128)} %bitcast.332, ...), kind=kLoop, calls=%fused_computation.146 | loop fusion | flops 884736 | bytes 536580 | tf_op jit(solution)/shard_map/convert_element_type | solution.py:115
  97.6 3.3 %collective-permute-start.17 = (bf16[256,128]{1,0:T(8,128)(2,1)S(1)}, bf16[256,128]{1,0:T(8,128)(2,1)S(1)}, u32[]{:S(2)}, u32[]{:S(2)}) collective-permute-start(bf16[256,128]{1,0:T(8,128)(2,1)S(1)} %get-tuple-element.47), channel_id=1, source_target_pairs={{0,24},{2,26},{4,28},{6,30},{8,16},{10,18},{12,20},{14,22},{16,8},... | collective-permute-start | bytes 196616 | tf_op jit(solution)/shard_map/ppermute | solution.py:45
  102.0 2.0 %fusion.81 = (bf16[1,256,128]{2,1,0:T(8,128)(2,1)}, bf16[256,128]{1,0:T(8,128)(2,1)}) fusion(bf16[256,128]{1,0:T(8,128)(2,1)} %collective-permute-done.9, bf16[256,128]{1,0:T(8,128)(2,1)} %collective-permute-done.8, bf16[256,128]{1,0:T(8,128)(2,1)} %collective-permute-done.7, f32[4,256,128]{2,1,0:T(8,128)} %bitcast.333, s32[]{:T(128)S(6)} %select_n.344, ...), kind=kLoop, calls=%fused_computation.166 | loop fusion | flops 622592 | bytes 466948 | tf_op jit(solution)/shard_map/stack | solution.py:55
  104.0 3.3 %collective-permute-start.12 = (bf16[256,128]{1,0:T(8,128)(2,1)}, bf16[256,128]{1,0:T(8,128)(2,1)}, u32[]{:S(2)}, u32[]{:S(2)}) collective-permute-start(bf16[256,128]{1,0:T(8,128)(2,1)} %get-tuple-element.51), channel_id=1, source_target_pairs={{0,24},{2,26},{4,28},{6,30},{8,16},{10,18},{12,20},{14,22},{16,8},... | collective-permute-start | bytes 196616 | tf_op jit(solution)/shard_map/ppermute | solution.py:45
  109.2 2.3 %gather_fusion.3 = bf16[4,256,128]{2,1,0:T(8,128)(2,1)} fusion(bf16[4,256,128]{2,1,0:T(8,128)(2,1)} %pad_maximum_fusion.5, s32[1024]{0:T(1024)} %pad_clamp_fusion), kind=kCustom, calls=%fused_computation.1.clone | custom fusion | bytes 524304 | tf_op jit(solution)/shard_map/jit(_take)/gather | solution.py:57
  114.5 2.4 %gather_fusion.2 = bf16[4,256,128]{2,1,0:T(8,128)(2,1)} fusion(bf16[4,256,128]{2,1,0:T(8,128)(2,1)} %pad_maximum_fusion.4, s32[1024]{0:T(1024)} %pad_clamp_fusion), kind=kCustom, calls=%fused_computation.clone | custom fusion | bytes 524304 | tf_op jit(solution)/shard_map/jit(_take)/gather | solution.py:57
  122.4 4.7 %collective-permute-done.18 = bf16[1024,128]{1,0:T(8,128)(2,1)S(1)} collective-permute-done((bf16[1024,128]{1,0:T(8,128)(2,1)S(1)}, bf16[1024,128]{1,0:T(8,128)(2,1)S(1)}, u32[]{:S(2)}, u32[]{:S(2)}) %collective-permute-start.18) | collective-permute-done | bytes 262176 | tf_op jit(solution)/shard_map/ppermute | solution.py:45
  127.3 2.9 %collective-permute-done.13 = bf16[1024,128]{1,0:T(8,128)(2,1)S(1)} collective-permute-done((bf16[1024,128]{1,0:T(8,128)(2,1)S(1)}, bf16[1024,128]{1,0:T(8,128)(2,1)S(1)}, u32[]{:S(2)}, u32[]{:S(2)}) %collective-permute-start.13) | collective-permute-done | bytes 262176 | tf_op jit(solution)/shard_map/ppermute | solution.py:45
  140.7 2.8 %collective-permute-start.20 = (bf16[8,4096]{1,0:T(8,128)(2,1)}, bf16[8,4096]{1,0:T(8,128)(2,1)}, u32[]{:S(2)}, u32[]{:S(2)}) collective-permute-start(bf16[8,4096]{1,0:T(8,128)(2,1)} %multiply_convert_fusion.4), channel_id=1, source_target_pairs={{0,8},{2,10},{4,12},{6,14},{8,0},{10,2},{12,4},{14,6},{16,24},{18,... | collective-permute-start | bytes 196616 | tf_op jit(solution)/shard_map/ppermute | solution.py:45
  145.3 3.0 %select_bitcast_fusion.5 = (bf16[1,2048,128]{2,1,0:T(8,128)(2,1)}, bf16[2048,128]{1,0:T(8,128)(2,1)}) fusion(bf16[2048,128]{1,0:T(8,128)(2,1)} %collective-permute-done.14, pred[]{:T(512)S(6)} %eq.62, bf16[2048,128]{1,0:T(8,128)(2,1)} %copy-done.6, f32[2048]{0:T(1024)} %bitcast.354, f32[2,2048,128]{2,1,0:T(8,128)} %bitcast.321, s32[]{:T(128)S(6)} %select_n.340, ...), kind=kLoop, calls=%fused_computation.79 | loop fusion | flops 2359296 | bytes 3694597 | tf_op jit(solution)/shard_map/stack | solution.py:54
  155.1 5.8 %collective-permute-done.23 = bf16[4,8,4096]{2,1,0:T(8,128)(2,1)S(1)} collective-permute-done((bf16[4,8,4096]{2,1,0:T(8,128)(2,1)S(1)}, bf16[4,8,4096]{2,1,0:T(8,128)(2,1)S(1)}, u32[]{:S(2)}, u32[]{:S(2)}) %collective-permute-start.23) | collective-permute-done | bytes 262176 | tf_op jit(solution)/shard_map/ppermute | solution.py:45
  161.8 2.7 %fusion.43 = f32[4,16,64,256]{3,2,1,0:T(8,128)} fusion(bf16[4,16,64,128]{3,2,1,0:T(8,128)(2,1)S(1)} %bitcast.330, bf16[256,4,128,1]{2,1,0,3:T(4,128)(2,1)S(1)} %bitcast.340), kind=kOutput, calls=%fused_computation.91 | convolution fusion | flops 268435456 | bytes 5505024 | tf_op jit(solution)/shard_map/tgn,gkpn->tgkp/dot_general | solution.py:179
  164.9 1.9 %copy-done.4 = bf16[4096,512]{1,0:T(8,128)(2,1)S(1)} copy-done((bf16[4096,512]{1,0:T(8,128)(2,1)S(1)}, bf16[4096,512]{1,0:T(8,128)(2,1)}, u32[]{:S(2)}) %copy-start.4) | copy-done | bytes 4194328
  172.3 4.9 %fusion.10 = bf16[256,4096]{0,1:T(8,128)(2,1)} fusion(f32[4,16,64,256]{3,2,1,0:T(8,128)} %fusion.43, f32[4,16,256,64]{2,3,1,0:T(8,128)} %fusion, bf16[256,4096]{0,1:T(8,128)(2,1)S(1)} %copy.149, f32[4096]{0:T(1024)S(1)} %mul.680, f32[256,64]{0,1:T(8,128)} %get-tuple-element.59), kind=kLoop, calls=%fused_computation.18 | loop fusion | flops 6291456 | bytes 12664832 | tf_op jit(solution)/shard_map/convert_element_type | solution.py:277
  177.3 4.1 %copy.168 = bf16[256,4096]{1,0:T(8,128)(2,1)} copy(bf16[256,4096]{0,1:T(8,128)(2,1)} %fusion.10) | data formatting | bytes 4194304
  (277 shorter events, 105.5 us)
Async XLA Ops:
  3.3 51.4 %collective-permute-start.2 = (f32[64]{0:T(128)}, f32[64]{0:T(128)}, u32[]{:S(2)}, u32[]{:S(2)}) collective-permute-start(f32[64]{0:T(128)} %get-tuple-element.66), channel_id=1, source_target_pairs={{0,24},{2,26},{4,28},{6,30},{8,16},{10,18},{12,20},{14,22},{16,8},... | collective-permute-start | bytes 776 | tf_op jit(solution)/shard_map/ppermute | solution.py:45
  8.4 46.3 %collective-permute-start.1 = (f32[64]{0:T(128)}, f32[64]{0:T(128)}, u32[]{:S(2)}, u32[]{:S(2)}) collective-permute-start(f32[64]{0:T(128)} %get-tuple-element.66), channel_id=1, source_target_pairs={{0,16},{2,18},{4,20},{6,22},{8,24},{10,26},{12,28},{14,30},{16,0},... | collective-permute-start | bytes 776 | tf_op jit(solution)/shard_map/ppermute | solution.py:45
  8.4 46.3 %collective-permute-start = (f32[64]{0:T(128)}, f32[64]{0:T(128)}, u32[]{:S(2)}, u32[]{:S(2)}) collective-permute-start(f32[64]{0:T(128)} %get-tuple-element.66), channel_id=1, source_target_pairs={{0,8},{2,10},{4,12},{6,14},{8,0},{10,2},{12,4},{14,6},{16,24},{18,... | collective-permute-start | bytes 776 | tf_op jit(solution)/shard_map/ppermute | solution.py:45
  16.8 53.7 %collective-permute-start.5 = (bf16[2048,128]{1,0:T(8,128)(2,1)}, bf16[2048,128]{1,0:T(8,128)(2,1)S(1)}, u32[]{:S(2)}, u32[]{:S(2)}) collective-permute-start(bf16[2048,128]{1,0:T(8,128)(2,1)} %fusion.36), channel_id=1, source_target_pairs={{0,2},{2,0},{4,6},{6,4},{8,10},{10,8},{12,14},{14,12},{16,18},{18,... | collective-permute-start | bytes 1572872 | tf_op jit(solution)/shard_map/ppermute | solution.py:45
  59.7 3.8 %collective-permute-start.4 = (f32[4,2,64]{2,0,1:T(4,128)S(1)}, f32[4,2,64]{2,0,1:T(4,128)S(1)}, u32[]{:S(2)}, u32[]{:S(2)}) collective-permute-start(f32[4,2,64]{2,0,1:T(4,128)S(1)} %maximum_bitcast_fusion.3), channel_id=1, source_target_pairs={{0,2},{2,0},{4,6},{6,4},{8,10},{10,8},{12,14},{14,12},{16,18},{18,... | collective-permute-start | bytes 6152 | tf_op jit(solution)/shard_map/ppermute | solution.py:45
  74.0 8.9 %collective-permute-start.6 = (bf16[1024,128]{1,0:T(8,128)(2,1)}, bf16[1024,128]{1,0:T(8,128)(2,1)S(1)}, u32[]{:S(2)}, u32[]{:S(2)}) collective-permute-start(bf16[1024,128]{1,0:T(8,128)(2,1)} %dynamic-slice_bitcast_fusion), channel_id=1, source_target_pairs={{0,4},{2,6},{4,0},{6,2},{8,12},{10,14},{12,8},{14,10},{16,20},{18,... | collective-permute-start | bytes 786440 | tf_op jit(solution)/shard_map/ppermute | solution.py:45
  84.8 10.2 %collective-permute-start.7 = (bf16[256,128]{1,0:T(8,128)(2,1)}, bf16[256,128]{1,0:T(8,128)(2,1)}, u32[]{:S(2)}, u32[]{:S(2)}) collective-permute-start(bf16[256,128]{1,0:T(8,128)(2,1)} %get-tuple-element.58), channel_id=1, source_target_pairs={{0,8},{2,10},{4,12},{6,14},{8,0},{10,2},{12,4},{14,6},{16,24},{18,... | collective-permute-start | bytes 196616 | tf_op jit(solution)/shard_map/ppermute | solution.py:45
  86.2 8.7 %collective-permute-start.8 = (bf16[256,128]{1,0:T(8,128)(2,1)}, bf16[256,128]{1,0:T(8,128)(2,1)}, u32[]{:S(2)}, u32[]{:S(2)}) collective-permute-start(bf16[256,128]{1,0:T(8,128)(2,1)} %get-tuple-element.57), channel_id=1, source_target_pairs={{0,16},{2,18},{4,20},{6,22},{8,24},{10,26},{12,28},{14,30},{16,0},... | collective-permute-start | bytes 196616 | tf_op jit(solution)/shard_map/ppermute | solution.py:45
  89.2 6.4 %collective-permute-start.9 = (bf16[256,128]{1,0:T(8,128)(2,1)}, bf16[256,128]{1,0:T(8,128)(2,1)}, u32[]{:S(2)}, u32[]{:S(2)}) collective-permute-start(bf16[256,128]{1,0:T(8,128)(2,1)} %get-tuple-element.56), channel_id=1, source_target_pairs={{0,24},{2,26},{4,28},{6,30},{8,16},{10,18},{12,20},{14,22},{16,8},... | collective-permute-start | bytes 196616 | tf_op jit(solution)/shard_map/ppermute | solution.py:45
  97.6 9.6 %collective-permute-start.17 = (bf16[256,128]{1,0:T(8,128)(2,1)S(1)}, bf16[256,128]{1,0:T(8,128)(2,1)S(1)}, u32[]{:S(2)}, u32[]{:S(2)}) collective-permute-start(bf16[256,128]{1,0:T(8,128)(2,1)S(1)} %get-tuple-element.47), channel_id=1, source_target_pairs={{0,24},{2,26},{4,28},{6,30},{8,16},{10,18},{12,20},{14,22},{16,8},... | collective-permute-start | bytes 196616 | tf_op jit(solution)/shard_map/ppermute | solution.py:45
  100.9 7.5 %collective-permute-start.16 = (bf16[256,128]{1,0:T(8,128)(2,1)S(1)}, bf16[256,128]{1,0:T(8,128)(2,1)S(1)}, u32[]{:S(2)}, u32[]{:S(2)}) collective-permute-start(bf16[256,128]{1,0:T(8,128)(2,1)S(1)} %get-tuple-element.47), channel_id=1, source_target_pairs={{0,16},{2,18},{4,20},{6,22},{8,24},{10,26},{12,28},{14,30},{16,0},... | collective-permute-start | bytes 196616 | tf_op jit(solution)/shard_map/ppermute | solution.py:45
  100.9 7.5 %collective-permute-start.15 = (bf16[256,128]{1,0:T(8,128)(2,1)S(1)}, bf16[256,128]{1,0:T(8,128)(2,1)S(1)}, u32[]{:S(2)}, u32[]{:S(2)}) collective-permute-start(bf16[256,128]{1,0:T(8,128)(2,1)S(1)} %get-tuple-element.47), channel_id=1, source_target_pairs={{0,8},{2,10},{4,12},{6,14},{8,0},{10,2},{12,4},{14,6},{16,24},{18,... | collective-permute-start | bytes 196616 | tf_op jit(solution)/shard_map/ppermute | solution.py:45
  104.0 7.5 %collective-permute-start.12 = (bf16[256,128]{1,0:T(8,128)(2,1)}, bf16[256,128]{1,0:T(8,128)(2,1)}, u32[]{:S(2)}, u32[]{:S(2)}) collective-permute-start(bf16[256,128]{1,0:T(8,128)(2,1)} %get-tuple-element.51), channel_id=1, source_target_pairs={{0,24},{2,26},{4,28},{6,30},{8,16},{10,18},{12,20},{14,22},{16,8},... | collective-permute-start | bytes 196616 | tf_op jit(solution)/shard_map/ppermute | solution.py:45
  107.3 5.5 %collective-permute-start.11 = (bf16[256,128]{1,0:T(8,128)(2,1)}, bf16[256,128]{1,0:T(8,128)(2,1)}, u32[]{:S(2)}, u32[]{:S(2)}) collective-permute-start(bf16[256,128]{1,0:T(8,128)(2,1)} %get-tuple-element.49), channel_id=1, source_target_pairs={{0,16},{2,18},{4,20},{6,22},{8,24},{10,26},{12,28},{14,30},{16,0},... | collective-permute-start | bytes 196616 | tf_op jit(solution)/shard_map/ppermute | solution.py:45
  107.3 5.5 %collective-permute-start.10 = (bf16[256,128]{1,0:T(8,128)(2,1)}, bf16[256,128]{1,0:T(8,128)(2,1)}, u32[]{:S(2)}, u32[]{:S(2)}) collective-permute-start(bf16[256,128]{1,0:T(8,128)(2,1)} %get-tuple-element.48), channel_id=1, source_target_pairs={{0,8},{2,10},{4,12},{6,14},{8,0},{10,2},{12,4},{14,6},{16,24},{18,... | collective-permute-start | bytes 196616 | tf_op jit(solution)/shard_map/ppermute | solution.py:45
  118.2 8.9 %collective-permute-start.18 = (bf16[1024,128]{1,0:T(8,128)(2,1)S(1)}, bf16[1024,128]{1,0:T(8,128)(2,1)S(1)}, u32[]{:S(2)}, u32[]{:S(2)}) collective-permute-start(bf16[1024,128]{1,0:T(8,128)(2,1)S(1)} %bitcast.339), channel_id=1, source_target_pairs={{0,4},{2,6},{4,0},{6,2},{8,12},{10,14},{12,8},{14,10},{16,20},{18,... | collective-permute-start | bytes 786440 | tf_op jit(solution)/shard_map/ppermute | solution.py:45
  121.8 8.4 %collective-permute-start.13 = (bf16[1024,128]{1,0:T(8,128)(2,1)S(1)}, bf16[1024,128]{1,0:T(8,128)(2,1)S(1)}, u32[]{:S(2)}, u32[]{:S(2)}) collective-permute-start(bf16[1024,128]{1,0:T(8,128)(2,1)S(1)} %fusion.32), channel_id=1, source_target_pairs={{0,4},{2,6},{4,0},{6,2},{8,12},{10,14},{12,8},{14,10},{16,20},{18,... | collective-permute-start | bytes 786440 | tf_op jit(solution)/shard_map/ppermute | solution.py:45
  127.2 5.5 %collective-permute-start.19 = (bf16[2048,128]{1,0:T(8,128)(2,1)S(1)}, bf16[2048,128]{1,0:T(8,128)(2,1)S(1)}, u32[]{:S(2)}, u32[]{:S(2)}) collective-permute-start(bf16[2048,128]{1,0:T(8,128)(2,1)S(1)} %bitcast.331), channel_id=1, source_target_pairs={{0,2},{2,0},{4,6},{6,4},{8,10},{10,8},{12,14},{14,12},{16,18},{18,... | collective-permute-start | bytes 1572872 | tf_op jit(solution)/shard_map/ppermute | solution.py:45
  132.7 12.5 %collective-permute-start.14 = (bf16[2048,128]{1,0:T(8,128)(2,1)}, bf16[2048,128]{1,0:T(8,128)(2,1)}, u32[]{:S(2)}, u32[]{:S(2)}) collective-permute-start(bf16[2048,128]{1,0:T(8,128)(2,1)} %fusion.23), channel_id=1, source_target_pairs={{0,2},{2,0},{4,6},{6,4},{8,10},{10,8},{12,14},{14,12},{16,18},{18,... | collective-permute-start | bytes 1572872 | tf_op jit(solution)/shard_map/ppermute | solution.py:45
  139.1 9.2 %collective-permute-start.22 = (bf16[8,4096]{1,0:T(8,128)(2,1)}, bf16[8,4096]{1,0:T(8,128)(2,1)}, u32[]{:S(2)}, u32[]{:S(2)}) collective-permute-start(bf16[8,4096]{1,0:T(8,128)(2,1)} %multiply_convert_fusion.4), channel_id=1, source_target_pairs={{0,24},{2,26},{4,28},{6,30},{8,16},{10,18},{12,20},{14,22},{16,8},... | collective-permute-start | bytes 196616 | tf_op jit(solution)/shard_map/ppermute | solution.py:45
  140.7 7.8 %collective-permute-start.21 = (bf16[8,4096]{1,0:T(8,128)(2,1)}, bf16[8,4096]{1,0:T(8,128)(2,1)}, u32[]{:S(2)}, u32[]{:S(2)}) collective-permute-start(bf16[8,4096]{1,0:T(8,128)(2,1)} %multiply_convert_fusion.4), channel_id=1, source_target_pairs={{0,16},{2,18},{4,20},{6,22},{8,24},{10,26},{12,28},{14,30},{16,0},... | collective-permute-start | bytes 196616 | tf_op jit(solution)/shard_map/ppermute | solution.py:45
  140.7 7.8 %collective-permute-start.20 = (bf16[8,4096]{1,0:T(8,128)(2,1)}, bf16[8,4096]{1,0:T(8,128)(2,1)}, u32[]{:S(2)}, u32[]{:S(2)}) collective-permute-start(bf16[8,4096]{1,0:T(8,128)(2,1)} %multiply_convert_fusion.4), channel_id=1, source_target_pairs={{0,8},{2,10},{4,12},{6,14},{8,0},{10,2},{12,4},{14,6},{16,24},{18,... | collective-permute-start | bytes 196616 | tf_op jit(solution)/shard_map/ppermute | solution.py:45
  152.6 8.3 %collective-permute-start.23 = (bf16[4,8,4096]{2,1,0:T(8,128)(2,1)S(1)}, bf16[4,8,4096]{2,1,0:T(8,128)(2,1)S(1)}, u32[]{:S(2)}, u32[]{:S(2)}) collective-permute-start(bf16[4,8,4096]{2,1,0:T(8,128)(2,1)S(1)} %broadcast_select_fusion.2), channel_id=1, source_target_pairs={{0,4},{2,6},{4,0},{6,2},{8,12},{10,14},{12,8},{14,10},{16,20},{18,... | collective-permute-start | bytes 786440 | tf_op jit(solution)/shard_map/ppermute | solution.py:45
  168.1 14.7 %collective-permute-start.25 = (f32[64,512]{1,0:T(8,128)}, f32[64,512]{1,0:T(8,128)}, u32[]{:S(2)}, u32[]{:S(2)}) collective-permute-start(f32[64,512]{1,0:T(8,128)} %dynamic-slice_bitcast_fusion.1), channel_id=1, source_target_pairs={{0,1},{1,0},{2,3},{3,2},{4,5},{5,4},{6,7},{7,6},{8,9},{9,8},{10,11... | collective-permute-start | bytes 393224 | tf_op jit(solution)/shard_map/ppermute | solution.py:45
  (48 other events, 534.1 us)

commit v2 on v0

v2 whole, which is shorter than its diff:
```python
import functools

import jax
import jax.numpy as jnp
from jax import lax
from jax.experimental import pallas as pl
from jax.experimental.pallas import tpu as pltpu
from jax.sharding import PartitionSpec as P

HEAD_DIM = 64
STATE_SIZE = 128
BLOCK_LEN = 256
DRAFTS = 8
EPSILON = 1e-05
EXTRA = 32
UP_ROWS = STATE_SIZE + EXTRA
READ_AT = STATE_SIZE + 16
LOG_AT = STATE_SIZE + 24
DOWN_ROWS = STATE_SIZE + 16

F32 = jnp.float32
BF16 = jnp.bfloat16


def tree_stages(count):
    factors, rest = [], count
    if rest > 1:
        factors.append(2)
        rest //= 2
    inner = 1
    while inner * inner * 4 <= rest:
        inner *= 2
    factors += [inner, rest // inner]
    stages, stride = [], 1
    for factor in factors:
        stages.append((factor, stride))
        stride *= factor
    assert stride == count
    return stages


def swap(value, axis, stage, offset):
    count, stride = lax.axis_size(axis), stage[1]
    return lax.ppermute(value, axis, [(k, k ^ (offset * stride)) for k in range(count)])


def place_of(stage):
    factor, stride = stage
    return lax.rem(lax.div(lax.axis_index("seq"), stride), factor)


def dot(a, b, dims=((1,), (0,))):
    return lax.dot_general(a, b, (dims, ((), ())), preferred_element_type=F32)


def split(value, parts):
    found = []
    for _ in range(parts):
        part = value.astype(BF16).astype(F32)
        found.append(part)
        value = value - part
    return found


def head_mask(rows, heads, lanes, lane0):
    row = lax.broadcasted_iota(jnp.int32, (rows, lanes), 0) & (heads - 1)
    head = lax.shift_right_logical(lax.broadcasted_iota(jnp.int32, (rows, lanes), 1) + lane0, 6)
    return jnp.where(row == head, 1.0, 0.0).astype(BF16)


def window(start, size):
    return pl.ds(pl.multiple_of(start, size), size)


def call(kernel, name, outs, args, smem=(), scratch=(), flops=0, exps=0, vmem=40):
    in_specs = [
        pl.BlockSpec(memory_space=pltpu.SMEM if k in smem else pltpu.VMEM) for k in range(len(args))
    ]
    moved = sum(a.size * a.dtype.itemsize for a in args)
    moved += sum(o.size * o.dtype.itemsize for o in outs)
    return pl.pallas_call(
        kernel,
        name=name,
        out_shape=outs,
        in_specs=in_specs,
        out_specs=[pl.BlockSpec(memory_space=pltpu.VMEM)] * len(outs),
        scratch_shapes=list(scratch),
        compiler_params=pltpu.CompilerParams(vmem_limit_bytes=vmem * 1024 * 1024),
        cost_estimate=pl.CostEstimate(flops=flops, bytes_accessed=moved, transcendentals=exps),
    )(*args)


def shape(dims, dtype):
    return jax.ShapeDtypeStruct(dims, dtype)


def open_kernel(
    stage,
    step_ref,
    rate_ref,
    skip_ref,
    x_ref,
    write_ref,
    owner_ref,
    ids_ref,
    kept_ref,
    din_ref,
    dgate_ref,
    dwrite_ref,
    dread_ref,
    dstep_ref,
    own_ref,
    sent_ref,
    run_ref,
    runt_ref,
    stept_ref,
    reach_ref,
    q1_ref,
    q2_ref,
    vread_ref,
    vwrite_ref,
    tail_ref,
    extra_ref,
):
    span, heads = step_ref.shape
    lanes = x_ref.shape[1]
    groups = write_ref.shape[1] // STATE_SIZE
    per_group = heads // groups
    wide = per_group * HEAD_DIM
    here = lax.axis_index("seq")
    place = place_of(stage)

    step = step_ref[...]
    log_decay = -step * rate_ref[...]
    lower = lax.broadcasted_iota(jnp.int32, (span, span), 0) >= lax.broadcasted_iota(
        jnp.int32, (span, span), 1
    )
    lower = jnp.where(lower, 1.0, 0.0).astype(BF16)
    running = sum(dot(lower, part.astype(BF16)) for part in split(log_decay, 3))
    total = running[span - 1 : span, :]
    to_end = jnp.exp(total - running) * step
    both = jnp.concatenate([running, step], axis=1)
    if 2 * heads < 128:
        both = jnp.concatenate([both, jnp.zeros((span, 128 - 2 * heads), F32)], axis=1)
    turned = both.T
    runt_ref[...] = turned[:heads]
    stept_ref[...] = turned[heads : 2 * heads]
    for g in range(groups):
        run_ref[g] = running[:, g * per_group : (g + 1) * per_group]
    reach_ref[...] = jnp.concatenate(split(jnp.exp(running), 2), axis=1).astype(BF16)
    end_parts = jnp.concatenate(split(to_end, 2), axis=1).astype(BF16)

    slots = owner_ref.shape[0]
    request = lax.fori_loop(
        0, slots, lambda r, found: jnp.where(owner_ref[r] == here, r, found), jnp.int32(0)
    )
    kept = kept_ref[request]
    candidates = din_ref.shape[0]
    row = lax.broadcasted_iota(jnp.int32, (DRAFTS, candidates), 0)
    col = lax.broadcasted_iota(jnp.int32, (DRAFTS, candidates), 1)
    pick = jnp.zeros((DRAFTS, candidates), F32)
    for i in range(DRAFTS):
        pick = jnp.where((row == i) & (col == ids_ref[request, i]), 1.0, pick)
    pick = pick.astype(BF16)
    vin = dot(pick, din_ref[...])
    vgate = dot(pick, dgate_ref[...])
    vwrite = dot(pick, dwrite_ref[...]).astype(BF16)
    vread = dot(pick, dread_ref[...]).astype(BF16)
    vwrite_ref[...] = vwrite
    vread_ref[...] = vread
    vstep = sum(dot(pick, part.astype(BF16)) for part in split(dstep_ref[...], 3))
    vlog = -vstep * rate_ref[...]
    index = lax.broadcasted_iota(jnp.int32, (DRAFTS, heads), 0)
    acc = jnp.zeros((1, heads), F32)
    vrun = jnp.zeros((DRAFTS, heads), F32)
    reach = jnp.zeros((1, heads), F32)
    for i in range(DRAFTS):
        acc = acc + vlog[i : i + 1]
        vrun = jnp.where(index == i, acc, vrun)
        reach = jnp.where(i < kept, acc, reach)
    others = jnp.where(index == 0, total, jnp.where(index == 1, skip_ref[...], reach))
    stacked = split(jnp.concatenate([vrun, vstep, others], axis=0), 3)
    stacked = jnp.concatenate(stacked, axis=0).astype(BF16)
    row = lax.broadcasted_iota(jnp.int32, (DRAFTS, wide), 0)
    is_owner = owner_ref[0] == here
    for g in range(groups):
        at = slice(g * wide, (g + 1) * wide)
        spread = dot(stacked, head_mask(heads, heads, wide, g * wide))
        spread = spread[0:24] + spread[24:48] + spread[48:72]
        vrun_l, vstep_l = spread[0:8], spread[8:16]
        total_l, skip_l, reach_l = spread[16:17], spread[17:18], spread[18:19]
        vin_g = vin[:, at]
        vr = vread[:, g * STATE_SIZE : (g + 1) * STATE_SIZE]
        vw = vwrite[:, g * STATE_SIZE : (g + 1) * STATE_SIZE]
        scores = dot(vr, vw, ((1,), (1,)))
        direct = skip_l * vin_g
        for j in range(DRAFTS):
            decay = jnp.exp(jnp.where(row >= j, vrun_l - vrun_l[j : j + 1], -jnp.inf))
            direct = direct + decay * scores[:, j : j + 1] * (vstep_l[j : j + 1] * vin_g[j : j + 1])
        gate = vgate[:, at]
        gate = gate / (1.0 + jnp.exp(-gate))
        q1 = direct * gate
        q2 = jnp.exp(vrun_l) * gate
        q1_ref[:, at] = q1
        q2_ref[:, at] = q2
        live = jnp.exp(jnp.where(row < kept, reach_l - vrun_l, -jnp.inf)) * vstep_l * vin_g
        keep_l = jnp.concatenate(
            split(jnp.exp(reach_l), 3) + [jnp.zeros((5, wide), F32)], axis=0
        )
        tail_ref[:, at] = jnp.concatenate(split(live, 3) + [keep_l], axis=0).astype(BF16)
        read_l = jnp.concatenate([vr.astype(F32)] * (wide // STATE_SIZE), axis=1)
        mine = jnp.concatenate([q1, q2, read_l], axis=0)
        mine = jnp.where(is_owner, mine, 0.0)
        logs = jnp.concatenate(split(total_l, 3) + [jnp.zeros((5, wide), F32)], axis=0)
        extra_ref[:, at] = jnp.concatenate([mine, logs], axis=0).astype(BF16)

    half = lanes // 2
    chunk = min(wide, half)
    for k, out_ref in ((1, sent_ref), (0, own_ref)):
        start = (place ^ k) * half
        out_ref[STATE_SIZE:, :] = extra_ref[:, window(start, half)]
        for at in range(0, half, chunk):
            lane0 = start + at
            group = lax.div(lane0, wide)
            scale = dot(end_parts, head_mask(2 * heads, heads, chunk, lane0))
            weighted = (x_ref[:, window(lane0, chunk)].astype(F32) * scale).astype(BF16)
            writes = write_ref[:, window(group * STATE_SIZE, STATE_SIZE)]
            writes = writes.astype(F32).T.astype(BF16)
            out_ref[:STATE_SIZE, at : at + chunk] = dot(writes, weighted).astype(BF16)


def logs_of(block):
    return block[0:1].astype(F32) + block[1:2].astype(F32) + block[2:3].astype(F32)


def weights_of(logs, place, target):
    spots = [place ^ k for k in range(len(logs))]
    found = []
    for k, spot in enumerate(spots):
        between = jnp.zeros_like(logs[0])
        for other, log in zip(spots, logs):
            if other is not spot:
                between = between + jnp.where((spot < other) & (other < target), log, 0.0)
        found.append(jnp.where(spot < target, jnp.exp(between), 0.0))
    return found


def carry_of(logs, place, target):
    ahead = jnp.zeros_like(logs[0])
    for k, log in enumerate(logs):
        ahead = ahead + jnp.where((place ^ k) < target, log, 0.0)
    return jnp.exp(ahead)


def up_kernel(stage, following, count, *refs):
    parts, outs = refs[:count], refs[count:]
    place, target = place_of(stage), place_of(following)
    width = outs[0].shape[1]
    chunk = min(256, width)
    order = list(range(1, len(outs))) + [0]
    for k in order:
        for at in range(0, width, chunk):
            start = at if len(outs) == 1 else (target ^ k) * width + at
            at_in = window(start, chunk)
            logs = [logs_of(part[LOG_AT:UP_ROWS, at_in]) for part in parts]
            scale = weights_of(logs, place, count)
            state = sum(
                w * part[:STATE_SIZE, at_in].astype(F32) for w, part in zip(scale, parts)
            )
            outs[k][:STATE_SIZE, at : at + chunk] = state.astype(BF16)
            mine = sum(part[STATE_SIZE:UP_ROWS, at_in].astype(F32) for part in parts)
            total = jnp.concatenate(
                split(sum(logs), 3) + [jnp.zeros((5, chunk), F32)], axis=0
            )
            outs[k][STATE_SIZE:, at : at + chunk] = jnp.concatenate(
                [mine[:24], total], axis=0
            ).astype(BF16)


def top_kernel(stage, count, *refs):
    parts, outs, prompt_ref = refs[:count], refs[count:-1], refs[-1]
    place = place_of(stage)
    width = prompt_ref.shape[1]
    logs = [logs_of(part[LOG_AT:UP_ROWS, :]) for part in parts]
    states = [part[:STATE_SIZE, :].astype(F32) for part in parts]
    final = sum(w * s for w, s in zip(weights_of(logs, place, count), states)).astype(BF16)
    prompt_ref[...] = final
    mine = sum(part[STATE_SIZE:LOG_AT, :].astype(F32) for part in parts)
    reads = mine[16:24, :STATE_SIZE].astype(BF16)
    gated = mine[0:8] + mine[8:16] * dot(reads, final)
    gated = jnp.concatenate(split(gated, 2), axis=0).astype(BF16)
    for k in list(range(1, len(outs))) + [0]:
        scale = weights_of(logs, place, place ^ k)
        outs[k][:STATE_SIZE, :] = sum(w * s for w, s in zip(scale, states)).astype(BF16)
        outs[k][STATE_SIZE:, :] = gated


def down_kernel(stage, above, above_count, count, *refs):
    pieces, parts = refs[:above_count], refs[above_count : above_count + count]
    outs = refs[above_count + count :]
    place, source = place_of(stage), place_of(above)
    width = pieces[0].shape[1]
    chunk = min(256, width)
    for k in list(range(1, len(outs))) + [0]:
        for piece in range(above_count):
            for at in range(0, width, chunk):
                start = at if above_count == 1 else (source ^ piece) * width + at
                at_out = window(start, chunk)
                block = pieces[piece][:, at : at + chunk]
                logs = [logs_of(part[LOG_AT:UP_ROWS, at_out]) for part in parts]
                state = carry_of(logs, place, place ^ k) * block[:STATE_SIZE].astype(F32)
                for w, part in zip(weights_of(logs, place, place ^ k), parts):
                    state = state + w * part[:STATE_SIZE, at_out].astype(F32)
                outs[k][:STATE_SIZE, at_out] = state.astype(BF16)
                outs[k][STATE_SIZE:, at_out] = block[STATE_SIZE:]


def intra_kernel(run_ref, runt_ref, stept_ref, skip_ref, x_ref, write_ref, read_ref, out_ref):
    span = x_ref.shape[0]
    heads = runt_ref.shape[0]
    mid = span // 2
    scores = dot(read_ref[...], write_ref[...], ((1,), (1,)))
    row = lax.broadcasted_iota(jnp.int32, (mid, mid), 0)
    causal = row >= lax.broadcasted_iota(jnp.int32, (mid, mid), 1)
    running = run_ref[0]
    spread = jnp.concatenate(split(skip_ref[...], 3) + [jnp.zeros((5, heads), F32)], axis=0)
    spread = dot(spread.astype(BF16), head_mask(heads, heads, x_ref.shape[1], 0))
    skip = spread[0:1] + spread[1:2] + spread[2:3]
    for pair in range(heads // 2):
        found = []
        for h in (2 * pair, 2 * pair + 1):
            x = x_ref[:, h * HEAD_DIM : (h + 1) * HEAD_DIM]
            t_run, j_run = running[:, h : h + 1], runt_ref[h : h + 1, :]
            step = stept_ref[h : h + 1, :]

            def mixed(rows, cols, masked):
                gap = t_run[rows] - j_run[:, cols]
                if masked:
                    gap = jnp.where(causal, gap, -jnp.inf)
                return (scores[rows, cols] * jnp.exp(gap) * step[:, cols]).astype(BF16)

            low, high = slice(0, mid), slice(mid, span)
            top = dot(mixed(low, low, True), x[low])
            bottom = dot(mixed(high, low, False), x[low]) + dot(mixed(high, high, True), x[high])
            found.append(jnp.concatenate([top, bottom], axis=0))
        at = slice(pair * 2 * HEAD_DIM, (pair + 1) * 2 * HEAD_DIM)
        both = jnp.concatenate(found, axis=1)
        out_ref[:, at] = both + skip[:, at] * x_ref[:, at].astype(F32)


def intra(run, runt, stept, skip, x, write, read, first, number):
    span, lanes = x.shape
    groups, _, per_group = run.shape
    wide = per_group * HEAD_DIM
    return pl.pallas_call(
        intra_kernel,
        name="intra",
        grid=(number,),
        out_shape=shape((span, number * wide), F32),
        in_specs=[
            pl.BlockSpec((1, span, per_group), lambda g: (g + first, 0, 0)),
            pl.BlockSpec((per_group, span), lambda g: (g + first, 0)),
            pl.BlockSpec((per_group, span), lambda g: (g + first, 0)),
            pl.BlockSpec((None, 1, per_group), lambda g: (g + first, 0, 0)),
            pl.BlockSpec((span, wide), lambda g: (0, g + first)),
            pl.BlockSpec((span, STATE_SIZE), lambda g: (0, g + first)),
            pl.BlockSpec((span, STATE_SIZE), lambda g: (0, g + first)),
        ],
        out_specs=pl.BlockSpec((span, wide), lambda g: (0, g)),
        compiler_params=pltpu.CompilerParams(vmem_limit_bytes=32 * 1024 * 1024),
        cost_estimate=pl.CostEstimate(
            flops=number * per_group * span * span * HEAD_DIM * 2,
            bytes_accessed=number * wide * span * 6,
            transcendentals=number * per_group * span * span * 3 // 4,
        ),
    )(run, runt, stept, skip.reshape(groups, 1, per_group), x, write, read)


def finish_kernel(stage, shares, *refs):
    reach_ref, read_ref, own_ref, got_ref = refs[:4]
    base_refs, out_ref = refs[4:-1], refs[-1]
    place = place_of(stage)
    heads = reach_ref.shape[1] // 2
    lanes = out_ref.shape[1]
    wide = lanes // (read_ref.shape[1] // STATE_SIZE)
    half = lanes // 2
    chunk = min(512, half)
    per_base = lanes // shares
    reach = reach_ref[...]
    for lane0 in range(0, lanes, chunk):
        group = lane0 // wide
        at = lane0 % half
        mine = place == lane0 // half
        entering = jnp.where(
            mine, own_ref[:STATE_SIZE, at : at + chunk], got_ref[:STATE_SIZE, at : at + chunk]
        )
        reads = read_ref[:, group * STATE_SIZE : (group + 1) * STATE_SIZE]
        inter = dot(reads, entering) * dot(reach, head_mask(2 * heads, heads, chunk, lane0))
        base = base_refs[lane0 // per_base]
        base_at = lane0 % per_base
        total = inter + base[:, base_at : base_at + chunk]
        out_ref[:, lane0 : lane0 + chunk] = total.astype(BF16)


def resident_kernel(state_ref, vread_ref, q1_ref, q2_ref, gain_ref, out_ref):
    drawn = dot(vread_ref[...], state_ref[...], ((1,), (1,)))
    gated = q1_ref[...] + q2_ref[...] * drawn
    out_ref[...] = normed(gated, gain_ref[...]).astype(BF16)


def normed(gated, gain):
    mean_square = jnp.mean(gated * gated, axis=1, keepdims=True)
    return gated * lax.rsqrt(mean_square + EPSILON) * gain


def resident_hidden(state, vread, q1, q2, gain):
    lanes = state.shape[0]
    groups = vread.shape[1] // STATE_SIZE
    wide = lanes // groups
    return pl.pallas_call(
        resident_kernel,
        name="resident_hidden",
        grid=(groups,),
        out_shape=shape((DRAFTS, lanes), BF16),
        in_specs=[
            pl.BlockSpec((wide, STATE_SIZE), lambda g: (g, 0)),
            pl.BlockSpec((DRAFTS, STATE_SIZE), lambda g: (0, g)),
            pl.BlockSpec((DRAFTS, wide), lambda g: (0, g)),
            pl.BlockSpec((DRAFTS, wide), lambda g: (0, g)),
            pl.BlockSpec((1, wide), lambda g: (0, g)),
        ],
        out_specs=pl.BlockSpec((DRAFTS, wide), lambda g: (0, g)),
        compiler_params=pltpu.CompilerParams(vmem_limit_bytes=32 * 1024 * 1024),
        cost_estimate=pl.CostEstimate(
            flops=2 * DRAFTS * lanes * STATE_SIZE,
            bytes_accessed=lanes * STATE_SIZE * 2,
            transcendentals=0,
        ),
    )(state, vread, q1, q2, gain)


def project_kernel(stages, head_count, *refs):
    owner_ref, own_rows, got_rows, own_ref, got_ref, gain_ref, weight_ref = refs[:7]
    outs = refs[7 : 7 + head_count]
    gated_ref, left_ref, total_ref = refs[7 + head_count :]
    group, groups = pl.program_id(0), pl.num_programs(0)
    here, head = lax.axis_index("seq"), lax.axis_index("head")
    place = place_of(stages[0])
    half = own_ref.shape[1]
    wide = weight_ref.shape[0]
    rows = own_rows.shape[0]

    @pl.when(group == 0)
    def _():
        for k, ref in enumerate((own_ref, got_ref)):
            both = ref[...].astype(F32)
            gated_ref[:, window((place ^ k) * half, half)] = both[0:8] + both[8:16]

    hidden = normed(gated_ref[:, window(group * wide, wide)], gain_ref[...])
    left_ref[0:rows, :] = own_rows[...]
    left_ref[rows : 2 * rows, :] = got_rows[...]
    left_ref[2 * rows :, :] = jnp.concatenate([hidden, jnp.zeros_like(hidden)], axis=0).astype(BF16)
    share = dot(left_ref[...], weight_ref[...])

    @pl.when(group == 0)
    def _():
        total_ref[...] = share

    @pl.when(group > 0)
    def _():
        total_ref[...] += share

    @pl.when(group == groups - 1)
    def _():
        slots = 2 * rows // DRAFTS
        per_head = slots // head_count
        offsets = [0]
        for factor, stride in reversed(stages):
            offsets = [a + k * stride for k in range(factor) for a in offsets]
        owner = owner_ref[0]
        tail = total_ref[2 * rows : 2 * rows + DRAFTS, :]
        for k in range(head_count):
            first = (head ^ k) * per_head
            for slot in range(per_head):
                at = slice(slot * DRAFTS, (slot + 1) * DRAFTS)

                offset = here ^ (first + slot)
                block = jnp.int32(0)
                for position, value in enumerate(offsets):
                    block = jnp.where(offset == value, position, block)
                from_block = total_ref[window(block * DRAFTS, DRAFTS), :]
                outs[k][at, :] = jnp.where(owner == first + slot, tail, from_block)


def project(stages, owner, own_rows, got_rows, own, got, gain, weight, head_count):
    lanes, cols = weight.shape
    rows = own_rows.shape[0]
    wide = gain.shape[1] // (gain.shape[1] // 1024)
    gated_at = STATE_SIZE // 16
    half = lanes // 2
    return pl.pallas_call(
        functools.partial(project_kernel, stages, head_count),
        name="project",
        grid=(lanes // wide,),
        out_shape=[shape((2 * rows // head_count, cols), F32)] * head_count,
        in_specs=[
            pl.BlockSpec(memory_space=pltpu.SMEM),
            pl.BlockSpec((rows, wide), lambda g: (0, g)),
            pl.BlockSpec((rows, wide), lambda g: (0, g)),
            pl.BlockSpec((16, half), lambda g: (gated_at, 0)),
            pl.BlockSpec((16, half), lambda g: (gated_at, 0)),
            pl.BlockSpec((1, wide), lambda g: (0, g)),
            pl.BlockSpec((wide, cols), lambda g: (g, 0)),
        ],
        out_specs=[pl.BlockSpec((2 * rows // head_count, cols), lambda g: (0, 0))] * head_count,
        scratch_shapes=[
            pltpu.VMEM((DRAFTS, lanes), F32),
            pltpu.VMEM((2 * rows + 16, wide), BF16),
            pltpu.VMEM((2 * rows + 16, cols), F32),
        ],
        compiler_params=pltpu.CompilerParams(vmem_limit_bytes=32 * 1024 * 1024),
        cost_estimate=pl.CostEstimate(
            flops=2 * (2 * rows + 16) * lanes * cols,
            bytes_accessed=lanes * cols * 2,
            transcendentals=0,
        ),
    )(owner, own_rows, got_rows, own, got, gain, weight)


def states_kernel(
    stages, scattered, owner_ref, resident_ref, own_ref, got_ref, tail_ref, vwrite_ref, new_ref, slice_ref, turned_ref
):
    here = lax.axis_index("seq")
    lanes = resident_ref.shape[0]
    groups = vwrite_ref.shape[1] // STATE_SIZE
    wide = lanes // groups
    half = lanes // 2
    blocks, width = [(0, 0)], half
    for stage in reversed(scattered):
        blocks = [(a[0] | (k * stage[1]), a[1]) for k in range(stage[0]) for a in blocks]
    width = half // len(blocks)
    for k, ref in enumerate((own_ref, got_ref)):
        for position, (offset, _) in enumerate(blocks):
            spot = here ^ (offset | k)
            lane = lax.rem(spot, 2) * half
            size = half
            for factor, stride in scattered:
                size = size // factor
                lane = lane + lax.rem(lax.div(spot, stride), factor) * size
            block = ref[:, position * width : (position + 1) * width]
            turned_ref[window(lane, width), :] = block.astype(F32).T
    per_slice = slice_ref.shape[1] // STATE_SIZE
    heads = slice_ref.shape[0]
    for k in range(per_slice):
        picked = turned_ref[pl.ds(here * per_slice + k, heads, stride=HEAD_DIM), :]
        slice_ref[:, k * STATE_SIZE : (k + 1) * STATE_SIZE] = picked.astype(BF16)
    is_owner = owner_ref[0] == here
    row = lax.broadcasted_iota(jnp.int32, (32, STATE_SIZE), 0)
    ones = jnp.where((row >= 24) & (row < 27), 1.0, 0.0)
    chunk = min(512, wide)
    for at in range(0, lanes, chunk):
        group = at // wide
        writes = vwrite_ref[:, group * STATE_SIZE : (group + 1) * STATE_SIZE].astype(F32)
        writes = jnp.concatenate([writes, writes, writes, jnp.zeros_like(writes)], axis=0)
        right = jnp.concatenate([writes, ones], axis=1).astype(BF16)
        left = tail_ref[:, at : at + chunk].astype(F32).T.astype(BF16)
        both = dot(left, right)
        start = jnp.where(
            is_owner, turned_ref[at : at + chunk, :], resident_ref[at : at + chunk, :].astype(F32)
        )
        new = start * both[:, STATE_SIZE:] + both[:, :STATE_SIZE]
        new_ref[at : at + chunk, :] = new.astype(BF16)


def on_device(
    prefill_input,
    prefill_step,
    write_proj,
    read_proj,
    decay_rate,
    skip_gain,
    resident_state,
    owner_slot,
    draft_ids,
    accepted_len,
    draft_input,
    draft_gate,
    draft_write,
    draft_read,
    draft_step,
    norm_gain,
    out_weight,
):
    span, lanes = prefill_input.shape
    assert span == BLOCK_LEN
    heads = decay_rate.shape[0]
    groups = write_proj.shape[1] // STATE_SIZE
    per_group = heads // groups
    half = lanes // 2
    seq_count, head_count = lax.axis_size("seq"), lax.axis_size("head")
    stages = tree_stages(seq_count)
    core, line, last = stages
    slots = owner_slot.shape[0]
    assert core[0] == 2 and slots == seq_count
    rate, skip, gain = decay_rate[None], skip_gain[None], norm_gain[None]
    resident = resident_state.reshape(lanes, STATE_SIZE)

    opened = call(
        functools.partial(open_kernel, core),
        "open_block",
        [
            shape((UP_ROWS, half), BF16),
            shape((UP_ROWS, half), BF16),
            shape((groups, span, per_group), F32),
            shape((heads, span), F32),
            shape((heads, span), F32),
            shape((span, 2 * heads), BF16),
            shape((DRAFTS, lanes), F32),
            shape((DRAFTS, lanes), F32),
            shape((DRAFTS, groups * STATE_SIZE), BF16),
            shape((DRAFTS, groups * STATE_SIZE), BF16),
            shape((32, lanes), BF16),
        ],
        (
            prefill_step, rate, skip, prefill_input, write_proj, owner_slot, draft_ids, accepted_len,
            draft_input, draft_gate, draft_write, draft_read, draft_step,
        ),
        smem=(5, 6, 7),
        scratch=[pltpu.VMEM((EXTRA, lanes), BF16)],
        flops=2 * span * lanes * STATE_SIZE * 2,
    )
    own, sent, run, runt, stept, reach, q1, q2, vread, vwrite, tail = opened
    core_parts = [own, swap(sent, "seq", core, 1)]

    line_width = half // line[0]
    split_last = line_width % (last[0] * 128) == 0
    last_width = line_width // last[0] if split_last else line_width
    outs = call(
        functools.partial(up_kernel, core, line, 2),
        "up_line",
        [shape((UP_ROWS, line_width), BF16)] * line[0],
        core_parts,
        flops=half * UP_ROWS * 4,
    )
    line_parts = [outs[0]] + [swap(outs[k], "seq", line, k) for k in range(1, line[0])]
    outs = call(
        functools.partial(up_kernel, line, last, line[0]),
        "up_last",
        [shape((UP_ROWS, last_width), BF16)] * (last[0] if split_last else 1),
        line_parts,
        flops=line_width * UP_ROWS * 4,
    )
    last_parts = [outs[0]] + [
        swap(outs[k if split_last else 0], "seq", last, k) for k in range(1, last[0])
    ]
    *outs, prompt = call(
        functools.partial(top_kernel, last, last[0]),
        "top",
        [shape((DOWN_ROWS, last_width), BF16)] * (last[0] if split_last else 1)
        + [shape((STATE_SIZE, last_width), BF16)],
        last_parts,
        flops=last_width * UP_ROWS * 16,
    )

    pieces = [outs[0]] + [swap(out, "seq", last, k) for k, out in enumerate(outs) if k > 0]
    outs = call(
        functools.partial(down_kernel, line, last, len(pieces), line[0]),
        "down_line",
        [shape((DOWN_ROWS, line_width), BF16)] * line[0],
        pieces + line_parts,
        flops=line_width * UP_ROWS * 8,
    )
    pieces = [outs[0]] + [swap(outs[k], "seq", line, k) for k in range(1, line[0])]
    outs = call(
        functools.partial(down_kernel, core, line, line[0], 2),
        "down_core",
        [shape((DOWN_ROWS, half), BF16)] * 2,
        pieces + core_parts,
        flops=half * UP_ROWS * 8,
    )
    entering = [outs[0], swap(outs[1], "seq", core, 1)]

    number = max(1, groups // 2)
    bases = [
        intra(run, runt, stept, skip, prefill_input, write_proj, read_proj, first, number)
        for first in range(0, groups, number)
    ]
    (prefill_out,) = call(
        functools.partial(finish_kernel, core, len(bases)),
        "finish",
        [shape((span, lanes), BF16)],
        (reach, read_proj, *entering, *bases),
        flops=2 * span * lanes * STATE_SIZE,
    )

    scattered = [line, last] if split_last else [line]
    for stage in reversed(scattered):
        parts = [prompt] + [swap(prompt, "seq", stage, k) for k in range(1, stage[0])]
        prompt = jnp.concatenate(parts, axis=1)
    prompts = [prompt, swap(prompt, "seq", core, 1)]
    new_state, state_slice = call(
        functools.partial(states_kernel, stages, scattered),
        "states",
        [
            shape((lanes, STATE_SIZE), BF16),
            shape((heads, HEAD_DIM // seq_count * STATE_SIZE), BF16),
        ],
        (owner_slot, resident, *prompts, tail, vwrite),
        smem=(0,),
        scratch=[pltpu.VMEM((lanes, STATE_SIZE), F32)],
        flops=2 * lanes * STATE_SIZE * 64,
    )

    hidden = resident_hidden(resident, vread, q1, q2, gain)
    for stage in (last, line):
        parts = [hidden] + [swap(hidden, "seq", stage, k) for k in range(1, stage[0])]
        hidden = jnp.concatenate(parts, axis=0)
    shares = project(
        stages, owner_slot, hidden, swap(hidden, "seq", core, 1), *entering, gain, out_weight, head_count
    )
    verify_out = shares[0]
    for k in range(1, head_count):
        verify_out = verify_out + swap(shares[k], "head", (head_count, 1), k)
    return (
        prefill_out,
        new_state.reshape(1, heads, HEAD_DIM, STATE_SIZE),
        verify_out.astype(BF16),
        state_slice,
    )


def solution(mesh):
    return jax.shard_map(
        on_device,
        mesh=mesh,
        in_specs=(
            P("seq", "head"),
            P("seq", "head"),
            P("seq", "head"),
            P("seq", "head"),
            P("head"),
            P("head"),
            P("seq", "head", None, None),
            P(),
            P(),
            P(),
            P("seq", "head"),
            P("seq", "head"),
            P("seq", "head"),
            P("seq", "head"),
            P("seq", "head"),
            P("head"),
            P("head", "seq"),
        ),
        out_specs=(
            P("seq", "head"),
            P("seq", "head", None, None),
            P("head", "seq"),
            P("head", "seq"),
        ),
        check_vma=False,
    )
```

time: 393 us -> 104 us (0.26)
  waiting for transfers between devices: 265 us -> 36.5 us
  other arithmetic: 53 us -> 1.59 us
  starting transfers between devices: 0.34 us -> 24 us
  Pallas kernels: 0 us -> 23 us
  blocking collectives: 23 us -> 0 us
  matrix products: 19.8 us -> 0 us
  between operations: 14.2 us -> 1.04 us
    all_gather x2 -> x0, waiting for transfers between devices: 177 us -> none  [the longest x1 143 us: carried_in(): everything = jax.tree.map(lambda part: lax.all_gather(part, axis), value)]
    psum x1 -> x0, waiting for transfers between devices: 87.5 us -> none  [from_root(): return lax.psum(block, axis)]
    ppermute x0 -> x21, waiting for transfers between devices: none -> 36.5 us  [swap(): lax.ppermute(value, axis, [(k, k ^ offset * stride) for k in range(count)])]
    select_n x17 -> x0, other arithmetic: 36.2 us -> none  [the longest x16 33.2 us: turn(): return jax.tree.map(lambda a, b: jnp.where(reached, a, b), new, before)]
    ppermute x0 -> x21, starting transfers between devices: none -> 24 us  [swap(): lax.ppermute(value, axis, [(k, k ^ offset * stride) for k in range(count)])]
    all_gather x1 -> x0, blocking collectives: 23 us -> none  [carried_in(): everything = jax.tree.map(lambda part: lax.all_gather(part, axis), value)]
    pallas_call x0 -> x12, Pallas kernels: none -> 23 us  [the longest x8 11.7 us: call(): pl.pallas_call(kernel, name=name, out_shape=outs, in_specs=in_specs, out_...]
    dot_general x14 -> x0, matrix products: 19.8 us -> none  [the longest x1 7.17 us: local_block(): jnp.einsum('gktj,jgkp->tgkp', mixing, incoming_vectors, preferred_element...]
  transfers between devices with their start and end apart: 4 -> 21, of which waited for: 3 -> 9; matrix products, arithmetic and copies ran while one was open for 7% -> 4% of each run, Pallas kernels for 0% -> 18%
where the time goes in v2:
time: 104 us
  waiting for transfers between devices  36.5 us (35%)
  starting transfers between devices  24 us (23%)
  Pallas kernels  23 us (22%)
  local copies, waits for them, and re-layouts  17.7 us (17%)
  other arithmetic  1.59 us (2%)
  between operations  1.04 us (1%)
    ppermute x21, waiting for transfers between devices, swap(): lax.ppermute(value, axis, [(k, k ^ offset * stride) for k in range(count)])  36.5 us
    ppermute x21, starting transfers between devices, swap(): lax.ppermute(value, axis, [(k, k ^ offset * stride) for k in range(count)])  24 us
    unnamed x78, local copies, waits for them, and re-layouts  16.3 us
    pallas_call x8, Pallas kernels, call(): pl.pallas_call(kernel, name=name, out_shape=outs, in_specs=in_specs, out_...  11.7 us
    pallas_call x2, Pallas kernels, intra(): pl.pallas_call(intra_kernel, name='intra', grid=(number,), out_shape=shap...  7.06 us
    pallas_call x1, Pallas kernels, project(): pl.pallas_call(functools.partial(project_kernel, stages, head_count), nam...  3.13 us
  transfers between devices with their start and end apart: 21, of which 9 were waited for; matrix products, arithmetic and copies ran while one was open for 4% of the time, Pallas kernels for 18%

profile of v2, /device:TPU:0, one launch (start us, length us, event | category | flops | bytes accessed | tf_op | source)
XLA Modules:
  0.0 103.9 jit_solution(875802063651506434)
XLA Ops:
  2.3 1.6 %copy-done = bf16[256,4096]{1,0:T(8,128)(2,1)S(1)} copy-done((bf16[256,4096]{1,0:T(8,128)(2,1)S(1)}, bf16[256,4096]{1,0:T(8,128)(2,1)}, u32[]{:S(2)}) %copy-start) | copy-done | bytes 2097176
  11.5 3.6 %open_block.1 = (bf16[160,2048]{1,0:T(8,128)(2,1)S(1)}, bf16[160,2048]{1,0:T(8,128)(2,1)S(1)}, f32[4,256,16]{2,1,0:T(8,128)S(1)}, f32[64,256]{1,0:T(8,128)S(1)},...) custom-call(f32[256,64]{1,0:T(8,128)S(1)} %copy.21.step_ref, ...), custom_call_target="tpu_custom_call" | custom-call | flops 536870912 | bytes 4838528 | tf_op jit(solution)/shard_map/open_block/pallas_call | solution.py:81
  16.3 3.0 %collective-permute-start.15 = (bf16[8,4096]{1,0:T(8,128)(2,1)S(1)}, bf16[8,4096]{1,0:T(8,128)(2,1)S(1)}, u32[]{:S(2)}, u32[]{:S(2)}) collective-permute-start(bf16[8,4096]{1,0:T(8,128)(2,1)S(1)} %resident_hidden.1), channel_id=1, source_target_pairs={{0,8},{2,10},{4,12},{6,14},{8,0},{10,2},{12,4},{14,6},{16,24},{18,... | collective-permute-start | bytes 196616 | tf_op jit(solution)/shard_map/ppermute | solution.py:44
  19.3 2.6 %collective-permute-start.16 = (bf16[8,4096]{1,0:T(8,128)(2,1)S(1)}, bf16[8,4096]{1,0:T(8,128)(2,1)S(1)}, u32[]{:S(2)}, u32[]{:S(2)}) collective-permute-start(bf16[8,4096]{1,0:T(8,128)(2,1)S(1)} %resident_hidden.1), channel_id=1, source_target_pairs={{0,16},{2,18},{4,20},{6,22},{8,24},{10,26},{12,28},{14,30},{16,0},... | collective-permute-start | bytes 196616 | tf_op jit(solution)/shard_map/ppermute | solution.py:44
  21.9 4.7 %collective-permute-done.16 = bf16[8,4096]{1,0:T(8,128)(2,1)S(1)} collective-permute-done((bf16[8,4096]{1,0:T(8,128)(2,1)S(1)}, bf16[8,4096]{1,0:T(8,128)(2,1)S(1)}, u32[]{:S(2)}, u32[]{:S(2)}) %collective-permute-start.16) | collective-permute-done | bytes 65568 | tf_op jit(solution)/shard_map/ppermute | solution.py:44
  26.6 1.4 %collective-permute-done.17 = bf16[8,4096]{1,0:T(8,128)(2,1)S(1)} collective-permute-done((bf16[8,4096]{1,0:T(8,128)(2,1)S(1)}, bf16[8,4096]{1,0:T(8,128)(2,1)S(1)}, u32[]{:S(2)}, u32[]{:S(2)}) %collective-permute-start.17) | collective-permute-done | bytes 65568 | tf_op jit(solution)/shard_map/ppermute | solution.py:44
  28.0 1.6 %collective-permute-start.18 = (bf16[32,4096]{1,0:T(8,128)(2,1)S(1)}, bf16[32,4096]{1,0:T(8,128)(2,1)S(1)}, u32[]{:S(2)}, u32[]{:S(2)}) collective-permute-start(bf16[32,4096]{1,0:T(8,128)(2,1)S(1)} %pad_maximum_fusion.1), channel_id=1, source_target_pairs={{0,4},{2,6},{4,0},{6,2},{8,12},{10,14},{12,8},{14,10},{16,20},{18,... | collective-permute-start | bytes 786440 | tf_op jit(solution)/shard_map/ppermute | solution.py:44
  30.5 11.0 %collective-permute-done.1.refs_1_.refs_5_ = bf16[160,1024]{1,0:T(8,128)(2,1)S(1)} collective-permute-done((bf16[160,1024]{1,0:T(8,128)(2,1)S(1)}, bf16[160,1024]{1,0:T(8,128)(2,1)S(1)}, u32[]{:S(2)}, u32[]{:S(2)}) %collective-permute-start.1) | collective-permute-done | bytes 327712 | tf_op jit(solution)/shard_map/ppermute | solution.py:44
  43.9 2.3 %collective-permute-start.4 = (bf16[160,256]{1,0:T(8,128)(2,1)S(1)}, bf16[160,256]{1,0:T(8,128)(2,1)S(1)}, u32[]{:S(2)}, u32[]{:S(2)}) collective-permute-start(bf16[160,256]{1,0:T(8,128)(2,1)S(1)} %get-tuple-element.42), channel_id=1, source_target_pairs={{0,24},{2,26},{4,28},{6,30},{8,16},{10,18},{12,20},{14,22},{16,8},... | collective-permute-start | bytes 245768 | tf_op jit(solution)/shard_map/ppermute | solution.py:44
  47.5 1.6 %collective-permute-done.3.refs_2_ = bf16[160,256]{1,0:T(8,128)(2,1)S(1)} collective-permute-done((bf16[160,256]{1,0:T(8,128)(2,1)S(1)}, bf16[160,256]{1,0:T(8,128)(2,1)S(1)}, u32[]{:S(2)}, u32[]{:S(2)}) %collective-permute-start.3) | collective-permute-done | bytes 81952 | tf_op jit(solution)/shard_map/ppermute | solution.py:44
  52.8 1.9 %collective-permute-start.11 = (bf16[128,256]{1,0:T(8,128)(2,1)S(1)}, bf16[128,256]{1,0:T(8,128)(2,1)S(1)}, u32[]{:S(2)}, u32[]{:S(2)}) collective-permute-start(bf16[128,256]{1,0:T(8,128)(2,1)S(1)} %get-tuple-element.54), channel_id=1, source_target_pairs={{0,16},{2,18},{4,20},{6,22},{8,24},{10,26},{12,28},{14,30},{16,0},... | collective-permute-start | bytes 196616 | tf_op jit(solution)/shard_map/ppermute | solution.py:44
  54.7 1.6 %collective-permute-start.12 = (bf16[128,256]{1,0:T(8,128)(2,1)S(1)}, bf16[128,256]{1,0:T(8,128)(2,1)S(1)}, u32[]{:S(2)}, u32[]{:S(2)}) collective-permute-start(bf16[128,256]{1,0:T(8,128)(2,1)S(1)} %get-tuple-element.54), channel_id=1, source_target_pairs={{0,24},{2,26},{4,28},{6,30},{8,16},{10,18},{12,20},{14,22},{16,8},... | collective-permute-start | bytes 196616 | tf_op jit(solution)/shard_map/ppermute | solution.py:44
  57.1 1.6 %collective-permute-start.7 = (bf16[144,256]{1,0:T(8,128)(2,1)S(1)}, bf16[144,256]{1,0:T(8,128)(2,1)S(1)}, u32[]{:S(2)}, u32[]{:S(2)}) collective-permute-start(bf16[144,256]{1,0:T(8,128)(2,1)S(1)} %get-tuple-element.46), channel_id=1, source_target_pairs={{0,24},{2,26},{4,28},{6,30},{8,16},{10,18},{12,20},{14,22},{16,8},... | collective-permute-start | bytes 221192 | tf_op jit(solution)/shard_map/ppermute | solution.py:44
  59.3 5.3 %collective-permute-done.6.refs_2_ = bf16[144,256]{1,0:T(8,128)(2,1)S(1)} collective-permute-done((bf16[144,256]{1,0:T(8,128)(2,1)S(1)}, bf16[144,256]{1,0:T(8,128)(2,1)S(1)}, u32[]{:S(2)}, u32[]{:S(2)}) %collective-permute-start.6) | collective-permute-done | bytes 73760 | tf_op jit(solution)/shard_map/ppermute | solution.py:44
  64.9 1.6 %collective-permute-start.8 = (bf16[144,1024]{1,0:T(8,128)(2,1)S(1)}, bf16[144,1024]{1,0:T(8,128)(2,1)S(1)}, u32[]{:S(2)}, u32[]{:S(2)}) collective-permute-start(bf16[144,1024]{1,0:T(8,128)(2,1)S(1)} %get-tuple-element.48), channel_id=1, source_target_pairs={{0,4},{2,6},{4,0},{6,2},{8,12},{10,14},{12,8},{14,10},{16,20},{18,... | collective-permute-start | bytes 884744 | tf_op jit(solution)/shard_map/ppermute | solution.py:44
  68.4 6.4 %collective-permute-done.8.refs_1_ = bf16[144,1024]{1,0:T(8,128)(2,1)S(1)} collective-permute-done((bf16[144,1024]{1,0:T(8,128)(2,1)S(1)}, bf16[144,1024]{1,0:T(8,128)(2,1)S(1)}, u32[]{:S(2)}, u32[]{:S(2)}) %collective-permute-start.8) | collective-permute-done | bytes 294944 | tf_op jit(solution)/shard_map/ppermute | solution.py:44
  76.4 3.6 %collective-permute-done.13 = bf16[128,1024]{1,0:T(8,128)(2,1)S(1)} collective-permute-done((bf16[128,1024]{1,0:T(8,128)(2,1)S(1)}, bf16[128,1024]{1,0:T(8,128)(2,1)S(1)}, u32[]{:S(2)}, u32[]{:S(2)}) %collective-permute-start.13) | collective-permute-done | bytes 262176 | tf_op jit(solution)/shard_map/ppermute | solution.py:44
  80.8 3.1 %project.1 = (f32[64,512]{1,0:T(8,128)S(1)}, f32[64,512]{1,0:T(8,128)}) custom-call(s32[16]{0:T(128)S(1)} %copy-done.29, bf16[64,4096]{1,0:T(8,128)(2,1)S(1)} %constant_dynamic-update-slice_fusion.5.refs_1_, bf16[64,4096]{1,0:T(8,128)(2,1)S(1)} %collective-permute-done.19.refs_2_, bf16[144,2048]{1,0:T(8,128)(2,1)S(1)} %get-tuple-element.49.refs_2_.refs_3_, ...), custom_call_target="tpu_custom_call" | custom-call | flops 603979776 | bytes 4194304 | tf_op jit(solution)/shard_map/project/pallas_call | solution.py:501
  84.6 1.5 %collective-permute-start.20 = (f32[64,512]{1,0:T(8,128)}, f32[64,512]{1,0:T(8,128)}, u32[]{:S(2)}, u32[]{:S(2)}) collective-permute-start(f32[64,512]{1,0:T(8,128)} %get-tuple-element.62), channel_id=1, source_target_pairs={{0,1},{1,0},{2,3},{3,2},{4,5},{5,4},{6,7},{7,6},{8,9},{9,8},{10,11... | collective-permute-start | bytes 393224 | tf_op jit(solution)/shard_map/ppermute | solution.py:44
  88.9 3.5 %intra.2.refs_4_ = f32[256,2048]{1,0:T(8,128)S(1)} custom-call(f32[4,256,16]{2,1,0:T(8,128)S(1)} %copy-done.13, f32[64,256]{1,0:T(8,128)S(1)} %get-tuple-element.52.runt_ref, f32[64,256]{1,0:T(8,128)S(1)} %get-tuple-element.53.stept_ref, f32[4,1,16]{2,1,0:T(1,128)S(1)} %bitcast.10, bf16[256,4096]{1,0:T(8,128)(2,1)S(1)} %copy-done.1, ...), custom_call_target="tpu_custom_call" | custom-call | flops 268435456 | bytes 3145728 | tf_op jit(solution)/shard_map/intra/pallas_call | solution.py:355
  92.4 3.5 %intra.3.refs_5_ = f32[256,2048]{1,0:T(8,128)S(1)} custom-call(f32[4,256,16]{2,1,0:T(8,128)S(1)} %copy-done.13, f32[64,256]{1,0:T(8,128)S(1)} %get-tuple-element.52.runt_ref, f32[64,256]{1,0:T(8,128)S(1)} %get-tuple-element.53.stept_ref, f32[4,1,16]{2,1,0:T(1,128)S(1)} %bitcast.11, bf16[256,4096]{1,0:T(8,128)(2,1)S(1)} %copy-done.1, ...), custom_call_target="tpu_custom_call" | custom-call | flops 268435456 | bytes 3145728 | tf_op jit(solution)/shard_map/intra/pallas_call | solution.py:355
  96.1 3.5 %states.1 = (bf16[4096,128]{1,0:T(8,128)(2,1)}, bf16[64,512]{1,0:T(8,128)(2,1)}) custom-call(s32[16]{0:T(128)S(1)} %copy-done.30, bf16[4096,128]{1,0:T(8,128)(2,1)S(1)} %bitcast.7, bf16[128,2048]{1,0:T(8,128)(2,1)} %constant_dynamic-update-slice_fusion.own_ref, bf16[128,2048]{1,0:T(8,128)(2,1)} %collective-permute-done.14.got_ref, ...), custom_call_target="tpu_custom_call" | custom-call | flops 67108864 | bytes 3481664 | tf_op jit(solution)/shard_map/states/pallas_call | solution.py:81
  99.6 2.7 %finish.1 = bf16[256,4096]{1,0:T(8,128)(2,1)} custom-call(bf16[256,128]{1,0:T(8,128)(2,1)S(1)} %copy-done.21, bf16[256,512]{1,0:T(8,128)(2,1)S(1)} %copy-done.11, bf16[144,2048]{1,0:T(8,128)(2,1)S(1)} %copy-done.7, bf16[144,2048]{1,0:T(8,128)(2,1)S(1)} %copy-done.9, f32[256,2048]{1,0:T(8,128)S(1)} %intra.2.refs_4_, f32[256,2048]{1,0:T(8,128)S(1)} %intra.3.refs_5_), custom_call_target="tpu_custom_call" | custom-call | flops 268435456 | bytes 7798784 | tf_op jit(solution)/shard_map/finish/pallas_call | solution.py:81
  102.3 1.6 %add_convert_fusion = bf16[64,512]{1,0:T(8,128)(2,1)} fusion(f32[64,512]{1,0:T(8,128)S(1)} %copy-done.19, f32[64,512]{1,0:T(8,128)} %collective-permute-done.20), kind=kLoop, calls=%fused_computation.2 | loop fusion | flops 65536 | bytes 327680 | tf_op jit(solution)/shard_map/convert_element_type | solution.py:727
  (114 shorter events, 28.0 us)
Async XLA Ops:
  15.1 26.6 %copy-start.12 = (f32[4,256,16]{2,1,0:T(8,128)}, f32[4,256,16]{2,1,0:T(8,128)S(1)}, u32[]{:S(2)}) copy-start(f32[4,256,16]{2,1,0:T(8,128)S(1)} %get-tuple-element.51.run_ref) | copy-start | bytes 196612
  15.1 26.6 %copy-start.14 = (bf16[32,4096]{1,0:T(8,128)(2,1)}, bf16[32,4096]{1,0:T(8,128)(2,1)S(1)}, u32[]{:S(2)}) copy-start(bf16[32,4096]{1,0:T(8,128)(2,1)S(1)} %get-tuple-element.55.tail_ref) | copy-start | bytes 786436
  15.1 26.6 %copy-start.20 = (bf16[256,128]{1,0:T(8,128)(2,1)}, bf16[256,128]{1,0:T(8,128)(2,1)S(1)}, u32[]{:S(2)}) copy-start(bf16[256,128]{1,0:T(8,128)(2,1)S(1)} %get-tuple-element.34.refs_0_) | copy-start | bytes 196612
  16.3 5.7 %collective-permute-start.15 = (bf16[8,4096]{1,0:T(8,128)(2,1)S(1)}, bf16[8,4096]{1,0:T(8,128)(2,1)S(1)}, u32[]{:S(2)}, u32[]{:S(2)}) collective-permute-start(bf16[8,4096]{1,0:T(8,128)(2,1)S(1)} %resident_hidden.1), channel_id=1, source_target_pairs={{0,8},{2,10},{4,12},{6,14},{8,0},{10,2},{12,4},{14,6},{16,24},{18,... | collective-permute-start | bytes 196616 | tf_op jit(solution)/shard_map/ppermute | solution.py:44
  19.3 7.3 %collective-permute-start.16 = (bf16[8,4096]{1,0:T(8,128)(2,1)S(1)}, bf16[8,4096]{1,0:T(8,128)(2,1)S(1)}, u32[]{:S(2)}, u32[]{:S(2)}) collective-permute-start(bf16[8,4096]{1,0:T(8,128)(2,1)S(1)} %resident_hidden.1), channel_id=1, source_target_pairs={{0,16},{2,18},{4,20},{6,22},{8,24},{10,26},{12,28},{14,30},{16,0},... | collective-permute-start | bytes 196616 | tf_op jit(solution)/shard_map/ppermute | solution.py:44
  21.9 6.1 %collective-permute-start.17 = (bf16[8,4096]{1,0:T(8,128)(2,1)S(1)}, bf16[8,4096]{1,0:T(8,128)(2,1)S(1)}, u32[]{:S(2)}, u32[]{:S(2)}) collective-permute-start(bf16[8,4096]{1,0:T(8,128)(2,1)S(1)} %resident_hidden.1), channel_id=1, source_target_pairs={{0,24},{2,26},{4,28},{6,30},{8,16},{10,18},{12,20},{14,22},{16,8},... | collective-permute-start | bytes 196616 | tf_op jit(solution)/shard_map/ppermute | solution.py:44
  21.9 7.7 %collective-permute-start = (bf16[160,2048]{1,0:T(8,128)(2,1)S(1)}, bf16[160,2048]{1,0:T(8,128)(2,1)S(1)}, u32[]{:S(2)}, u32[]{:S(2)}) collective-permute-start(bf16[160,2048]{1,0:T(8,128)(2,1)S(1)} %get-tuple-element.36), channel_id=1, source_target_pairs={{0,2},{2,0},{4,6},{6,4},{8,10},{10,8},{12,14},{14,12},{16,18},{18,... | collective-permute-start | bytes 1966088 | tf_op jit(solution)/shard_map/ppermute | solution.py:44
  28.0 23.7 %collective-permute-start.18 = (bf16[32,4096]{1,0:T(8,128)(2,1)S(1)}, bf16[32,4096]{1,0:T(8,128)(2,1)S(1)}, u32[]{:S(2)}, u32[]{:S(2)}) collective-permute-start(bf16[32,4096]{1,0:T(8,128)(2,1)S(1)} %pad_maximum_fusion.1), channel_id=1, source_target_pairs={{0,4},{2,6},{4,0},{6,2},{8,12},{10,14},{12,8},{14,10},{16,20},{18,... | collective-permute-start | bytes 786440 | tf_op jit(solution)/shard_map/ppermute | solution.py:44
  29.9 11.6 %collective-permute-start.1 = (bf16[160,1024]{1,0:T(8,128)(2,1)S(1)}, bf16[160,1024]{1,0:T(8,128)(2,1)S(1)}, u32[]{:S(2)}, u32[]{:S(2)}) collective-permute-start(bf16[160,1024]{1,0:T(8,128)(2,1)S(1)} %get-tuple-element.38), channel_id=1, source_target_pairs={{0,4},{2,6},{4,0},{6,2},{8,12},{10,14},{12,8},{14,10},{16,20},{18,... | collective-permute-start | bytes 983048 | tf_op jit(solution)/shard_map/ppermute | solution.py:44
  41.7 5.7 %collective-permute-start.2 = (bf16[160,256]{1,0:T(8,128)(2,1)S(1)}, bf16[160,256]{1,0:T(8,128)(2,1)S(1)}, u32[]{:S(2)}, u32[]{:S(2)}) collective-permute-start(bf16[160,256]{1,0:T(8,128)(2,1)S(1)} %get-tuple-element.40), channel_id=1, source_target_pairs={{0,8},{2,10},{4,12},{6,14},{8,0},{10,2},{12,4},{14,6},{16,24},{18,... | collective-permute-start | bytes 245768 | tf_op jit(solution)/shard_map/ppermute | solution.py:44
  42.5 6.6 %collective-permute-start.3 = (bf16[160,256]{1,0:T(8,128)(2,1)S(1)}, bf16[160,256]{1,0:T(8,128)(2,1)S(1)}, u32[]{:S(2)}, u32[]{:S(2)}) collective-permute-start(bf16[160,256]{1,0:T(8,128)(2,1)S(1)} %get-tuple-element.41), channel_id=1, source_target_pairs={{0,16},{2,18},{4,20},{6,22},{8,24},{10,26},{12,28},{14,30},{16,0},... | collective-permute-start | bytes 245768 | tf_op jit(solution)/shard_map/ppermute | solution.py:44
  43.9 6.4 %collective-permute-start.4 = (bf16[160,256]{1,0:T(8,128)(2,1)S(1)}, bf16[160,256]{1,0:T(8,128)(2,1)S(1)}, u32[]{:S(2)}, u32[]{:S(2)}) collective-permute-start(bf16[160,256]{1,0:T(8,128)(2,1)S(1)} %get-tuple-element.42), channel_id=1, source_target_pairs={{0,24},{2,26},{4,28},{6,30},{8,16},{10,18},{12,20},{14,22},{16,8},... | collective-permute-start | bytes 245768 | tf_op jit(solution)/shard_map/ppermute | solution.py:44
  50.6 6.5 %collective-permute-start.5 = (bf16[144,256]{1,0:T(8,128)(2,1)S(1)}, bf16[144,256]{1,0:T(8,128)(2,1)S(1)}, u32[]{:S(2)}, u32[]{:S(2)}) collective-permute-start(bf16[144,256]{1,0:T(8,128)(2,1)S(1)} %get-tuple-element.44), channel_id=1, source_target_pairs={{0,8},{2,10},{4,12},{6,14},{8,0},{10,2},{12,4},{14,6},{16,24},{18,... | collective-permute-start | bytes 221192 | tf_op jit(solution)/shard_map/ppermute | solution.py:44
  51.8 14.8 %collective-permute-start.10 = (bf16[128,256]{1,0:T(8,128)(2,1)S(1)}, bf16[128,256]{1,0:T(8,128)(2,1)S(1)}, u32[]{:S(2)}, u32[]{:S(2)}) collective-permute-start(bf16[128,256]{1,0:T(8,128)(2,1)S(1)} %get-tuple-element.54), channel_id=1, source_target_pairs={{0,8},{2,10},{4,12},{6,14},{8,0},{10,2},{12,4},{14,6},{16,24},{18,... | collective-permute-start | bytes 196616 | tf_op jit(solution)/shard_map/ppermute | solution.py:44
  52.8 13.8 %collective-permute-start.11 = (bf16[128,256]{1,0:T(8,128)(2,1)S(1)}, bf16[128,256]{1,0:T(8,128)(2,1)S(1)}, u32[]{:S(2)}, u32[]{:S(2)}) collective-permute-start(bf16[128,256]{1,0:T(8,128)(2,1)S(1)} %get-tuple-element.54), channel_id=1, source_target_pairs={{0,16},{2,18},{4,20},{6,22},{8,24},{10,26},{12,28},{14,30},{16,0},... | collective-permute-start | bytes 196616 | tf_op jit(solution)/shard_map/ppermute | solution.py:44
  54.7 11.9 %collective-permute-start.12 = (bf16[128,256]{1,0:T(8,128)(2,1)S(1)}, bf16[128,256]{1,0:T(8,128)(2,1)S(1)}, u32[]{:S(2)}, u32[]{:S(2)}) collective-permute-start(bf16[128,256]{1,0:T(8,128)(2,1)S(1)} %get-tuple-element.54), channel_id=1, source_target_pairs={{0,24},{2,26},{4,28},{6,30},{8,16},{10,18},{12,20},{14,22},{16,8},... | collective-permute-start | bytes 196616 | tf_op jit(solution)/shard_map/ppermute | solution.py:44
  56.2 8.3 %collective-permute-start.6 = (bf16[144,256]{1,0:T(8,128)(2,1)S(1)}, bf16[144,256]{1,0:T(8,128)(2,1)S(1)}, u32[]{:S(2)}, u32[]{:S(2)}) collective-permute-start(bf16[144,256]{1,0:T(8,128)(2,1)S(1)} %get-tuple-element.45), channel_id=1, source_target_pairs={{0,16},{2,18},{4,20},{6,22},{8,24},{10,26},{12,28},{14,30},{16,0},... | collective-permute-start | bytes 221192 | tf_op jit(solution)/shard_map/ppermute | solution.py:44
  57.1 7.5 %collective-permute-start.7 = (bf16[144,256]{1,0:T(8,128)(2,1)S(1)}, bf16[144,256]{1,0:T(8,128)(2,1)S(1)}, u32[]{:S(2)}, u32[]{:S(2)}) collective-permute-start(bf16[144,256]{1,0:T(8,128)(2,1)S(1)} %get-tuple-element.46), channel_id=1, source_target_pairs={{0,24},{2,26},{4,28},{6,30},{8,16},{10,18},{12,20},{14,22},{16,8},... | collective-permute-start | bytes 221192 | tf_op jit(solution)/shard_map/ppermute | solution.py:44
  64.6 16.2 %collective-permute-start.19 = (bf16[64,4096]{1,0:T(8,128)(2,1)S(1)}, bf16[64,4096]{1,0:T(8,128)(2,1)S(1)}, u32[]{:S(2)}, u32[]{:S(2)}) collective-permute-start(bf16[64,4096]{1,0:T(8,128)(2,1)S(1)} %constant_dynamic-update-slice_fusion.5.refs_1_), channel_id=1, source_target_pairs={{0,2},{2,0},{4,6},{6,4},{8,10},{10,8},{12,14},{14,12},{16,18},{18,... | collective-permute-start | bytes 1572872 | tf_op jit(solution)/shard_map/ppermute | solution.py:44
  64.9 9.9 %collective-permute-start.8 = (bf16[144,1024]{1,0:T(8,128)(2,1)S(1)}, bf16[144,1024]{1,0:T(8,128)(2,1)S(1)}, u32[]{:S(2)}, u32[]{:S(2)}) collective-permute-start(bf16[144,1024]{1,0:T(8,128)(2,1)S(1)} %get-tuple-element.48), channel_id=1, source_target_pairs={{0,4},{2,6},{4,0},{6,2},{8,12},{10,14},{12,8},{14,10},{16,20},{18,... | collective-permute-start | bytes 884744 | tf_op jit(solution)/shard_map/ppermute | solution.py:44
  66.6 13.4 %collective-permute-start.13 = (bf16[128,1024]{1,0:T(8,128)(2,1)S(1)}, bf16[128,1024]{1,0:T(8,128)(2,1)S(1)}, u32[]{:S(2)}, u32[]{:S(2)}) collective-permute-start(bf16[128,1024]{1,0:T(8,128)(2,1)S(1)} %pad_maximum_fusion), channel_id=1, source_target_pairs={{0,4},{2,6},{4,0},{6,2},{8,12},{10,14},{12,8},{14,10},{16,20},{18,... | collective-permute-start | bytes 786440 | tf_op jit(solution)/shard_map/ppermute | solution.py:44
  75.6 5.2 %collective-permute-start.9 = (bf16[144,2048]{1,0:T(8,128)(2,1)S(1)}, bf16[144,2048]{1,0:T(8,128)(2,1)S(1)}, u32[]{:S(2)}, u32[]{:S(2)}) collective-permute-start(bf16[144,2048]{1,0:T(8,128)(2,1)S(1)} %get-tuple-element.50), channel_id=1, source_target_pairs={{0,2},{2,0},{4,6},{6,4},{8,10},{10,8},{12,14},{14,12},{16,18},{18,... | collective-permute-start | bytes 1769480 | tf_op jit(solution)/shard_map/ppermute | solution.py:44
  80.8 15.3 %collective-permute-start.14 = (bf16[128,2048]{1,0:T(8,128)(2,1)}, bf16[128,2048]{1,0:T(8,128)(2,1)}, u32[]{:S(2)}, u32[]{:S(2)}) collective-permute-start(bf16[128,2048]{1,0:T(8,128)(2,1)} %constant_dynamic-update-slice_fusion.own_ref), channel_id=1, source_target_pairs={{0,2},{2,0},{4,6},{6,4},{8,10},{10,8},{12,14},{14,12},{16,18},{18,... | collective-permute-start | bytes 1572872 | tf_op jit(solution)/shard_map/ppermute | solution.py:44
  84.6 17.7 %collective-permute-start.20 = (f32[64,512]{1,0:T(8,128)}, f32[64,512]{1,0:T(8,128)}, u32[]{:S(2)}, u32[]{:S(2)}) collective-permute-start(f32[64,512]{1,0:T(8,128)} %get-tuple-element.62), channel_id=1, source_target_pairs={{0,1},{1,0},{2,3},{3,2},{4,5},{5,4},{6,7},{7,6},{8,9},{9,8},{10,11... | collective-permute-start | bytes 393224 | tf_op jit(solution)/shard_map/ppermute | solution.py:44
  (31 other events, 140.7 us)

commit v3 on v2

v3 whole, which is shorter than its diff:
```python
import functools

import jax
import jax.numpy as jnp
from jax import lax
from jax.experimental import pallas as pl
from jax.experimental.pallas import tpu as pltpu
from jax.sharding import PartitionSpec as P

HEAD_DIM = 64
STATE_SIZE = 128
BLOCK_LEN = 256
DRAFTS = 8
EPSILON = 1e-05
EXTRA = 32
UP_ROWS = STATE_SIZE + EXTRA
READ_AT = STATE_SIZE + 16
LOG_AT = STATE_SIZE + 24
DOWN_ROWS = STATE_SIZE + 16

F32 = jnp.float32
BF16 = jnp.bfloat16


def tree_stages(count):
    factors, rest = [], count
    if rest > 1:
        factors.append(2)
        rest //= 2
    inner = 1
    while inner * inner * 4 <= rest:
        inner *= 2
    factors += [inner, rest // inner]
    stages, stride = [], 1
    for factor in factors:
        stages.append((factor, stride))
        stride *= factor
    assert stride == count
    return stages


def swap(value, axis, stage, offset):
    count, stride = lax.axis_size(axis), stage[1]
    return lax.ppermute(value, axis, [(k, k ^ (offset * stride)) for k in range(count)])


def place_of(stage):
    factor, stride = stage
    return lax.rem(lax.div(lax.axis_index("seq"), stride), factor)


def dot(a, b, dims=((1,), (0,))):
    return lax.dot_general(a, b, (dims, ((), ())), preferred_element_type=F32)


def split(value, parts):
    found = []
    for _ in range(parts):
        part = value.astype(BF16).astype(F32)
        found.append(part)
        value = value - part
    return found


def head_mask(rows, heads, lanes, lane0):
    row = lax.broadcasted_iota(jnp.int32, (rows, lanes), 0) & (heads - 1)
    head = lax.shift_right_logical(lax.broadcasted_iota(jnp.int32, (rows, lanes), 1) + lane0, 6)
    return jnp.where(row == head, 1.0, 0.0).astype(BF16)


def window(start, size):
    return pl.ds(pl.multiple_of(start, size), size)


def ordered(kernel, count):
    return lambda *refs: kernel(*refs[count:])


ANYWHERE = pl.BlockSpec(memory_space=pl.ANY)
WHOLE = pl.BlockSpec(memory_space=pltpu.VMEM)
IN_HBM = pl.BlockSpec(memory_space=pltpu.HBM)


def call(
    kernel, name, outs, args, specs=None, out_specs=None, grid=(), after=(), scratch=(), alias=None,
    flops=0, exps=0, moved=None, vmem=32,
):
    if specs is None:
        specs = [WHOLE] * len(args)
    if out_specs is None:
        out_specs = [WHOLE] * len(outs)
    if moved is None:
        moved = sum(a.size * a.dtype.itemsize for a in (*args, *outs))
    first = len(after)
    return pl.pallas_call(
        ordered(kernel, first),
        name=name,
        grid=grid,
        out_shape=outs,
        in_specs=[ANYWHERE] * first + specs,
        out_specs=out_specs,
        scratch_shapes=list(scratch),
        input_output_aliases={first + k: v for k, v in (alias or {}).items()},
        compiler_params=pltpu.CompilerParams(vmem_limit_bytes=vmem * 1024 * 1024),
        cost_estimate=pl.CostEstimate(flops=flops, bytes_accessed=moved, transcendentals=exps),
    )(*after, *args)


def in_hbm(value):
    return pltpu.with_memory_space_constraint(value, pltpu.HBM)


def shape(dims, dtype):
    return jax.ShapeDtypeStruct(dims, dtype)


def open_kernel(stage, count, *refs):
    sources, rest = refs[:count], refs[count:]
    outs, scratch = rest[:13], rest[13:]
    own_ref, sent_ref, run_ref, runt_ref, stept_ref, reach_ref, skip_out = outs[:7]
    q1_ref, q2_ref, vread_ref, vwrite_ref, tail_ref, owner_out = outs[7:]
    extra_ref, sems, held = scratch[0], scratch[1], scratch[2:]
    fetches = [
        pltpu.make_async_copy(source, target, sems.at[k])
        for k, (source, target) in enumerate(zip(sources, held))
    ]
    for fetch in fetches:
        fetch.start()
    for fetch in fetches[:-2]:
        fetch.wait()
    turned_ref, rate_ref, skip_ref, owner_ref, ids_ref, kept_ref = held[:6]
    din_ref, dgate_ref, dwrite_ref, dread_ref, dstep_ref, write_ref, x_ref = held[6:]
    heads, span = turned_ref.shape
    lanes = x_ref.shape[1]
    groups = write_ref.shape[1] // STATE_SIZE
    per_group = heads // groups
    wide = per_group * HEAD_DIM
    here = lax.axis_index("seq")
    place = place_of(stage)
    owner_out[...] = jnp.zeros(owner_out.shape, jnp.int32) + owner_ref[0]

    step_rows = turned_ref[...]
    stept_ref[...] = step_rows
    pad = (-heads) % 128
    if pad:
        step_rows = jnp.concatenate([step_rows, jnp.zeros((pad, span), F32)], axis=0)
    step = step_rows.T[:, :heads]
    log_decay = -step * rate_ref[...]
    lower = lax.broadcasted_iota(jnp.int32, (span, span), 0) >= lax.broadcasted_iota(
        jnp.int32, (span, span), 1
    )
    lower = jnp.where(lower, 1.0, 0.0).astype(BF16)
    running = sum(dot(lower, part.astype(BF16)) for part in split(log_decay, 3))
    total = running[span - 1 : span, :]
    to_end = jnp.exp(total - running) * step
    wide_run = running
    if pad:
        wide_run = jnp.concatenate([running, jnp.zeros((span, pad), F32)], axis=1)
    runt_ref[...] = wide_run.T[:heads]
    for g in range(groups):
        run_ref[g] = running[:, g * per_group : (g + 1) * per_group]
    reach_ref[...] = jnp.concatenate(split(jnp.exp(running), 2), axis=1).astype(BF16)
    end_parts = jnp.concatenate(split(to_end, 2), axis=1).astype(BF16)

    slots = owner_ref.shape[0]
    request = lax.fori_loop(
        0, slots, lambda r, found: jnp.where(owner_ref[r] == here, r, found), jnp.int32(0)
    )
    kept = kept_ref[request]
    candidates = din_ref.shape[0]
    row = lax.broadcasted_iota(jnp.int32, (DRAFTS, candidates), 0)
    col = lax.broadcasted_iota(jnp.int32, (DRAFTS, candidates), 1)
    pick = jnp.zeros((DRAFTS, candidates), F32)
    for i in range(DRAFTS):
        pick = jnp.where((row == i) & (col == ids_ref[i, request]), 1.0, pick)
    pick = pick.astype(BF16)
    vin = dot(pick, din_ref[...])
    vgate = dot(pick, dgate_ref[...])
    vwrite = dot(pick, dwrite_ref[...]).astype(BF16)
    vread = dot(pick, dread_ref[...]).astype(BF16)
    vwrite_ref[...] = vwrite
    vread_ref[...] = vread
    vstep = sum(dot(pick, part.astype(BF16)) for part in split(dstep_ref[...], 3))
    vlog = -vstep * rate_ref[...]
    index = lax.broadcasted_iota(jnp.int32, (DRAFTS, heads), 0)
    acc = jnp.zeros((1, heads), F32)
    vrun = jnp.zeros((DRAFTS, heads), F32)
    reach = jnp.zeros((1, heads), F32)
    for i in range(DRAFTS):
        acc = acc + vlog[i : i + 1]
        vrun = jnp.where(index == i, acc, vrun)
        reach = jnp.where(i < kept, acc, reach)
    others = jnp.where(index == 0, total, jnp.where(index == 1, skip_ref[...], reach))
    stacked = split(jnp.concatenate([vrun, vstep, others], axis=0), 3)
    stacked = jnp.concatenate(stacked, axis=0).astype(BF16)
    row = lax.broadcasted_iota(jnp.int32, (DRAFTS, wide), 0)
    is_owner = owner_ref[0] == here
    for g in range(groups):
        at = slice(g * wide, (g + 1) * wide)
        spread = dot(stacked, head_mask(heads, heads, wide, g * wide))
        spread = spread[0:24] + spread[24:48] + spread[48:72]
        vrun_l, vstep_l = spread[0:8], spread[8:16]
        total_l, skip_l, reach_l = spread[16:17], spread[17:18], spread[18:19]
        skip_out[:, at] = skip_l
        vin_g = vin[:, at]
        vr = vread[:, g * STATE_SIZE : (g + 1) * STATE_SIZE]
        vw = vwrite[:, g * STATE_SIZE : (g + 1) * STATE_SIZE]
        scores = dot(vr, vw, ((1,), (1,)))
        direct = skip_l * vin_g
        for j in range(DRAFTS):
            decay = jnp.exp(jnp.where(row >= j, vrun_l - vrun_l[j : j + 1], -jnp.inf))
            direct = direct + decay * scores[:, j : j + 1] * (vstep_l[j : j + 1] * vin_g[j : j + 1])
        gate = vgate[:, at]
        gate = gate / (1.0 + jnp.exp(-gate))
        q1 = direct * gate
        q2 = jnp.exp(vrun_l) * gate
        q1_ref[:, at] = q1
        q2_ref[:, at] = q2
        live = jnp.exp(jnp.where(row < kept, reach_l - vrun_l, -jnp.inf)) * vstep_l * vin_g
        keep_l = jnp.concatenate(
            split(jnp.exp(reach_l), 3) + [jnp.zeros((5, wide), F32)], axis=0
        )
        tail_ref[:, at] = jnp.concatenate(split(live, 3) + [keep_l], axis=0).astype(BF16)
        read_l = jnp.concatenate([vr.astype(F32)] * (wide // STATE_SIZE), axis=1)
        mine = jnp.concatenate([q1, q2, read_l], axis=0)
        mine = jnp.where(is_owner, mine, 0.0)
        logs = jnp.concatenate(split(total_l, 3) + [jnp.zeros((5, wide), F32)], axis=0)
        extra_ref[:, at] = jnp.concatenate([mine, logs], axis=0).astype(BF16)

    for fetch in fetches[-2:]:
        fetch.wait()
    half = lanes // 2
    chunk = min(wide, half)
    for k, out_ref in ((1, sent_ref), (0, own_ref)):
        start = (place ^ k) * half
        out_ref[STATE_SIZE:, :] = extra_ref[:, window(start, half)]
        for at in range(0, half, chunk):
            lane0 = start + at
            group = lax.div(lane0, wide)
            scale = dot(end_parts, head_mask(2 * heads, heads, chunk, lane0))
            weighted = (x_ref[:, window(lane0, chunk)].astype(F32) * scale).astype(BF16)
            writes = write_ref[:, window(group * STATE_SIZE, STATE_SIZE)]
            writes = writes.astype(F32).T.astype(BF16)
            out_ref[:STATE_SIZE, at : at + chunk] = dot(writes, weighted).astype(BF16)


def logs_of(block):
    return block[0:1].astype(F32) + block[1:2].astype(F32) + block[2:3].astype(F32)


def weights_of(logs, place, target):
    spots = [place ^ k for k in range(len(logs))]
    found = []
    for k, spot in enumerate(spots):
        between = jnp.zeros_like(logs[0])
        for other, log in zip(spots, logs):
            if other is not spot:
                between = between + jnp.where((spot < other) & (other < target), log, 0.0)
        found.append(jnp.where(spot < target, jnp.exp(between), 0.0))
    return found


def carry_of(logs, place, target):
    ahead = jnp.zeros_like(logs[0])
    for k, log in enumerate(logs):
        ahead = ahead + jnp.where((place ^ k) < target, log, 0.0)
    return jnp.exp(ahead)


def up_kernel(stage, following, count, *refs):
    parts, outs = refs[:count], refs[count:]
    place, target = place_of(stage), place_of(following)
    width = outs[0].shape[1]
    chunk = min(256, width)
    order = list(range(1, len(outs))) + [0]
    for k in order:
        for at in range(0, width, chunk):
            start = at if len(outs) == 1 else (target ^ k) * width + at
            at_in = window(start, chunk)
            logs = [logs_of(part[LOG_AT:UP_ROWS, at_in]) for part in parts]
            scale = weights_of(logs, place, count)
            state = sum(
                w * part[:STATE_SIZE, at_in].astype(F32) for w, part in zip(scale, parts)
            )
            outs[k][:STATE_SIZE, at : at + chunk] = state.astype(BF16)
            mine = sum(part[STATE_SIZE:UP_ROWS, at_in].astype(F32) for part in parts)
            total = jnp.concatenate(
                split(sum(logs), 3) + [jnp.zeros((5, chunk), F32)], axis=0
            )
            outs[k][STATE_SIZE:, at : at + chunk] = jnp.concatenate(
                [mine[:24], total], axis=0
            ).astype(BF16)


def top_kernel(stage, count, *refs):
    parts, outs, prompt_ref = refs[:count], refs[count:-1], refs[-1]
    place = place_of(stage)
    width = prompt_ref.shape[1]
    logs = [logs_of(part[LOG_AT:UP_ROWS, :]) for part in parts]
    states = [part[:STATE_SIZE, :].astype(F32) for part in parts]
    final = sum(w * s for w, s in zip(weights_of(logs, place, count), states)).astype(BF16)
    prompt_ref[...] = final
    mine = sum(part[STATE_SIZE:LOG_AT, :].astype(F32) for part in parts)
    reads = mine[16:24, :STATE_SIZE].astype(BF16)
    gated = mine[0:8] + mine[8:16] * dot(reads, final)
    gated = jnp.concatenate(split(gated, 2), axis=0).astype(BF16)
    for k in list(range(1, len(outs))) + [0]:
        scale = weights_of(logs, place, place ^ k)
        outs[k][:STATE_SIZE, :] = sum(w * s for w, s in zip(scale, states)).astype(BF16)
        outs[k][STATE_SIZE:, :] = gated


def down_kernel(stage, above, above_count, count, handed, *refs):
    pieces, parts = refs[:above_count], refs[above_count : above_count + count]
    outs = refs[above_count + count :]
    if handed:
        outs[-1][...] = outs[0][...]
        outs = outs[1:-1]
    place, source = place_of(stage), place_of(above)
    width = pieces[0].shape[1]
    chunk = min(256, width)
    for k in list(range(1, len(outs))) + [0]:
        for piece in range(above_count):
            for at in range(0, width, chunk):
                start = at if above_count == 1 else (source ^ piece) * width + at
                at_out = window(start, chunk)
                block = pieces[piece][:, at : at + chunk]
                logs = [logs_of(part[LOG_AT:UP_ROWS, at_out]) for part in parts]
                state = carry_of(logs, place, place ^ k) * block[:STATE_SIZE].astype(F32)
                for w, part in zip(weights_of(logs, place, place ^ k), parts):
                    state = state + w * part[:STATE_SIZE, at_out].astype(F32)
                outs[k][:STATE_SIZE, at_out] = state.astype(BF16)
                outs[k][STATE_SIZE:, at_out] = block[STATE_SIZE:]


def intra_kernel(run_ref, runt_ref, stept_ref, skip_ref, x_ref, write_ref, read_ref, *refs):
    out_ref = refs[-1]
    span = x_ref.shape[0]
    heads = runt_ref.shape[0]
    mid = span // 2
    scores = dot(read_ref[...], write_ref[...], ((1,), (1,)))
    row = lax.broadcasted_iota(jnp.int32, (mid, mid), 0)
    causal = row >= lax.broadcasted_iota(jnp.int32, (mid, mid), 1)
    running = run_ref[0]
    low, high = slice(0, mid), slice(mid, span)
    for pair in range(heads // 2):
        found = []
        for h in (2 * pair, 2 * pair + 1):
            x = x_ref[:, h * HEAD_DIM : (h + 1) * HEAD_DIM]
            t_run, j_run = running[:, h : h + 1], runt_ref[h : h + 1, :]
            step = stept_ref[h : h + 1, :]

            def mixed(rows, cols, masked):
                gap = t_run[rows] - j_run[:, cols]
                if masked:
                    gap = jnp.where(causal, gap, -jnp.inf)
                return (scores[rows, cols] * jnp.exp(gap) * step[:, cols]).astype(BF16)

            top = dot(mixed(low, low, True), x[low])
            bottom = dot(mixed(high, low, False), x[low]) + dot(mixed(high, high, True), x[high])
            found.append(jnp.concatenate([top, bottom], axis=0))
        at = slice(pair * 2 * HEAD_DIM, (pair + 1) * 2 * HEAD_DIM)
        both = jnp.concatenate(found, axis=1)
        out_ref[:, at] = both + skip_ref[:, at] * x_ref[:, at].astype(F32)


def intra(run, runt, stept, skip, x, write, read, first, number, base, after):
    span, lanes = x.shape
    groups, _, per_group = run.shape
    wide = per_group * HEAD_DIM
    args = [run, runt, stept, skip, x, write, read]
    specs = [
        pl.BlockSpec((1, span, per_group), lambda g: (g + first, 0, 0)),
        pl.BlockSpec((per_group, span), lambda g: (g + first, 0)),
        pl.BlockSpec((per_group, span), lambda g: (g + first, 0)),
        pl.BlockSpec((1, wide), lambda g: (0, g + first)),
        pl.BlockSpec((span, wide), lambda g: (0, g + first)),
        pl.BlockSpec((span, STATE_SIZE), lambda g: (0, g + first)),
        pl.BlockSpec((span, STATE_SIZE), lambda g: (0, g + first)),
    ]
    alias = {}
    if base is not None:
        alias = {len(args): 0}
        args.append(base)
        specs.append(ANYWHERE)
    (base,) = call(
        intra_kernel,
        "intra",
        [shape((span, lanes), F32)],
        args,
        specs=specs,
        out_specs=[pl.BlockSpec((span, wide), lambda g: (0, g + first))],
        grid=(number,),
        after=after,
        alias=alias,
        flops=number * per_group * span * span * HEAD_DIM * 2,
        moved=number * wide * span * 6,
        exps=number * per_group * span * span * 3 // 4,
    )
    return base


def finish_kernel(stage, chunks, reach_ref, read_ref, own_ref, got_ref, base_ref, out_ref):
    place = place_of(stage)
    step = pl.program_id(0)
    heads = reach_ref.shape[1] // 2
    chunk = out_ref.shape[1]
    mine = place == lax.div(step, chunks // 2)
    entering = jnp.where(mine, own_ref[:STATE_SIZE, :], got_ref[:STATE_SIZE, :])
    inter = dot(read_ref[...], entering)
    inter = inter * dot(reach_ref[...], head_mask(2 * heads, heads, chunk, step * chunk))
    out_ref[...] = (inter + base_ref[...]).astype(BF16)


def finish(stage, reach, read, own, got, base, after=()):
    span, lanes = base.shape
    wide = lanes // (read.shape[1] // STATE_SIZE)
    half = lanes // 2
    chunk = min(512, half)
    chunks, halves = lanes // chunk, half // chunk
    entering = pl.BlockSpec((DOWN_ROWS, chunk), lambda c: (0, lax.rem(c, halves)))
    return call(
        functools.partial(finish_kernel, stage, chunks),
        "finish",
        [shape((span, lanes), BF16)],
        (reach, read, own, got, base),
        specs=[
            pl.BlockSpec(reach.shape, lambda c: (0, 0)),
            pl.BlockSpec((span, STATE_SIZE), lambda c: (0, lax.div(c * chunk, wide))),
            entering,
            entering,
            pl.BlockSpec((span, chunk), lambda c: (0, c)),
        ],
        out_specs=[pl.BlockSpec((span, chunk), lambda c: (0, c))],
        grid=(chunks,),
        after=after,
        flops=2 * span * lanes * STATE_SIZE,
    )[0]


def resident_kernel(state_ref, vread_ref, q1_ref, q2_ref, gain_ref, out_ref):
    drawn = dot(vread_ref[...], state_ref[...], ((1,), (1,)))
    gated = q1_ref[...] + q2_ref[...] * drawn
    out_ref[...] = normed(gated, gain_ref[...]).astype(BF16)


def normed(gated, gain):
    mean_square = jnp.mean(gated * gated, axis=1, keepdims=True)
    return gated * lax.rsqrt(mean_square + EPSILON) * gain


def resident_hidden(state, vread, q1, q2, gain, after):
    lanes = state.shape[0]
    groups = vread.shape[1] // STATE_SIZE
    wide = lanes // groups
    rows = pl.BlockSpec((DRAFTS, wide), lambda g: (0, g))
    return call(
        resident_kernel,
        "resident_hidden",
        [shape((DRAFTS, lanes), BF16)],
        (state, vread, q1, q2, gain),
        specs=[
            pl.BlockSpec((wide, STATE_SIZE), lambda g: (g, 0)),
            pl.BlockSpec((DRAFTS, STATE_SIZE), lambda g: (0, g)),
            rows,
            rows,
            pl.BlockSpec((1, wide), lambda g: (0, g)),
        ],
        out_specs=[rows],
        grid=(groups,),
        after=after,
        flops=2 * DRAFTS * lanes * STATE_SIZE,
    )[0]


def join_kernel(axis, *refs):
    out_ref = refs[-1]
    for k, ref in enumerate(refs[:-1]):
        size = ref.shape[axis]
        at = slice(k * size, (k + 1) * size)
        if axis == 0:
            out_ref[at, :] = ref[...]
        else:
            out_ref[:, at] = ref[...]


def join(parts, axis, after=()):
    dims = list(parts[0].shape)
    dims[axis] *= len(parts)
    return call(
        functools.partial(join_kernel, axis), "join", [shape(tuple(dims), parts[0].dtype)], parts, after=after
    )[0]


def project_kernel(stages, head_count, *refs):
    owner_ref, own_rows, got_rows, own_ref, got_ref, gain_ref, weight_ref = refs[:7]
    outs = refs[7 : 7 + head_count]
    gated_ref, left_ref, total_ref = refs[7 + head_count :]
    here, head = lax.axis_index("seq"), lax.axis_index("head")
    place = place_of(stages[0])
    half = own_ref.shape[1]
    lanes = weight_ref.shape[0]
    wide = min(1024, lanes)
    rows = own_rows.shape[0]
    for k, ref in enumerate((own_ref, got_ref)):
        both = ref[STATE_SIZE:, :].astype(F32)
        gated_ref[:, window((place ^ k) * half, half)] = both[0:8] + both[8:16]
    left_ref[0:rows, :] = own_rows[...]
    left_ref[rows : 2 * rows, :] = got_rows[...]
    for lane0 in range(0, lanes, wide):
        at = slice(lane0, lane0 + wide)
        hidden = normed(gated_ref[:, at], gain_ref[:, at])
        hidden = jnp.concatenate([hidden, jnp.zeros_like(hidden)], axis=0)
        left_ref[2 * rows :, at] = hidden.astype(BF16)
    total_ref[...] = dot(left_ref[...], weight_ref[...])

    slots = 2 * rows // DRAFTS
    per_head = slots // head_count
    offsets = [0]
    for factor, stride in reversed(stages):
        offsets = [a + k * stride for k in range(factor) for a in offsets]
    owner = owner_ref[...]
    tail = total_ref[2 * rows : 2 * rows + DRAFTS, :]
    for k in list(range(1, head_count)) + [0]:
        first = (head ^ k) * per_head
        for slot in range(per_head):
            at = slice(slot * DRAFTS, (slot + 1) * DRAFTS)
            offset = here ^ (first + slot)
            block = jnp.int32(0)
            for position, value in enumerate(offsets):
                block = jnp.where(offset == value, position, block)
            from_block = total_ref[window(block * DRAFTS, DRAFTS), :]
            outs[k][at, :] = jnp.where(owner == first + slot, tail, from_block)


def project(stages, owner, own_rows, got_rows, own, got, gain, weight, head_count):
    lanes, cols = weight.shape
    rows = own_rows.shape[0]
    return call(
        functools.partial(project_kernel, stages, head_count),
        "project",
        [shape((2 * rows // head_count, cols), F32)] * head_count,
        (owner, own_rows, got_rows, own, got, gain, weight),

        scratch=[
            pltpu.VMEM((DRAFTS, lanes), F32),
            pltpu.VMEM((2 * rows + 16, lanes), BF16),
            pltpu.VMEM((2 * rows + 16, cols), F32),
        ],
        flops=2 * (2 * rows + 16) * lanes * cols,
    )


def states_kernel(stages, scattered, shares, *refs):
    owner_ref, resident_ref, own_ref, got_ref, tail_ref, vwrite_ref = refs[:6]
    share_refs = refs[6 : 6 + shares]
    new_ref, slice_ref, verify_ref, turned_ref = refs[6 + shares :]
    here, step = lax.axis_index("seq"), pl.program_id(0)

    @pl.when(step == 0)
    def _():
        verify_ref[...] = sum(ref[...] for ref in share_refs).astype(BF16)

    chunk = resident_ref.shape[0]
    half = own_ref.shape[1]
    blocks = [0]
    for factor, stride in reversed(scattered):
        blocks = [a | (k * stride) for k in range(factor) for a in blocks]
    width = half // len(blocks)
    for at in range(0, chunk, width):
        lane = step * chunk + at
        spot, size = lax.div(lane, half), half
        rest = lax.rem(lane, half)
        for factor, stride in scattered:
            size = size // factor
            spot = spot | (lax.div(rest, size) * stride)
            rest = lax.rem(rest, size)
        offset = spot ^ here
        position = jnp.int32(0)
        for place, value in enumerate(blocks):
            position = jnp.where((offset & sum_of(scattered)) == value, place, position)
        found = jnp.where(
            lax.rem(offset, 2) == 0,
            own_ref[:, window(position * width, width)],
            got_ref[:, window(position * width, width)],
        )
        turned_ref[at : at + width, :] = found.astype(F32).T
    per_slice = slice_ref.shape[1] // STATE_SIZE
    heads = slice_ref.shape[0]
    for k in range(per_slice):
        picked = turned_ref[pl.ds(here * per_slice + k, heads, stride=HEAD_DIM), :]
        slice_ref[:, k * STATE_SIZE : (k + 1) * STATE_SIZE] = picked.astype(BF16)
    is_owner = owner_ref[0:1, :STATE_SIZE] == here
    row = lax.broadcasted_iota(jnp.int32, (32, STATE_SIZE), 0)
    ones = jnp.where((row >= 24) & (row < 27), 1.0, 0.0)
    writes = vwrite_ref[...].astype(F32)
    writes = jnp.concatenate([writes, writes, writes, jnp.zeros_like(writes)], axis=0)
    right = jnp.concatenate([writes, ones], axis=1).astype(BF16)
    left = tail_ref[...].astype(F32).T.astype(BF16)
    both = dot(left, right)
    start = jnp.where(is_owner, turned_ref[...], resident_ref[...].astype(F32))
    new_ref[...] = (start * both[:, STATE_SIZE:] + both[:, :STATE_SIZE]).astype(BF16)


def sum_of(stages):
    return sum((factor - 1) * stride for factor, stride in stages)


def states(stages, scattered, owner, resident, own, got, tail, vwrite, shares, seq_count):
    lanes = resident.shape[0]
    wide = lanes // (vwrite.shape[1] // STATE_SIZE)
    chunk = min(512, wide)
    heads = lanes // HEAD_DIM
    rows, cols = shares[0].shape
    fixed = pl.BlockSpec((rows, cols), lambda c: (0, 0))
    return call(
        functools.partial(states_kernel, stages, scattered, len(shares)),
        "states",
        [
            shape((lanes, STATE_SIZE), BF16),
            shape((heads, HEAD_DIM // seq_count * STATE_SIZE), BF16),
            shape((rows, cols), BF16),
        ],
        (owner, resident, own, got, tail, vwrite, *shares),
        specs=[
            WHOLE,
            pl.BlockSpec((chunk, STATE_SIZE), lambda c: (c, 0)),
            WHOLE,
            WHOLE,
            pl.BlockSpec((32, chunk), lambda c: (0, c)),
            pl.BlockSpec((DRAFTS, STATE_SIZE), lambda c: (0, lax.div(c * chunk, wide))),
        ]
        + [WHOLE] * len(shares),
        out_specs=[
            pl.BlockSpec((chunk, STATE_SIZE), lambda c: (c, 0)),
            pl.BlockSpec((chunk // HEAD_DIM, HEAD_DIM // seq_count * STATE_SIZE), lambda c: (c, 0)),
            fixed,
        ],
        grid=(lanes // chunk,),
        scratch=[pltpu.VMEM((chunk, STATE_SIZE), F32)],
        flops=2 * lanes * STATE_SIZE * 64,
    )


def on_device(
    prefill_input,
    prefill_step,
    write_proj,
    read_proj,
    decay_rate,
    skip_gain,
    resident_state,
    owner_slot,
    draft_ids,
    accepted_len,
    draft_input,
    draft_gate,
    draft_write,
    draft_read,
    draft_step,
    norm_gain,
    out_weight,
):
    span, lanes = prefill_input.shape
    assert span == BLOCK_LEN
    heads = decay_rate.shape[0]
    groups = write_proj.shape[1] // STATE_SIZE
    per_group = heads // groups
    half = lanes // 2
    seq_count, head_count = lax.axis_size("seq"), lax.axis_size("head")
    stages = tree_stages(seq_count)
    core, line, last = stages
    slots = owner_slot.shape[0]
    assert core[0] == 2 and slots == seq_count
    rate, skip, gain = decay_rate[None], skip_gain[None], norm_gain[None]
    resident = resident_state.reshape(lanes, STATE_SIZE)

    inputs = (
        prefill_step.T, rate, skip, owner_slot, draft_ids.T, accepted_len, draft_input, draft_gate,
        draft_write, draft_read, draft_step, write_proj, prefill_input,
    )
    inputs = [in_hbm(value) for value in inputs]
    opened = call(
        functools.partial(open_kernel, core, len(inputs)),
        "open_block",
        [
            shape((UP_ROWS, half), BF16),
            shape((UP_ROWS, half), BF16),
            shape((groups, span, per_group), F32),
            shape((heads, span), F32),
            shape((heads, span), F32),
            shape((span, 2 * heads), BF16),
            shape((1, lanes), F32),
            shape((DRAFTS, lanes), F32),
            shape((DRAFTS, lanes), F32),
            shape((DRAFTS, groups * STATE_SIZE), BF16),
            shape((DRAFTS, groups * STATE_SIZE), BF16),
            shape((32, lanes), BF16),
            shape((DRAFTS, out_weight.shape[1]), jnp.int32),
        ],
        inputs,
        specs=[IN_HBM] * len(inputs),
        scratch=[pltpu.VMEM((EXTRA, lanes), BF16), pltpu.SemaphoreType.DMA((len(inputs),))]
        + [
            (pltpu.SMEM if value.dtype == jnp.int32 else pltpu.VMEM)(value.shape, value.dtype)
            for value in inputs
        ],
        flops=2 * span * lanes * STATE_SIZE * 2,
    )
    prefill_input, write_proj, read_proj, resident, gain = (
        in_hbm(value) for value in (prefill_input, write_proj, read_proj, resident, gain)
    )
    own, sent, run, runt, stept, reach, skip_lanes, q1, q2, vread, vwrite, tail, owner = opened
    core_parts = [own, swap(sent, "seq", core, 1)]

    number = max(1, groups // 4)
    firsts = list(range(0, groups, number))
    base = None

    def fill(after):
        nonlocal base
        if firsts:
            base = intra(
                run, runt, stept, skip_lanes, prefill_input, write_proj, read_proj, firsts.pop(0), number,
                base, after,
            )
        return [base]

    def exchange(parts, stage):
        got = {k: swap(parts[k], "seq", stage, k) for k in range(stage[0] - 1, 0, -1)}
        return [parts[0]] + [got[k] for k in range(1, stage[0])]

    line_width = half // line[0]
    split_last = line_width % (last[0] * 128) == 0
    last_width = line_width // last[0] if split_last else line_width
    outs = call(
        functools.partial(up_kernel, core, line, 2),
        "up_line",
        [shape((UP_ROWS, line_width), BF16)] * line[0],
        core_parts,
        flops=half * UP_ROWS * 4,
    )
    line_parts = exchange(outs, line)
    hidden = resident_hidden(resident, vread, q1, q2, gain, [outs[-1]])
    hidden = join(exchange([hidden] * last[0], last), 0)
    outs = call(
        functools.partial(up_kernel, line, last, line[0]),
        "up_last",
        [shape((UP_ROWS, last_width), BF16)] * (last[0] if split_last else 1),
        line_parts,
        after=[hidden],
        flops=line_width * UP_ROWS * 4,
    )
    last_parts = exchange(outs if split_last else outs * last[0], last)
    hiddens = exchange([hidden] * line[0], line)
    fill([outs[-1]])
    filled = fill([])
    *outs, prompt = call(
        functools.partial(top_kernel, last, last[0]),
        "top",
        [shape((DOWN_ROWS, last_width), BF16)] * (last[0] if split_last else 1)
        + [shape((STATE_SIZE, last_width), BF16)],
        last_parts,
        after=filled,
        flops=last_width * UP_ROWS * 16,
    )

    pieces = exchange(outs, last) if split_last else outs
    filled = fill([outs[-1]])
    hidden = join(hiddens, 0)
    *outs, prompt = call(
        functools.partial(down_kernel, line, last, len(pieces), line[0], True),
        "down_line",
        [shape((DOWN_ROWS, line_width), BF16)] * line[0] + [shape(prompt.shape, BF16)],
        [*pieces, *line_parts, prompt],
        after=[*filled, hidden],
        flops=line_width * UP_ROWS * 8,
    )
    pieces = exchange(outs, line)
    filled = fill([outs[-1]])
    scattered = [line, last] if split_last else [line]
    if split_last:
        prompts = exchange([prompt] * last[0], last)
    outs = call(
        functools.partial(down_kernel, core, line, line[0], 2, False),
        "down_core",
        [shape((DOWN_ROWS, half), BF16)] * 2,
        pieces + core_parts,
        after=filled,
        flops=half * UP_ROWS * 8,
    )
    if split_last:
        prompt = join(prompts, 1, [outs[-1]])
    entering = exchange(outs, core)
    while firsts:
        fill([])
    prefill_out = finish(core, reach, read_proj, *entering, base)

    shares = project(
        stages, owner, hidden, swap(hidden, "seq", core, 1), *entering, norm_gain[None], out_weight, head_count
    )
    shares = [shares[0]] + [swap(shares[k], "head", (head_count, 1), k) for k in range(1, head_count)]

    prompt = join(exchange([prompt] * line[0], line), 1)
    prompts = exchange([prompt] * 2, core)
    new_state, state_slice, verify_out = states(
        stages, scattered, owner, resident, *prompts, tail, vwrite, shares, seq_count
    )
    return (
        prefill_out,
        new_state.reshape(1, heads, HEAD_DIM, STATE_SIZE),
        verify_out,
        state_slice,
    )


def solution(mesh):
    return jax.shard_map(
        on_device,
        mesh=mesh,
        in_specs=(
            P("seq", "head"),
            P("seq", "head"),
            P("seq", "head"),
            P("seq", "head"),
            P("head"),
            P("head"),
            P("seq", "head", None, None),
            P(),
            P(),
            P(),
            P("seq", "head"),
            P("seq", "head"),
            P("seq", "head"),
            P("seq", "head"),
            P("seq", "head"),
            P("head"),
            P("head", "seq"),
        ),
        out_specs=(
            P("seq", "head"),
            P("seq", "head", None, None),
            P("head", "seq"),
            P("head", "seq"),
        ),
        check_vma=False,
    )
```

time: 104 us -> 74.9 us (0.72)
  waiting for transfers between devices: 36.5 us -> 13.8 us
  local copies, waits for them, and re-layouts: 17.7 us -> 0.01 us
  Pallas kernels: 23 us -> 33 us
  starting transfers between devices: 24 us -> 26.6 us
  other arithmetic: 1.59 us -> 0 us
    ppermute x21, waiting for transfers between devices: 36.5 us -> 13.8 us  [swap(): lax.ppermute(value, axis, [(k, k ^ offset * stride) for k in range(count)])]
    unnamed x78 -> x4, local copies, waits for them, and re-layouts: 16.3 us -> 0.01 us
    pallas_call x12 -> x18, Pallas kernels: 23 us -> 33 us  [call(): pl.pallas_call(ordered(kernel, first), name=name, grid=grid, out_shape=ou...]
    ppermute x21, starting transfers between devices: 24 us -> 26.6 us  [swap(): lax.ppermute(value, axis, [(k, k ^ offset * stride) for k in range(count)])]
    convert_element_type x1 -> x0, other arithmetic: 1.55 us -> none  [on_device(): verify_out.astype(BF16)]
  transfers between devices with their start and end apart: 21 -> 21, of which waited for: 9 -> 7; matrix products, arithmetic and copies ran while one was open for 4% -> 0% of each run, Pallas kernels for 18% -> 29%
where the time goes in v3:
time: 74.9 us; the launch traced here: 74.2 us
  Pallas kernels  33 us (44%)
  starting transfers between devices  26.6 us (36%)
  waiting for transfers between devices  13.8 us (18%)
  between operations  0.86 us (1%)
    pallas_call x18, Pallas kernels, call(): pl.pallas_call(ordered(kernel, first), name=name, grid=grid, out_shape=ou...  33 us
    ppermute x21, starting transfers between devices, swap(): lax.ppermute(value, axis, [(k, k ^ offset * stride) for k in range(count)])  26.6 us
    ppermute x21, waiting for transfers between devices, swap(): lax.ppermute(value, axis, [(k, k ^ offset * stride) for k in range(count)])  13.8 us
  transfers between devices with their start and end apart: 21, of which 7 were waited for; matrix products, arithmetic and copies ran while one was open for 0% of the time, Pallas kernels for 29%

profile of v3, /device:TPU:0, one launch (start us, length us, event | category | flops | bytes accessed | tf_op | source)
XLA Modules:
  0.0 74.2 jit_solution(15344053700208203866)
XLA Ops:
  0.6 4.3 %open_block.1 = (bf16[160,2048]{1,0:T(8,128)(2,1)S(1)}, bf16[160,2048]{1,0:T(8,128)(2,1)S(1)}, f32[4,256,16]{2,1,0:T(8,128)S(1)}, f32[64,256]{1,0:T(8,128)S(1)},...) custom-call(f32[64,256]{1,0:T(8,128)} %bitcast.11, ...), custom_call_target="tpu_custom_call" | custom-call | flops 536870912 | bytes 4871296 | tf_op jit(solution)/shard_map/open_block/pallas_call | solution.py:95
  5.4 1.7 %collective-permute-done.refs_1_.refs_4_ = bf16[160,2048]{1,0:T(8,128)(2,1)S(1)} collective-permute-done((bf16[160,2048]{1,0:T(8,128)(2,1)S(1)}, bf16[160,2048]{1,0:T(8,128)(2,1)S(1)}, u32[]{:S(2)}, u32[]{:S(2)}) %collective-permute-start) | collective-permute-done | bytes 655392 | tf_op jit(solution)/shard_map/ppermute | solution.py:44
  7.5 3.0 %collective-permute-start.4 = (bf16[160,1024]{1,0:T(8,128)(2,1)S(1)}, bf16[160,1024]{1,0:T(8,128)(2,1)S(1)}, u32[]{:S(2)}, u32[]{:S(2)}) collective-permute-start(bf16[160,1024]{1,0:T(8,128)(2,1)S(1)} %get-tuple-element.45.refs_0_), channel_id=1, source_target_pairs={{0,4},{2,6},{4,0},{6,2},{8,12},{10,14},{12,8},{14,10},{16,20},{18,... | collective-permute-start | bytes 983048 | tf_op jit(solution)/shard_map/ppermute | solution.py:44
  10.4 2.7 %resident_hidden.1.refs_0_ = bf16[8,4096]{1,0:T(8,128)(2,1)S(1)} custom-call(bf16[160,1024]{1,0:T(8,128)(2,1)S(1)} %get-tuple-element.45.refs_0_, bf16[4096,128]{1,0:T(8,128)(2,1)} %bitcast.9, bf16[8,512]{1,0:T(8,128)(2,1)S(1)} %get-tuple-element.46.refs_2_, f32[8,4096]{1,0:T(8,128)S(1)} %get-tuple-element.47.refs_3_, ...), custom_call_target="tpu_custom_call" | custom-call | flops 8388608 | bytes 1400832 | tf_op jit(solution)/shard_map/resident_hidden/pallas_call | solution.py:95
  13.2 1.6 %collective-permute-start.1 = (bf16[8,4096]{1,0:T(8,128)(2,1)S(1)}, bf16[8,4096]{1,0:T(8,128)(2,1)S(1)}, u32[]{:S(2)}, u32[]{:S(2)}) collective-permute-start(bf16[8,4096]{1,0:T(8,128)(2,1)S(1)} %resident_hidden.1.refs_0_), channel_id=1, source_target_pairs={{0,8},{2,10},{4,12},{6,14},{8,0},{10,2},{12,4},{14,6},{16,24},{18,... | collective-permute-start | bytes 196616 | tf_op jit(solution)/shard_map/ppermute | solution.py:44
  14.8 2.6 %collective-permute-start.2 = (bf16[8,4096]{1,0:T(8,128)(2,1)S(1)}, bf16[8,4096]{1,0:T(8,128)(2,1)S(1)}, u32[]{:S(2)}, u32[]{:S(2)}) collective-permute-start(bf16[8,4096]{1,0:T(8,128)(2,1)S(1)} %resident_hidden.1.refs_0_), channel_id=1, source_target_pairs={{0,16},{2,18},{4,20},{6,22},{8,24},{10,26},{12,28},{14,30},{16,0},... | collective-permute-start | bytes 196616 | tf_op jit(solution)/shard_map/ppermute | solution.py:44
  17.6 4.5 %collective-permute-done.2.refs_2_ = bf16[8,4096]{1,0:T(8,128)(2,1)S(1)} collective-permute-done((bf16[8,4096]{1,0:T(8,128)(2,1)S(1)}, bf16[8,4096]{1,0:T(8,128)(2,1)S(1)}, u32[]{:S(2)}, u32[]{:S(2)}) %collective-permute-start.2) | collective-permute-done | bytes 65568 | tf_op jit(solution)/shard_map/ppermute | solution.py:44
  22.1 1.4 %collective-permute-done.3.refs_3_ = bf16[8,4096]{1,0:T(8,128)(2,1)S(1)} collective-permute-done((bf16[8,4096]{1,0:T(8,128)(2,1)S(1)}, bf16[8,4096]{1,0:T(8,128)(2,1)S(1)}, u32[]{:S(2)}, u32[]{:S(2)}) %collective-permute-start.3) | collective-permute-done | bytes 65568 | tf_op jit(solution)/shard_map/ppermute | solution.py:44
  24.3 2.3 %collective-permute-start.6 = (bf16[160,256]{1,0:T(8,128)(2,1)S(1)}, bf16[160,256]{1,0:T(8,128)(2,1)S(1)}, u32[]{:S(2)}, u32[]{:S(2)}) collective-permute-start(bf16[160,256]{1,0:T(8,128)(2,1)S(1)} %get-tuple-element.53), channel_id=1, source_target_pairs={{0,16},{2,18},{4,20},{6,22},{8,24},{10,26},{12,28},{14,30},{16,0},... | collective-permute-start | bytes 245768 | tf_op jit(solution)/shard_map/ppermute | solution.py:44
  26.6 2.0 %collective-permute-start.7 = (bf16[160,256]{1,0:T(8,128)(2,1)S(1)}, bf16[160,256]{1,0:T(8,128)(2,1)S(1)}, u32[]{:S(2)}, u32[]{:S(2)}) collective-permute-start(bf16[160,256]{1,0:T(8,128)(2,1)S(1)} %get-tuple-element.50.refs_0_), channel_id=1, source_target_pairs={{0,24},{2,26},{4,28},{6,30},{8,16},{10,18},{12,20},{14,22},{16,8},... | collective-permute-start | bytes 245768 | tf_op jit(solution)/shard_map/ppermute | solution.py:44
  28.7 2.7 %intra.4.refs_7_ = f32[256,4096]{1,0:T(8,128)S(1)} custom-call(bf16[160,256]{1,0:T(8,128)(2,1)S(1)} %get-tuple-element.50.refs_0_, f32[4,256,16]{2,1,0:T(8,128)S(1)} %get-tuple-element.39.refs_1_.refs_0_, f32[64,256]{1,0:T(8,128)S(1)} %get-tuple-element.40.refs_2_.refs_1_, f32[64,256]{1,0:T(8,128)S(1)} %get-tuple-element.41.refs_3_.refs_2_, ...), custom_call_target="tpu_custom_call" | custom-call | flops 134217728 | bytes 1572864 | tf_op jit(solution)/shard_map/intra/pallas_call | solution.py:95
  31.4 2.7 %intra.5.refs_0_.refs_8_ = f32[256,4096]{1,0:T(8,128)S(1)} custom-call(f32[4,256,16]{2,1,0:T(8,128)S(1)} %get-tuple-element.39.refs_1_.refs_0_, f32[64,256]{1,0:T(8,128)S(1)} %get-tuple-element.40.refs_2_.refs_1_, f32[64,256]{1,0:T(8,128)S(1)} %get-tuple-element.41.refs_3_.refs_2_, ...), custom_call_target="tpu_custom_call", output_to_operand_aliasing={{}: (7, {})} | custom-call | flops 134217728 | bytes 1572864 | tf_op jit(solution)/shard_map/intra/pallas_call | solution.py:95
  35.2 1.4 %collective-permute-start.11 = (bf16[144,256]{1,0:T(8,128)(2,1)S(1)}, bf16[144,256]{1,0:T(8,128)(2,1)S(1)}, u32[]{:S(2)}, u32[]{:S(2)}) collective-permute-start(bf16[144,256]{1,0:T(8,128)(2,1)S(1)} %get-tuple-element.54.refs_0_), channel_id=1, source_target_pairs={{0,24},{2,26},{4,28},{6,30},{8,16},{10,18},{12,20},{14,22},{16,8},... | collective-permute-start | bytes 221192 | tf_op jit(solution)/shard_map/ppermute | solution.py:44
  36.6 1.4 %collective-permute-start.9 = (bf16[144,256]{1,0:T(8,128)(2,1)S(1)}, bf16[144,256]{1,0:T(8,128)(2,1)S(1)}, u32[]{:S(2)}, u32[]{:S(2)}) collective-permute-start(bf16[144,256]{1,0:T(8,128)(2,1)S(1)} %get-tuple-element.56), channel_id=1, source_target_pairs={{0,8},{2,10},{4,12},{6,14},{8,0},{10,2},{12,4},{14,6},{16,24},{18,... | collective-permute-start | bytes 221192 | tf_op jit(solution)/shard_map/ppermute | solution.py:44
  38.1 2.7 %intra.6.refs_0_.refs_8_ = f32[256,4096]{1,0:T(8,128)S(1)} custom-call(bf16[144,256]{1,0:T(8,128)(2,1)S(1)} %get-tuple-element.54.refs_0_, f32[4,256,16]{2,1,0:T(8,128)S(1)} %get-tuple-element.39.refs_1_.refs_0_, f32[64,256]{1,0:T(8,128)S(1)} %get-tuple-element.40.refs_2_.refs_1_, ...), custom_call_target="tpu_custom_call", output_to_operand_aliasing={{}: (8, {})} | custom-call | flops 134217728 | bytes 1572864 | tf_op jit(solution)/shard_map/intra/pallas_call | solution.py:95
  42.1 2.6 %collective-permute-start.12 = (bf16[144,1024]{1,0:T(8,128)(2,1)S(1)}, bf16[144,1024]{1,0:T(8,128)(2,1)S(1)}, u32[]{:S(2)}, u32[]{:S(2)}) collective-permute-start(bf16[144,1024]{1,0:T(8,128)(2,1)S(1)} %get-tuple-element.59.refs_0_), channel_id=1, source_target_pairs={{0,4},{2,6},{4,0},{6,2},{8,12},{10,14},{12,8},{14,10},{16,20},{18,... | collective-permute-start | bytes 884744 | tf_op jit(solution)/shard_map/ppermute | solution.py:44
  44.7 2.1 %collective-permute-start.15 = (bf16[128,256]{1,0:T(8,128)(2,1)S(1)}, bf16[128,256]{1,0:T(8,128)(2,1)S(1)}, u32[]{:S(2)}, u32[]{:S(2)}) collective-permute-start(bf16[128,256]{1,0:T(8,128)(2,1)S(1)} %get-tuple-element.64.refs_1_), channel_id=1, source_target_pairs={{0,16},{2,18},{4,20},{6,22},{8,24},{10,26},{12,28},{14,30},{16,0},... | collective-permute-start | bytes 196616 | tf_op jit(solution)/shard_map/ppermute | solution.py:44
  46.9 2.2 %collective-permute-start.16 = (bf16[128,256]{1,0:T(8,128)(2,1)S(1)}, bf16[128,256]{1,0:T(8,128)(2,1)S(1)}, u32[]{:S(2)}, u32[]{:S(2)}) collective-permute-start(bf16[128,256]{1,0:T(8,128)(2,1)S(1)} %get-tuple-element.64.refs_1_), channel_id=1, source_target_pairs={{0,24},{2,26},{4,28},{6,30},{8,16},{10,18},{12,20},{14,22},{16,8},... | collective-permute-start | bytes 196616 | tf_op jit(solution)/shard_map/ppermute | solution.py:44
  49.1 2.7 %intra.7.refs_0_.refs_4_ = f32[256,4096]{1,0:T(8,128)S(1)} custom-call(bf16[144,1024]{1,0:T(8,128)(2,1)S(1)} %get-tuple-element.59.refs_0_, f32[4,256,16]{2,1,0:T(8,128)S(1)} %get-tuple-element.39.refs_1_.refs_0_, f32[64,256]{1,0:T(8,128)S(1)} %get-tuple-element.40.refs_2_.refs_1_, ...), custom_call_target="tpu_custom_call", output_to_operand_aliasing={{}: (8, {})} | custom-call | flops 134217728 | bytes 1572864 | tf_op jit(solution)/shard_map/intra/pallas_call | solution.py:95
  52.9 1.0 %collective-permute-start.17 = (bf16[128,1024]{1,0:T(8,128)(2,1)S(1)}, bf16[128,1024]{1,0:T(8,128)(2,1)S(1)}, u32[]{:S(2)}, u32[]{:S(2)}) collective-permute-start(bf16[128,1024]{1,0:T(8,128)(2,1)S(1)} %join.6.refs_0_), channel_id=1, source_target_pairs={{0,4},{2,6},{4,0},{6,2},{8,12},{10,14},{12,8},{14,10},{16,20},{18,... | collective-permute-start | bytes 786440 | tf_op jit(solution)/shard_map/ppermute | solution.py:44
  54.4 4.9 %collective-permute-done.17.refs_1_ = bf16[128,1024]{1,0:T(8,128)(2,1)S(1)} collective-permute-done((bf16[128,1024]{1,0:T(8,128)(2,1)S(1)}, bf16[128,1024]{1,0:T(8,128)(2,1)S(1)}, u32[]{:S(2)}, u32[]{:S(2)}) %collective-permute-start.17) | collective-permute-done | bytes 262176 | tf_op jit(solution)/shard_map/ppermute | solution.py:44
  60.5 1.6 %collective-permute-start.20 = (f32[64,512]{1,0:T(8,128)S(1)}, f32[64,512]{1,0:T(8,128)S(1)}, u32[]{:S(2)}, u32[]{:S(2)}) collective-permute-start(f32[64,512]{1,0:T(8,128)S(1)} %get-tuple-element.68), channel_id=1, source_target_pairs={{0,1},{1,0},{2,3},{3,2},{4,5},{5,4},{6,7},{7,6},{8,9},{9,8},{10,11... | collective-permute-start | bytes 393224 | tf_op jit(solution)/shard_map/ppermute | solution.py:44
  62.0 5.9 %finish.1 = bf16[256,4096]{1,0:T(8,128)(2,1)} custom-call(bf16[256,128]{1,0:T(8,128)(2,1)S(1)} %get-tuple-element.38.refs_0_, bf16[256,512]{1,0:T(8,128)(2,1)} %refs_1_.1, bf16[144,2048]{1,0:T(8,128)(2,1)S(1)} %get-tuple-element.61.refs_2_.refs_3_, bf16[144,2048]{1,0:T(8,128)(2,1)S(1)} %collective-permute-done.13.refs_3_.refs_4_, ...), custom_call_target="tpu_custom_call" | custom-call | flops 268435456 | bytes 7798784 | tf_op jit(solution)/shard_map/finish/pallas_call | solution.py:95
  67.9 6.3 %states.1 = (bf16[4096,128]{1,0:T(8,128)(2,1)}, bf16[64,512]{1,0:T(8,128)(2,1)}, bf16[64,512]{1,0:T(8,128)(2,1)}) custom-call(s32[8,512]{1,0:T(8,128)S(1)} %get-tuple-element.63.refs_0_, bf16[4096,128]{1,0:T(8,128)(2,1)} %bitcast.10, bf16[128,2048]{1,0:T(8,128)(2,1)S(1)} %join.7.refs_2_, bf16[128,2048]{1,0:T(8,128)(2,1)S(1)} %collective-permute-done.18.refs_3_, ...), custom_call_target="tpu_custom_call" | custom-call | flops 67108864 | bytes 3825664 | tf_op jit(solution)/shard_map/states/pallas_call | solution.py:95
  (40 shorter events, 6.8 us)
Async XLA Ops:
  4.9 2.2 %collective-permute-start = (bf16[160,2048]{1,0:T(8,128)(2,1)S(1)}, bf16[160,2048]{1,0:T(8,128)(2,1)S(1)}, u32[]{:S(2)}, u32[]{:S(2)}) collective-permute-start(bf16[160,2048]{1,0:T(8,128)(2,1)S(1)} %get-tuple-element.44), channel_id=1, source_target_pairs={{0,2},{2,0},{4,6},{6,4},{8,10},{10,8},{12,14},{14,12},{16,18},{18,... | collective-permute-start | bytes 1966088 | tf_op jit(solution)/shard_map/ppermute | solution.py:44
  7.5 16.6 %collective-permute-start.4 = (bf16[160,1024]{1,0:T(8,128)(2,1)S(1)}, bf16[160,1024]{1,0:T(8,128)(2,1)S(1)}, u32[]{:S(2)}, u32[]{:S(2)}) collective-permute-start(bf16[160,1024]{1,0:T(8,128)(2,1)S(1)} %get-tuple-element.45.refs_0_), channel_id=1, source_target_pairs={{0,4},{2,6},{4,0},{6,2},{8,12},{10,14},{12,8},{14,10},{16,20},{18,... | collective-permute-start | bytes 983048 | tf_op jit(solution)/shard_map/ppermute | solution.py:44
  13.2 4.5 %collective-permute-start.1 = (bf16[8,4096]{1,0:T(8,128)(2,1)S(1)}, bf16[8,4096]{1,0:T(8,128)(2,1)S(1)}, u32[]{:S(2)}, u32[]{:S(2)}) collective-permute-start(bf16[8,4096]{1,0:T(8,128)(2,1)S(1)} %resident_hidden.1.refs_0_), channel_id=1, source_target_pairs={{0,8},{2,10},{4,12},{6,14},{8,0},{10,2},{12,4},{14,6},{16,24},{18,... | collective-permute-start | bytes 196616 | tf_op jit(solution)/shard_map/ppermute | solution.py:44
  14.8 7.3 %collective-permute-start.2 = (bf16[8,4096]{1,0:T(8,128)(2,1)S(1)}, bf16[8,4096]{1,0:T(8,128)(2,1)S(1)}, u32[]{:S(2)}, u32[]{:S(2)}) collective-permute-start(bf16[8,4096]{1,0:T(8,128)(2,1)S(1)} %resident_hidden.1.refs_0_), channel_id=1, source_target_pairs={{0,16},{2,18},{4,20},{6,22},{8,24},{10,26},{12,28},{14,30},{16,0},... | collective-permute-start | bytes 196616 | tf_op jit(solution)/shard_map/ppermute | solution.py:44
  17.4 6.1 %collective-permute-start.3 = (bf16[8,4096]{1,0:T(8,128)(2,1)S(1)}, bf16[8,4096]{1,0:T(8,128)(2,1)S(1)}, u32[]{:S(2)}, u32[]{:S(2)}) collective-permute-start(bf16[8,4096]{1,0:T(8,128)(2,1)S(1)} %resident_hidden.1.refs_0_), channel_id=1, source_target_pairs={{0,24},{2,26},{4,28},{6,30},{8,16},{10,18},{12,20},{14,22},{16,8},... | collective-permute-start | bytes 196616 | tf_op jit(solution)/shard_map/ppermute | solution.py:44
  23.5 14.6 %collective-permute-start.8 = (bf16[32,4096]{1,0:T(8,128)(2,1)S(1)}, bf16[32,4096]{1,0:T(8,128)(2,1)S(1)}, u32[]{:S(2)}, u32[]{:S(2)}) collective-permute-start(bf16[32,4096]{1,0:T(8,128)(2,1)S(1)} %join.4.refs_0_), channel_id=1, source_target_pairs={{0,4},{2,6},{4,0},{6,2},{8,12},{10,14},{12,8},{14,10},{16,20},{18,... | collective-permute-start | bytes 786440 | tf_op jit(solution)/shard_map/ppermute | solution.py:44
  24.2 9.9 %collective-permute-start.5 = (bf16[160,256]{1,0:T(8,128)(2,1)S(1)}, bf16[160,256]{1,0:T(8,128)(2,1)S(1)}, u32[]{:S(2)}, u32[]{:S(2)}) collective-permute-start(bf16[160,256]{1,0:T(8,128)(2,1)S(1)} %get-tuple-element.52), channel_id=1, source_target_pairs={{0,8},{2,10},{4,12},{6,14},{8,0},{10,2},{12,4},{14,6},{16,24},{18,... | collective-permute-start | bytes 245768 | tf_op jit(solution)/shard_map/ppermute | solution.py:44
  24.3 9.9 %collective-permute-start.6 = (bf16[160,256]{1,0:T(8,128)(2,1)S(1)}, bf16[160,256]{1,0:T(8,128)(2,1)S(1)}, u32[]{:S(2)}, u32[]{:S(2)}) collective-permute-start(bf16[160,256]{1,0:T(8,128)(2,1)S(1)} %get-tuple-element.53), channel_id=1, source_target_pairs={{0,16},{2,18},{4,20},{6,22},{8,24},{10,26},{12,28},{14,30},{16,0},... | collective-permute-start | bytes 245768 | tf_op jit(solution)/shard_map/ppermute | solution.py:44
  26.6 7.5 %collective-permute-start.7 = (bf16[160,256]{1,0:T(8,128)(2,1)S(1)}, bf16[160,256]{1,0:T(8,128)(2,1)S(1)}, u32[]{:S(2)}, u32[]{:S(2)}) collective-permute-start(bf16[160,256]{1,0:T(8,128)(2,1)S(1)} %get-tuple-element.50.refs_0_), channel_id=1, source_target_pairs={{0,24},{2,26},{4,28},{6,30},{8,16},{10,18},{12,20},{14,22},{16,8},... | collective-permute-start | bytes 245768 | tf_op jit(solution)/shard_map/ppermute | solution.py:44
  34.5 6.3 %collective-permute-start.10 = (bf16[144,256]{1,0:T(8,128)(2,1)S(1)}, bf16[144,256]{1,0:T(8,128)(2,1)S(1)}, u32[]{:S(2)}, u32[]{:S(2)}) collective-permute-start(bf16[144,256]{1,0:T(8,128)(2,1)S(1)} %get-tuple-element.57), channel_id=1, source_target_pairs={{0,16},{2,18},{4,20},{6,22},{8,24},{10,26},{12,28},{14,30},{16,0},... | collective-permute-start | bytes 221192 | tf_op jit(solution)/shard_map/ppermute | solution.py:44
  35.2 6.3 %collective-permute-start.11 = (bf16[144,256]{1,0:T(8,128)(2,1)S(1)}, bf16[144,256]{1,0:T(8,128)(2,1)S(1)}, u32[]{:S(2)}, u32[]{:S(2)}) collective-permute-start(bf16[144,256]{1,0:T(8,128)(2,1)S(1)} %get-tuple-element.54.refs_0_), channel_id=1, source_target_pairs={{0,24},{2,26},{4,28},{6,30},{8,16},{10,18},{12,20},{14,22},{16,8},... | collective-permute-start | bytes 221192 | tf_op jit(solution)/shard_map/ppermute | solution.py:44
  36.6 5.1 %collective-permute-start.9 = (bf16[144,256]{1,0:T(8,128)(2,1)S(1)}, bf16[144,256]{1,0:T(8,128)(2,1)S(1)}, u32[]{:S(2)}, u32[]{:S(2)}) collective-permute-start(bf16[144,256]{1,0:T(8,128)(2,1)S(1)} %get-tuple-element.56), channel_id=1, source_target_pairs={{0,8},{2,10},{4,12},{6,14},{8,0},{10,2},{12,4},{14,6},{16,24},{18,... | collective-permute-start | bytes 221192 | tf_op jit(solution)/shard_map/ppermute | solution.py:44
  42.1 9.7 %collective-permute-start.12 = (bf16[144,1024]{1,0:T(8,128)(2,1)S(1)}, bf16[144,1024]{1,0:T(8,128)(2,1)S(1)}, u32[]{:S(2)}, u32[]{:S(2)}) collective-permute-start(bf16[144,1024]{1,0:T(8,128)(2,1)S(1)} %get-tuple-element.59.refs_0_), channel_id=1, source_target_pairs={{0,4},{2,6},{4,0},{6,2},{8,12},{10,14},{12,8},{14,10},{16,20},{18,... | collective-permute-start | bytes 884744 | tf_op jit(solution)/shard_map/ppermute | solution.py:44
  44.7 7.9 %collective-permute-start.14 = (bf16[128,256]{1,0:T(8,128)(2,1)S(1)}, bf16[128,256]{1,0:T(8,128)(2,1)S(1)}, u32[]{:S(2)}, u32[]{:S(2)}) collective-permute-start(bf16[128,256]{1,0:T(8,128)(2,1)S(1)} %get-tuple-element.64.refs_1_), channel_id=1, source_target_pairs={{0,8},{2,10},{4,12},{6,14},{8,0},{10,2},{12,4},{14,6},{16,24},{18,... | collective-permute-start | bytes 196616 | tf_op jit(solution)/shard_map/ppermute | solution.py:44
  44.7 7.9 %collective-permute-start.15 = (bf16[128,256]{1,0:T(8,128)(2,1)S(1)}, bf16[128,256]{1,0:T(8,128)(2,1)S(1)}, u32[]{:S(2)}, u32[]{:S(2)}) collective-permute-start(bf16[128,256]{1,0:T(8,128)(2,1)S(1)} %get-tuple-element.64.refs_1_), channel_id=1, source_target_pairs={{0,16},{2,18},{4,20},{6,22},{8,24},{10,26},{12,28},{14,30},{16,0},... | collective-permute-start | bytes 196616 | tf_op jit(solution)/shard_map/ppermute | solution.py:44
  46.9 6.1 %collective-permute-start.16 = (bf16[128,256]{1,0:T(8,128)(2,1)S(1)}, bf16[128,256]{1,0:T(8,128)(2,1)S(1)}, u32[]{:S(2)}, u32[]{:S(2)}) collective-permute-start(bf16[128,256]{1,0:T(8,128)(2,1)S(1)} %get-tuple-element.64.refs_1_), channel_id=1, source_target_pairs={{0,24},{2,26},{4,28},{6,30},{8,16},{10,18},{12,20},{14,22},{16,8},... | collective-permute-start | bytes 196616 | tf_op jit(solution)/shard_map/ppermute | solution.py:44
  51.8 7.7 %copy-start = (bf16[4096,512]{1,0:T(8,128)(2,1)S(1)}, bf16[4096,512]{1,0:T(8,128)(2,1)}, u32[]{:S(2)}) copy-start(bf16[4096,512]{1,0:T(8,128)(2,1)} %refs_6_.11) | copy-start | bytes 12582916
  51.8 7.7 %copy-start.1 = (f32[4096]{0:T(1024)S(1)}, f32[4096]{0:T(1024)}, u32[]{:S(2)}) copy-start(f32[4096]{0:T(1024)} %param.32) | copy-start | bytes 49156
  52.9 6.4 %collective-permute-start.17 = (bf16[128,1024]{1,0:T(8,128)(2,1)S(1)}, bf16[128,1024]{1,0:T(8,128)(2,1)S(1)}, u32[]{:S(2)}, u32[]{:S(2)}) collective-permute-start(bf16[128,1024]{1,0:T(8,128)(2,1)S(1)} %join.6.refs_0_), channel_id=1, source_target_pairs={{0,4},{2,6},{4,0},{6,2},{8,12},{10,14},{12,8},{14,10},{16,20},{18,... | collective-permute-start | bytes 786440 | tf_op jit(solution)/shard_map/ppermute | solution.py:44
  53.9 5.6 %collective-permute-start.13 = (bf16[144,2048]{1,0:T(8,128)(2,1)S(1)}, bf16[144,2048]{1,0:T(8,128)(2,1)S(1)}, u32[]{:S(2)}, u32[]{:S(2)}) collective-permute-start(bf16[144,2048]{1,0:T(8,128)(2,1)S(1)} %get-tuple-element.62.refs_0_), channel_id=1, source_target_pairs={{0,2},{2,0},{4,6},{6,4},{8,10},{10,8},{12,14},{14,12},{16,18},{18,... | collective-permute-start | bytes 1769480 | tf_op jit(solution)/shard_map/ppermute | solution.py:44
  53.9 5.6 %collective-permute-start.19 = (bf16[64,4096]{1,0:T(8,128)(2,1)S(1)}, bf16[64,4096]{1,0:T(8,128)(2,1)S(1)}, u32[]{:S(2)}, u32[]{:S(2)}) collective-permute-start(bf16[64,4096]{1,0:T(8,128)(2,1)S(1)} %join.5.refs_1_), channel_id=1, source_target_pairs={{0,2},{2,0},{4,6},{6,4},{8,10},{10,8},{12,14},{14,12},{16,18},{18,... | collective-permute-start | bytes 1572872 | tf_op jit(solution)/shard_map/ppermute | solution.py:44
  59.4 8.5 %collective-permute-start.18 = (bf16[128,2048]{1,0:T(8,128)(2,1)S(1)}, bf16[128,2048]{1,0:T(8,128)(2,1)S(1)}, u32[]{:S(2)}, u32[]{:S(2)}) collective-permute-start(bf16[128,2048]{1,0:T(8,128)(2,1)S(1)} %join.7.refs_2_), channel_id=1, source_target_pairs={{0,2},{2,0},{4,6},{6,4},{8,10},{10,8},{12,14},{14,12},{16,18},{18,... | collective-permute-start | bytes 1572872 | tf_op jit(solution)/shard_map/ppermute | solution.py:44
  60.5 7.5 %collective-permute-start.20 = (f32[64,512]{1,0:T(8,128)S(1)}, f32[64,512]{1,0:T(8,128)S(1)}, u32[]{:S(2)}, u32[]{:S(2)}) collective-permute-start(f32[64,512]{1,0:T(8,128)S(1)} %get-tuple-element.68), channel_id=1, source_target_pairs={{0,1},{1,0},{2,3},{3,2},{4,5},{5,4},{6,7},{7,6},{8,9},{9,8},{10,11... | collective-permute-start | bytes 393224 | tf_op jit(solution)/shard_map/ppermute | solution.py:44

commit v4 on v3

--- a/solution.py
+++ b/solution.py
@@ -114,22 +114,24 @@
     return jax.ShapeDtypeStruct(dims, dtype)
 
 
-def open_kernel(stage, count, *refs):
+def open_kernel(stage, count, passed, *refs):
     sources, rest = refs[:count], refs[count:]
-    outs, scratch = rest[:13], rest[13:]
+    outs, scratch = rest[: 13 + passed], rest[13 + passed :]
+    outs, later = outs[:13], list(outs[13:])
     own_ref, sent_ref, run_ref, runt_ref, stept_ref, reach_ref, skip_out = outs[:7]
     q1_ref, q2_ref, vread_ref, vwrite_ref, tail_ref, owner_out = outs[7:]
-    extra_ref, sems, held = scratch[0], scratch[1], scratch[2:]
+    extra_ref, sems, held = scratch[0], scratch[1], [*scratch[2:], *later]
     fetches = [
         pltpu.make_async_copy(source, target, sems.at[k])
         for k, (source, target) in enumerate(zip(sources, held))
     ]
     for fetch in fetches:
         fetch.start()
-    for fetch in fetches[:-2]:
+    early = count - passed
+    for fetch in fetches[:early]:
         fetch.wait()
     turned_ref, rate_ref, skip_ref, owner_ref, ids_ref, kept_ref = held[:6]
-    din_ref, dgate_ref, dwrite_ref, dread_ref, dstep_ref, write_ref, x_ref = held[6:]
+    din_ref, dgate_ref, dwrite_ref, dread_ref, dstep_ref, write_ref, x_ref = held[6:13]
     heads, span = turned_ref.shape
     lanes = x_ref.shape[1]
     groups = write_ref.shape[1] // STATE_SIZE
@@ -227,7 +229,7 @@
         logs = jnp.concatenate(split(total_l, 3) + [jnp.zeros((5, wide), F32)], axis=0)
         extra_ref[:, at] = jnp.concatenate([mine, logs], axis=0).astype(BF16)
 
-    for fetch in fetches[-2:]:
+    for fetch in fetches[early : early + 2]:
         fetch.wait()
     half = lanes // 2
     chunk = min(wide, half)
@@ -242,6 +244,8 @@
             writes = write_ref[:, window(group * STATE_SIZE, STATE_SIZE)]
             writes = writes.astype(F32).T.astype(BF16)
             out_ref[:STATE_SIZE, at : at + chunk] = dot(writes, weighted).astype(BF16)
+    for fetch in fetches[early + 2 :]:
+        fetch.wait()
 
 
 def logs_of(block):
@@ -333,21 +337,27 @@
                 outs[k][STATE_SIZE:, at_out] = block[STATE_SIZE:]
 
 
-def intra_kernel(run_ref, runt_ref, stept_ref, skip_ref, x_ref, write_ref, read_ref, *refs):
-    out_ref = refs[-1]
-    span = x_ref.shape[0]
-    heads = runt_ref.shape[0]
+def intra_kernel(group, run_ref, runt_ref, stept_ref, skip_ref, x_ref, write_ref, read_ref, *refs):
+    fetch = None
+    out_ref = refs[0]
+    if len(refs) > 1:
+        source_ref, out_ref, held_ref, sem = refs
+        fetch = pltpu.make_async_copy(source_ref, held_ref, sem)
+        fetch.start()
+    span, heads = run_ref.shape[1:]
     mid = span // 2
-    scores = dot(read_ref[...], write_ref[...], ((1,), (1,)))
+    states = slice(group * STATE_SIZE, (group + 1) * STATE_SIZE)
+    scores = dot(read_ref[:, states], write_ref[:, states], ((1,), (1,)))
     row = lax.broadcasted_iota(jnp.int32, (mid, mid), 0)
     causal = row >= lax.broadcasted_iota(jnp.int32, (mid, mid), 1)
-    running = run_ref[0]
+    running = run_ref[group]
     low, high = slice(0, mid), slice(mid, span)
     for pair in range(heads // 2):
         found = []
-        for h in (2 * pair, 2 * pair + 1):
+        for k in (2 * pair, 2 * pair + 1):
+            h = group * heads + k
             x = x_ref[:, h * HEAD_DIM : (h + 1) * HEAD_DIM]
-            t_run, j_run = running[:, h : h + 1], runt_ref[h : h + 1, :]
+            t_run, j_run = running[:, k : k + 1], runt_ref[h : h + 1, :]
             step = stept_ref[h : h + 1, :]
 
             def mixed(rows, cols, masked):
@@ -360,88 +370,83 @@
             bottom = dot(mixed(high, low, False), x[low]) + dot(mixed(high, high, True), x[high])
             found.append(jnp.concatenate([top, bottom], axis=0))
         at = slice(pair * 2 * HEAD_DIM, (pair + 1) * 2 * HEAD_DIM)
+        lanes = slice((group * heads + 2 * pair) * HEAD_DIM, (group * heads + 2 * pair + 2) * HEAD_DIM)
         both = jnp.concatenate(found, axis=1)
-        out_ref[:, at] = both + skip_ref[:, at] * x_ref[:, at].astype(F32)
-
-
-def intra(run, runt, stept, skip, x, write, read, first, number, base, after):
-    span, lanes = x.shape
-    groups, _, per_group = run.shape
+        out_ref[:, at] = both + skip_ref[:, lanes] * x_ref[:, lanes].astype(F32)
+    if fetch is not None:
+        fetch.wait()
+
+
+def intra(group, run, runt, stept, skip, x, write, read, after, wanted=()):
+    span, per_group = run.shape[1:]
     wide = per_group * HEAD_DIM
-    args = [run, runt, stept, skip, x, write, read]
-    specs = [
-        pl.BlockSpec((1, span, per_group), lambda g: (g + first, 0, 0)),
-        pl.BlockSpec((per_group, span), lambda g: (g + first, 0)),
-        pl.BlockSpec((per_group, span), lambda g: (g + first, 0)),
-        pl.BlockSpec((1, wide), lambda g: (0, g + first)),
-        pl.BlockSpec((span, wide), lambda g: (0, g + first)),
-        pl.BlockSpec((span, STATE_SIZE), lambda g: (0, g + first)),
-        pl.BlockSpec((span, STATE_SIZE), lambda g: (0, g + first)),
-    ]
-    alias = {}
-    if base is not None:
-        alias = {len(args): 0}
-        args.append(base)
-        specs.append(ANYWHERE)
-    (base,) = call(
-        intra_kernel,
+    return call(
+        functools.partial(intra_kernel, group),
         "intra",
-        [shape((span, lanes), F32)],
-        args,
-        specs=specs,
-        out_specs=[pl.BlockSpec((span, wide), lambda g: (0, g + first))],
-        grid=(number,),
+        [shape((span, wide), F32)] + [shape(value.shape, value.dtype) for value in wanted],
+        (run, runt, stept, skip, x, write, read, *map(in_hbm, wanted)),
+        specs=[WHOLE] * 7 + [IN_HBM] * len(wanted),
+        scratch=[pltpu.SemaphoreType.DMA] * len(wanted),
         after=after,
-        alias=alias,
-        flops=number * per_group * span * span * HEAD_DIM * 2,
-        moved=number * wide * span * 6,
-        exps=number * per_group * span * span * 3 // 4,
-    )
-    return base
-
-
-def finish_kernel(stage, chunks, reach_ref, read_ref, own_ref, got_ref, base_ref, out_ref):
+        flops=per_group * span * span * HEAD_DIM * 2,
+        moved=wide * span * 6,
+        exps=per_group * span * span * 3 // 4,
+    )
+
+
+def finish_kernel(stage, reach_ref, read_ref, own_ref, got_ref, *refs):
+    base_refs, (out_ref, token_ref, held_ref, sems) = refs[:-4], refs[-4:]
+    token_ref[...] = jnp.zeros_like(token_ref)
     place = place_of(stage)
-    step = pl.program_id(0)
     heads = reach_ref.shape[1] // 2
-    chunk = out_ref.shape[1]
-    mine = place == lax.div(step, chunks // 2)
-    entering = jnp.where(mine, own_ref[:STATE_SIZE, :], got_ref[:STATE_SIZE, :])
-    inter = dot(read_ref[...], entering)
-    inter = inter * dot(reach_ref[...], head_mask(2 * heads, heads, chunk, step * chunk))
-    out_ref[...] = (inter + base_ref[...]).astype(BF16)
-
-
-def finish(stage, reach, read, own, got, base, after=()):
-    span, lanes = base.shape
-    wide = lanes // (read.shape[1] // STATE_SIZE)
+    lanes = held_ref.shape[1]
+    wide = lanes // len(base_refs)
     half = lanes // 2
-    chunk = min(512, half)
-    chunks, halves = lanes // chunk, half // chunk
-    entering = pl.BlockSpec((DOWN_ROWS, chunk), lambda c: (0, lax.rem(c, halves)))
+    chunk = lanes // sems.shape[0]
+    copies = []
+    for k, lane0 in enumerate(range(0, lanes, chunk)):
+        group, at = lane0 // wide, lane0 % half
+        at_in, at_out = slice(at, at + chunk), slice(lane0, lane0 + chunk)
+        entering = jnp.where(
+            place == lane0 // half, own_ref[:STATE_SIZE, at_in], got_ref[:STATE_SIZE, at_in]
+        )
+        inter = dot(read_ref[:, group * STATE_SIZE : (group + 1) * STATE_SIZE], entering)
+        inter = inter * dot(reach_ref[...], head_mask(2 * heads, heads, chunk, lane0))
+        base = base_refs[group][:, lane0 % wide : lane0 % wide + chunk]
+        held_ref[:, at_out] = (inter + base).astype(BF16)
+        copies.append(
+            pltpu.make_async_copy(held_ref.at[:, at_out], out_ref.at[:, at_out], sems.at[k])
+        )
+        copies[-1].start()
+    for copy in copies:
+        copy.wait()
+
+
+def finish(stage, reach, read, own, got, bases, after):
+    span = read.shape[0]
+    lanes = 2 * own.shape[1]
+    chunk = min(512, own.shape[1])
     return call(
-        functools.partial(finish_kernel, stage, chunks),
+        functools.partial(finish_kernel, stage),
         "finish",
-        [shape((span, lanes), BF16)],
-        (reach, read, own, got, base),
-        specs=[
-            pl.BlockSpec(reach.shape, lambda c: (0, 0)),
-            pl.BlockSpec((span, STATE_SIZE), lambda c: (0, lax.div(c * chunk, wide))),
-            entering,
-            entering,
-            pl.BlockSpec((span, chunk), lambda c: (0, c)),
-        ],
-        out_specs=[pl.BlockSpec((span, chunk), lambda c: (0, c))],
-        grid=(chunks,),
+        [shape((span, lanes), BF16), shape((8, 128), F32)],
+        (reach, read, own, got, *bases),
+        out_specs=[IN_HBM, WHOLE],
         after=after,
+        scratch=[pltpu.VMEM((span, lanes), BF16), pltpu.SemaphoreType.DMA((lanes // chunk,))],
         flops=2 * span * lanes * STATE_SIZE,
-    )[0]
+    )
 
 
 def resident_kernel(state_ref, vread_ref, q1_ref, q2_ref, gain_ref, out_ref):
-    drawn = dot(vread_ref[...], state_ref[...], ((1,), (1,)))
-    gated = q1_ref[...] + q2_ref[...] * drawn
-    out_ref[...] = normed(gated, gain_ref[...]).astype(BF16)
+    groups = vread_ref.shape[1] // STATE_SIZE
+    wide = state_ref.shape[0] // groups
+    for g in range(groups):
+        at = slice(g * wide, (g + 1) * wide)
+        reads = vread_ref[:, g * STATE_SIZE : (g + 1) * STATE_SIZE]
+        drawn = dot(reads, state_ref[at, :], ((1,), (1,)))
+        gated = q1_ref[:, at] + q2_ref[:, at] * drawn
+        out_ref[:, at] = normed(gated, gain_ref[:, at]).astype(BF16)
 
 
 def normed(gated, gain):
@@ -451,23 +456,11 @@
 
 def resident_hidden(state, vread, q1, q2, gain, after):
     lanes = state.shape[0]
-    groups = vread.shape[1] // STATE_SIZE
-    wide = lanes // groups
-    rows = pl.BlockSpec((DRAFTS, wide), lambda g: (0, g))
     return call(
         resident_kernel,
         "resident_hidden",
         [shape((DRAFTS, lanes), BF16)],
         (state, vread, q1, q2, gain),
-        specs=[
-            pl.BlockSpec((wide, STATE_SIZE), lambda g: (g, 0)),
-            pl.BlockSpec((DRAFTS, STATE_SIZE), lambda g: (0, g)),
-            rows,
-            rows,
-            pl.BlockSpec((1, wide), lambda g: (0, g)),
-        ],
-        out_specs=[rows],
-        grid=(groups,),
         after=after,
         flops=2 * DRAFTS * lanes * STATE_SIZE,
     )[0]
@@ -551,93 +544,84 @@
     )
 
 
-def states_kernel(stages, scattered, shares, *refs):
+def states_kernel(scattered, shares, *refs):
     owner_ref, resident_ref, own_ref, got_ref, tail_ref, vwrite_ref = refs[:6]
     share_refs = refs[6 : 6 + shares]
-    new_ref, slice_ref, verify_ref, turned_ref = refs[6 + shares :]
-    here, step = lax.axis_index("seq"), pl.program_id(0)
-
-    @pl.when(step == 0)
-    def _():
-        verify_ref[...] = sum(ref[...] for ref in share_refs).astype(BF16)
-
-    chunk = resident_ref.shape[0]
-    half = own_ref.shape[1]
+    new_ref, slice_ref, verify_ref, turned_ref, held_ref, sems = refs[6 + shares :]
+    here = lax.axis_index("seq")
+    verify_ref[...] = sum(ref[...] for ref in share_refs).astype(BF16)
+    lanes = resident_ref.shape[0]
+    half = lanes // 2
+    wide = lanes // (vwrite_ref.shape[1] // STATE_SIZE)
     blocks = [0]
     for factor, stride in reversed(scattered):
         blocks = [a | (k * stride) for k in range(factor) for a in blocks]
     width = half // len(blocks)
-    for at in range(0, chunk, width):
-        lane = step * chunk + at
-        spot, size = lax.div(lane, half), half
-        rest = lax.rem(lane, half)
-        for factor, stride in scattered:
-            size = size // factor
-            spot = spot | (lax.div(rest, size) * stride)
-            rest = lax.rem(rest, size)
-        offset = spot ^ here
-        position = jnp.int32(0)
-        for place, value in enumerate(blocks):
-            position = jnp.where((offset & sum_of(scattered)) == value, place, position)
-        found = jnp.where(
-            lax.rem(offset, 2) == 0,
-            own_ref[:, window(position * width, width)],
-            got_ref[:, window(position * width, width)],
-        )
-        turned_ref[at : at + width, :] = found.astype(F32).T
+    chunk = lanes // sems.shape[0]
+    is_owner = owner_ref[0:1, :STATE_SIZE] == here
+    row = lax.broadcasted_iota(jnp.int32, (32, STATE_SIZE), 0)
+    ones = jnp.where((row >= 24) & (row < 27), 1.0, 0.0)
+    copies = []
+    for part in range(sems.shape[0]):
+        rows = slice(part * chunk, (part + 1) * chunk)
+        for lane in range(part * chunk, (part + 1) * chunk, width):
+            spot, size, rest = lane // half, half, lane % half
+            for factor, stride in scattered:
+                size = size // factor
+                spot |= rest // size * stride
+                rest %= size
+            offset = spot ^ here
+            position = jnp.int32(0)
+            for place, value in enumerate(blocks):
+                position = jnp.where((offset & sum_of(scattered)) == value, place, position)
+            found = jnp.where(
+                lax.rem(offset, 2) == 0,
+                own_ref[:, window(position * width, width)],
+                got_ref[:, window(position * width, width)],
+            )
+            turned_ref[lane : lane + width, :] = found.astype(F32).T
+        group = part * chunk // wide
+        writes = vwrite_ref[:, group * STATE_SIZE : (group + 1) * STATE_SIZE].astype(F32)
+        writes = jnp.concatenate([writes, writes, writes, jnp.zeros_like(writes)], axis=0)
+        right = jnp.concatenate([writes, ones], axis=1).astype(BF16)
+        left = tail_ref[:, rows].astype(F32).T.astype(BF16)
+        both = dot(left, right)
+        start = jnp.where(is_owner, turned_ref[rows, :], resident_ref[rows, :].astype(F32))
+        held_ref[rows, :] = (start * both[:, STATE_SIZE:] + both[:, :STATE_SIZE]).astype(BF16)
+        copies.append(pltpu.make_async_copy(held_ref.at[rows, :], new_ref.at[rows, :], sems.at[part]))
+        copies[-1].start()
     per_slice = slice_ref.shape[1] // STATE_SIZE
     heads = slice_ref.shape[0]
     for k in range(per_slice):
         picked = turned_ref[pl.ds(here * per_slice + k, heads, stride=HEAD_DIM), :]
         slice_ref[:, k * STATE_SIZE : (k + 1) * STATE_SIZE] = picked.astype(BF16)
-    is_owner = owner_ref[0:1, :STATE_SIZE] == here
-    row = lax.broadcasted_iota(jnp.int32, (32, STATE_SIZE), 0)
-    ones = jnp.where((row >= 24) & (row < 27), 1.0, 0.0)
-    writes = vwrite_ref[...].astype(F32)
-    writes = jnp.concatenate([writes, writes, writes, jnp.zeros_like(writes)], axis=0)
-    right = jnp.concatenate([writes, ones], axis=1).astype(BF16)
-    left = tail_ref[...].astype(F32).T.astype(BF16)
-    both = dot(left, right)
-    start = jnp.where(is_owner, turned_ref[...], resident_ref[...].astype(F32))
-    new_ref[...] = (start * both[:, STATE_SIZE:] + both[:, :STATE_SIZE]).astype(BF16)
+    for copy in copies:
+        copy.wait()
 
 
 def sum_of(stages):
     return sum((factor - 1) * stride for factor, stride in stages)
 
 
-def states(stages, scattered, owner, resident, own, got, tail, vwrite, shares, seq_count):
+def states(scattered, owner, resident, own, got, tail, vwrite, shares, seq_count):
     lanes = resident.shape[0]
     wide = lanes // (vwrite.shape[1] // STATE_SIZE)
     chunk = min(512, wide)
-    heads = lanes // HEAD_DIM
-    rows, cols = shares[0].shape
-    fixed = pl.BlockSpec((rows, cols), lambda c: (0, 0))
     return call(
-        functools.partial(states_kernel, stages, scattered, len(shares)),
+        functools.partial(states_kernel, scattered, len(shares)),
         "states",
         [
             shape((lanes, STATE_SIZE), BF16),
-            shape((heads, HEAD_DIM // seq_count * STATE_SIZE), BF16),
-            shape((rows, cols), BF16),
+            shape((lanes // HEAD_DIM, HEAD_DIM // seq_count * STATE_SIZE), BF16),
+            shape(shares[0].shape, BF16),
         ],
         (owner, resident, own, got, tail, vwrite, *shares),
-        specs=[
-            WHOLE,
-            pl.BlockSpec((chunk, STATE_SIZE), lambda c: (c, 0)),
-            WHOLE,
-            WHOLE,
-            pl.BlockSpec((32, chunk), lambda c: (0, c)),
-            pl.BlockSpec((DRAFTS, STATE_SIZE), lambda c: (0, lax.div(c * chunk, wide))),
-        ]
-        + [WHOLE] * len(shares),
-        out_specs=[
-            pl.BlockSpec((chunk, STATE_SIZE), lambda c: (c, 0)),
-            pl.BlockSpec((chunk // HEAD_DIM, HEAD_DIM // seq_count * STATE_SIZE), lambda c: (c, 0)),
-            fixed,
+        out_specs=[IN_HBM, WHOLE, WHOLE],
+        scratch=[
+            pltpu.VMEM((lanes, STATE_SIZE), F32),
+            pltpu.VMEM((lanes, STATE_SIZE), BF16),
+            pltpu.SemaphoreType.DMA((lanes // chunk,)),
         ],
-        grid=(lanes // chunk,),
-        scratch=[pltpu.VMEM((chunk, STATE_SIZE), F32)],
         flops=2 * lanes * STATE_SIZE * 64,
     )
 
@@ -677,11 +661,12 @@
 
     inputs = (
         prefill_step.T, rate, skip, owner_slot, draft_ids.T, accepted_len, draft_input, draft_gate,
-        draft_write, draft_read, draft_step, write_proj, prefill_input,
-    )
+        draft_write, draft_read, draft_step, write_proj, prefill_input, read_proj, resident, gain,
+    )
+    passed = 5
     inputs = [in_hbm(value) for value in inputs]
     opened = call(
-        functools.partial(open_kernel, core, len(inputs)),
+        functools.partial(open_kernel, core, len(inputs), passed),
         "open_block",
         [
             shape((UP_ROWS, half), BF16),
@@ -697,34 +682,32 @@
             shape((DRAFTS, groups * STATE_SIZE), BF16),
             shape((32, lanes), BF16),
             shape((DRAFTS, out_weight.shape[1]), jnp.int32),
-        ],
+        ]
+        + [shape(value.shape, value.dtype) for value in inputs[-passed:]],
         inputs,
         specs=[IN_HBM] * len(inputs),
         scratch=[pltpu.VMEM((EXTRA, lanes), BF16), pltpu.SemaphoreType.DMA((len(inputs),))]
         + [
             (pltpu.SMEM if value.dtype == jnp.int32 else pltpu.VMEM)(value.shape, value.dtype)
-            for value in inputs
+            for value in inputs[:-passed]
         ],
         flops=2 * span * lanes * STATE_SIZE * 2,
     )
-    prefill_input, write_proj, read_proj, resident, gain = (
-        in_hbm(value) for value in (prefill_input, write_proj, read_proj, resident, gain)
-    )
-    own, sent, run, runt, stept, reach, skip_lanes, q1, q2, vread, vwrite, tail, owner = opened
+    own, sent, run, runt, stept, reach, skip_lanes, q1, q2, vread, vwrite, tail, owner = opened[:13]
+    writes, x, reads, resident, gain = opened[13:]
     core_parts = [own, swap(sent, "seq", core, 1)]
 
-    number = max(1, groups // 4)
-    firsts = list(range(0, groups, number))
-    base = None
+    bases, fetched = [], []
 
     def fill(after):
-        nonlocal base
-        if firsts:
-            base = intra(
-                run, runt, stept, skip_lanes, prefill_input, write_proj, read_proj, firsts.pop(0), number,
-                base, after,
+        if len(bases) < groups:
+            wanted = [] if bases else [out_weight]
+            base, *found = intra(
+                len(bases), run, runt, stept, skip_lanes, x, writes, reads, after, wanted
             )
-        return [base]
+            bases.append(base)
+            fetched.extend(found)
+        return bases[-1:]
 
     def exchange(parts, stage):
         got = {k: swap(parts[k], "seq", stage, k) for k in range(stage[0] - 1, 0, -1)}
@@ -753,8 +736,7 @@
     )
     last_parts = exchange(outs if split_last else outs * last[0], last)
     hiddens = exchange([hidden] * line[0], line)
-    fill([outs[-1]])
-    filled = fill([])
+    filled = fill([outs[-1]]) + fill(bases[-1:])
     *outs, prompt = call(
         functools.partial(top_kernel, last, last[0]),
         "top",
@@ -780,31 +762,29 @@
     filled = fill([outs[-1]])
     scattered = [line, last] if split_last else [line]
     if split_last:
-        prompts = exchange([prompt] * last[0], last)
+        prompt = join(exchange([prompt] * last[0], last), 1)
     outs = call(
         functools.partial(down_kernel, core, line, line[0], 2, False),
         "down_core",
         [shape((DOWN_ROWS, half), BF16)] * 2,
         pieces + core_parts,
-        after=filled,
+        after=filled + [prompt],
         flops=half * UP_ROWS * 8,
     )
-    if split_last:
-        prompt = join(prompts, 1, [outs[-1]])
     entering = exchange(outs, core)
-    while firsts:
+    while len(bases) < groups:
         fill([])
-    prefill_out = finish(core, reach, read_proj, *entering, base)
 
     shares = project(
-        stages, owner, hidden, swap(hidden, "seq", core, 1), *entering, norm_gain[None], out_weight, head_count
-    )
+        stages, owner, hidden, swap(hidden, "seq", core, 1), *entering, gain, fetched[0], head_count
+    )
+    prefill_out, token = finish(core, reach, reads, *entering, bases, shares[:1])
     shares = [shares[0]] + [swap(shares[k], "head", (head_count, 1), k) for k in range(1, head_count)]
 
-    prompt = join(exchange([prompt] * line[0], line), 1)
+    prompt = join(exchange([prompt] * line[0], line), 1, [token, *shares[1:]])
     prompts = exchange([prompt] * 2, core)
     new_state, state_slice, verify_out = states(
-        stages, scattered, owner, resident, *prompts, tail, vwrite, shares, seq_count
+        scattered, owner, resident, *prompts, tail, vwrite, shares, seq_count
     )
     return (
         prefill_out,

time: 74.9 us -> 66.6 us (0.89)
  Pallas kernels: 33 us -> 20.6 us
  waiting for transfers between devices: 13.8 us -> 19.3 us
  starting transfers between devices: 26.6 us -> 25.7 us
    pallas_call x18, Pallas kernels: 33 us -> 20.6 us  [call(): pl.pallas_call(ordered(kernel, first), name=name, grid=grid, out_shape=ou...]
    ppermute x21, waiting for transfers between devices: 13.8 us -> 19.3 us  [swap(): lax.ppermute(value, axis, [(k, k ^ offset * stride) for k in range(count)])]
    ppermute x21, starting transfers between devices: 26.6 us -> 25.7 us  [swap(): lax.ppermute(value, axis, [(k, k ^ offset * stride) for k in range(count)])]
  transfers between devices with their start and end apart: 21 -> 21, of which waited for: 7 -> 9; matrix products, arithmetic and copies ran while one was open for 0% -> 0% of each run, Pallas kernels for 29% -> 19%
where the time goes in v4:
time: 66.6 us; the launch traced here: 66.5 us
  starting transfers between devices  25.7 us (39%)
  Pallas kernels  20.6 us (31%)
  waiting for transfers between devices  19.3 us (29%)
  between operations  0.82 us (1%)
    ppermute x21, starting transfers between devices, swap(): lax.ppermute(value, axis, [(k, k ^ offset * stride) for k in range(count)])  25.7 us
    pallas_call x18, Pallas kernels, call(): pl.pallas_call(ordered(kernel, first), name=name, grid=grid, out_shape=ou...  20.6 us
    ppermute x21, waiting for transfers between devices, swap(): lax.ppermute(value, axis, [(k, k ^ offset * stride) for k in range(count)])  19.3 us
  transfers between devices with their start and end apart: 21, of which 9 were waited for; matrix products, arithmetic and copies ran while one was open for 0% of the time, Pallas kernels for 19%

profile of v4, /device:TPU:0, one launch (start us, length us, event | category | flops | bytes accessed | tf_op | source)
XLA Modules:
  0.0 66.5 jit_solution(11773854728628865895)
XLA Ops:
  0.6 4.3 %open_block.1 = (bf16[160,2048]{1,0:T(8,128)(2,1)S(1)}, bf16[160,2048]{1,0:T(8,128)(2,1)S(1)}, f32[4,256,16]{2,1,0:T(8,128)S(1)}, f32[64,256]{1,0:T(8,128)S(1)},...) custom-call(f32[64,256]{1,0:T(8,128)} %bitcast.8, ...), custom_call_target="tpu_custom_call" | custom-call | flops 536870912 | bytes 9884800 | tf_op jit(solution)/shard_map/open_block/pallas_call | solution.py:95
  5.5 1.7 %collective-permute-done.refs_1_.refs_5_ = bf16[160,2048]{1,0:T(8,128)(2,1)S(1)} collective-permute-done((bf16[160,2048]{1,0:T(8,128)(2,1)S(1)}, bf16[160,2048]{1,0:T(8,128)(2,1)S(1)}, u32[]{:S(2)}, u32[]{:S(2)}) %collective-permute-start) | collective-permute-done | bytes 655392 | tf_op jit(solution)/shard_map/ppermute | solution.py:44
  7.5 3.0 %collective-permute-start.6 = (bf16[160,1024]{1,0:T(8,128)(2,1)S(1)}, bf16[160,1024]{1,0:T(8,128)(2,1)S(1)}, u32[]{:S(2)}, u32[]{:S(2)}) collective-permute-start(bf16[160,1024]{1,0:T(8,128)(2,1)S(1)} %get-tuple-element.50.refs_0_), channel_id=1, source_target_pairs={{0,4},{2,6},{4,0},{6,2},{8,12},{10,14},{12,8},{14,10},{16,20},{18,... | collective-permute-start | bytes 983048 | tf_op jit(solution)/shard_map/ppermute | solution.py:44
  10.9 1.6 %collective-permute-start.1 = (bf16[8,4096]{1,0:T(8,128)(2,1)S(1)}, bf16[8,4096]{1,0:T(8,128)(2,1)S(1)}, u32[]{:S(2)}, u32[]{:S(2)}) collective-permute-start(bf16[8,4096]{1,0:T(8,128)(2,1)S(1)} %resident_hidden.1.refs_0_), channel_id=1, source_target_pairs={{0,8},{2,10},{4,12},{6,14},{8,0},{10,2},{12,4},{14,6},{16,24},{18,... | collective-permute-start | bytes 196616 | tf_op jit(solution)/shard_map/ppermute | solution.py:44
  12.5 2.6 %collective-permute-start.2 = (bf16[8,4096]{1,0:T(8,128)(2,1)S(1)}, bf16[8,4096]{1,0:T(8,128)(2,1)S(1)}, u32[]{:S(2)}, u32[]{:S(2)}) collective-permute-start(bf16[8,4096]{1,0:T(8,128)(2,1)S(1)} %resident_hidden.1.refs_0_), channel_id=1, source_target_pairs={{0,16},{2,18},{4,20},{6,22},{8,24},{10,26},{12,28},{14,30},{16,0},... | collective-permute-start | bytes 196616 | tf_op jit(solution)/shard_map/ppermute | solution.py:44
  15.3 4.5 %collective-permute-done.2.refs_2_ = bf16[8,4096]{1,0:T(8,128)(2,1)S(1)} collective-permute-done((bf16[8,4096]{1,0:T(8,128)(2,1)S(1)}, bf16[8,4096]{1,0:T(8,128)(2,1)S(1)}, u32[]{:S(2)}, u32[]{:S(2)}) %collective-permute-start.2) | collective-permute-done | bytes 65568 | tf_op jit(solution)/shard_map/ppermute | solution.py:44
  22.1 2.3 %collective-permute-start.8 = (bf16[160,256]{1,0:T(8,128)(2,1)S(1)}, bf16[160,256]{1,0:T(8,128)(2,1)S(1)}, u32[]{:S(2)}, u32[]{:S(2)}) collective-permute-start(bf16[160,256]{1,0:T(8,128)(2,1)S(1)} %get-tuple-element.68), channel_id=1, source_target_pairs={{0,16},{2,18},{4,20},{6,22},{8,24},{10,26},{12,28},{14,30},{16,0},... | collective-permute-start | bytes 245768 | tf_op jit(solution)/shard_map/ppermute | solution.py:44
  24.4 2.0 %collective-permute-start.9 = (bf16[160,256]{1,0:T(8,128)(2,1)S(1)}, bf16[160,256]{1,0:T(8,128)(2,1)S(1)}, u32[]{:S(2)}, u32[]{:S(2)}) collective-permute-start(bf16[160,256]{1,0:T(8,128)(2,1)S(1)} %get-tuple-element.57.refs_0_), channel_id=1, source_target_pairs={{0,24},{2,26},{4,28},{6,30},{8,16},{10,18},{12,20},{14,22},{16,8},... | collective-permute-start | bytes 245768 | tf_op jit(solution)/shard_map/ppermute | solution.py:44
  26.4 3.6 %intra.4 = (f32[256,1024]{1,0:T(8,128)S(1)}, bf16[4096,512]{1,0:T(8,128)(2,1)S(1)}) custom-call(bf16[160,256]{1,0:T(8,128)(2,1)S(1)} %get-tuple-element.57.refs_0_, f32[4,256,16]{2,1,0:T(8,128)S(1)} %get-tuple-element.58.refs_1_, f32[64,256]{1,0:T(8,128)S(1)} %get-tuple-element.59.refs_2_, f32[64,256]{1,0:T(8,128)S(1)} %get-tuple-element.60.refs_3_, ...), custom_call_target="tpu_custom_call" | custom-call | flops 134217728 | bytes 1572864 | tf_op jit(solution)/shard_map/intra/pallas_call | solution.py:95
  30.1 1.6 %intra.5.refs_1_.refs_6_ = f32[256,1024]{1,0:T(8,128)S(1)} custom-call(f32[256,1024]{1,0:T(8,128)S(1)} %get-tuple-element.65.refs_0_.refs_5_, f32[4,256,16]{2,1,0:T(8,128)S(1)} %get-tuple-element.58.refs_1_, f32[64,256]{1,0:T(8,128)S(1)} %get-tuple-element.59.refs_2_, f32[64,256]{1,0:T(8,128)S(1)} %get-tuple-element.60.refs_3_, ...), custom_call_target="tpu_custom_call" | custom-call | flops 134217728 | bytes 1572864 | tf_op jit(solution)/shard_map/intra/pallas_call | solution.py:95
  32.3 2.2 %collective-permute-start.11 = (bf16[144,256]{1,0:T(8,128)(2,1)S(1)}, bf16[144,256]{1,0:T(8,128)(2,1)S(1)}, u32[]{:S(2)}, u32[]{:S(2)}) collective-permute-start(bf16[144,256]{1,0:T(8,128)(2,1)S(1)} %get-tuple-element.72), channel_id=1, source_target_pairs={{0,16},{2,18},{4,20},{6,22},{8,24},{10,26},{12,28},{14,30},{16,0},... | collective-permute-start | bytes 221192 | tf_op jit(solution)/shard_map/ppermute | solution.py:44
  34.5 2.0 %collective-permute-start.12 = (bf16[144,256]{1,0:T(8,128)(2,1)S(1)}, bf16[144,256]{1,0:T(8,128)(2,1)S(1)}, u32[]{:S(2)}, u32[]{:S(2)}) collective-permute-start(bf16[144,256]{1,0:T(8,128)(2,1)S(1)} %get-tuple-element.69.refs_0_), channel_id=1, source_target_pairs={{0,24},{2,26},{4,28},{6,30},{8,16},{10,18},{12,20},{14,22},{16,8},... | collective-permute-start | bytes 221192 | tf_op jit(solution)/shard_map/ppermute | solution.py:44
  36.6 1.6 %intra.6.refs_0_.refs_7_ = f32[256,1024]{1,0:T(8,128)S(1)} custom-call(bf16[144,256]{1,0:T(8,128)(2,1)S(1)} %get-tuple-element.69.refs_0_, f32[4,256,16]{2,1,0:T(8,128)S(1)} %get-tuple-element.58.refs_1_, f32[64,256]{1,0:T(8,128)S(1)} %get-tuple-element.59.refs_2_, f32[64,256]{1,0:T(8,128)S(1)} %get-tuple-element.60.refs_3_, ...), custom_call_target="tpu_custom_call" | custom-call | flops 134217728 | bytes 1572864 | tf_op jit(solution)/shard_map/intra/pallas_call | solution.py:95
  38.2 2.4 %collective-permute-done.12.refs_5_ = bf16[144,256]{1,0:T(8,128)(2,1)S(1)} collective-permute-done((bf16[144,256]{1,0:T(8,128)(2,1)S(1)}, bf16[144,256]{1,0:T(8,128)(2,1)S(1)}, u32[]{:S(2)}, u32[]{:S(2)}) %collective-permute-start.12) | collective-permute-done | bytes 73760 | tf_op jit(solution)/shard_map/ppermute | solution.py:44
  41.0 1.7 %collective-permute-start.16 = (bf16[144,1024]{1,0:T(8,128)(2,1)S(1)}, bf16[144,1024]{1,0:T(8,128)(2,1)S(1)}, u32[]{:S(2)}, u32[]{:S(2)}) collective-permute-start(bf16[144,1024]{1,0:T(8,128)(2,1)S(1)} %get-tuple-element.74.refs_0_), channel_id=1, source_target_pairs={{0,4},{2,6},{4,0},{6,2},{8,12},{10,14},{12,8},{14,10},{16,20},{18,... | collective-permute-start | bytes 884744 | tf_op jit(solution)/shard_map/ppermute | solution.py:44
  42.6 3.2 %collective-permute-start.14 = (bf16[128,256]{1,0:T(8,128)(2,1)S(1)}, bf16[128,256]{1,0:T(8,128)(2,1)S(1)}, u32[]{:S(2)}, u32[]{:S(2)}) collective-permute-start(bf16[128,256]{1,0:T(8,128)(2,1)S(1)} %get-tuple-element.75.refs_0_), channel_id=1, source_target_pairs={{0,16},{2,18},{4,20},{6,22},{8,24},{10,26},{12,28},{14,30},{16,0},... | collective-permute-start | bytes 196616 | tf_op jit(solution)/shard_map/ppermute | solution.py:44
  47.0 1.6 %intra.7.refs_0_.refs_8_ = f32[256,1024]{1,0:T(8,128)S(1)} custom-call(bf16[144,1024]{1,0:T(8,128)(2,1)S(1)} %get-tuple-element.74.refs_0_, f32[4,256,16]{2,1,0:T(8,128)S(1)} %get-tuple-element.58.refs_1_, f32[64,256]{1,0:T(8,128)S(1)} %get-tuple-element.59.refs_2_, f32[64,256]{1,0:T(8,128)S(1)} %get-tuple-element.60.refs_3_, ...), custom_call_target="tpu_custom_call" | custom-call | flops 134217728 | bytes 1572864 | tf_op jit(solution)/shard_map/intra/pallas_call | solution.py:95
  48.7 3.3 %collective-permute-done.15.refs_3_ = bf16[128,256]{1,0:T(8,128)(2,1)S(1)} collective-permute-done((bf16[128,256]{1,0:T(8,128)(2,1)S(1)}, bf16[128,256]{1,0:T(8,128)(2,1)S(1)}, u32[]{:S(2)}, u32[]{:S(2)}) %collective-permute-start.15) | collective-permute-done | bytes 65568 | tf_op jit(solution)/shard_map/ppermute | solution.py:44
  53.4 2.2 %collective-permute-done.5.refs_2_ = bf16[64,4096]{1,0:T(8,128)(2,1)S(1)} collective-permute-done((bf16[64,4096]{1,0:T(8,128)(2,1)S(1)}, bf16[64,4096]{1,0:T(8,128)(2,1)S(1)}, u32[]{:S(2)}, u32[]{:S(2)}) %collective-permute-start.5) | collective-permute-done | bytes 524320 | tf_op jit(solution)/shard_map/ppermute | solution.py:44
  56.5 1.6 %collective-permute-start.18 = (f32[64,512]{1,0:T(8,128)S(1)}, f32[64,512]{1,0:T(8,128)S(1)}, u32[]{:S(2)}, u32[]{:S(2)}) collective-permute-start(f32[64,512]{1,0:T(8,128)S(1)} %get-tuple-element.84), channel_id=1, source_target_pairs={{0,1},{1,0},{2,3},{3,2},{4,5},{5,4},{6,7},{7,6},{8,9},{9,8},{10,11... | collective-permute-start | bytes 393224 | tf_op jit(solution)/shard_map/ppermute | solution.py:44
  58.0 2.0 %finish.1 = (bf16[256,4096]{1,0:T(8,128)(2,1)}, f32[8,128]{1,0:T(8,128)S(1)}) custom-call(f32[64,512]{1,0:T(8,128)S(1)} %get-tuple-element.80.refs_0_.refs_6_, bf16[256,128]{1,0:T(8,128)(2,1)S(1)} %get-tuple-element.81.refs_1_, bf16[256,512]{1,0:T(8,128)(2,1)S(1)} %get-tuple-element.64.refs_7_.refs_2_, bf16[144,2048]{1,0:T(8,128)(2,1)S(1)} %get-tuple-element.77.refs_3_, ...), custom_call_target="tpu_custom_call" | custom-call | flops 268435456 | bytes 7802880 | tf_op jit(solution)/shard_map/finish/pallas_call | solution.py:95
  60.1 1.5 %collective-permute-done.19.refs_3_ = bf16[128,1024]{1,0:T(8,128)(2,1)S(1)} collective-permute-done((bf16[128,1024]{1,0:T(8,128)(2,1)S(1)}, bf16[128,1024]{1,0:T(8,128)(2,1)S(1)}, u32[]{:S(2)}, u32[]{:S(2)}) %collective-permute-start.19) | collective-permute-done | bytes 262176 | tf_op jit(solution)/shard_map/ppermute | solution.py:44
  62.2 1.9 %collective-permute-done.20.refs_3_ = bf16[128,2048]{1,0:T(8,128)(2,1)S(1)} collective-permute-done((bf16[128,2048]{1,0:T(8,128)(2,1)S(1)}, bf16[128,2048]{1,0:T(8,128)(2,1)S(1)}, u32[]{:S(2)}, u32[]{:S(2)}) %collective-permute-start.20) | collective-permute-done | bytes 524320 | tf_op jit(solution)/shard_map/ppermute | solution.py:44
  64.1 2.4 %states.1 = (bf16[4096,128]{1,0:T(8,128)(2,1)}, bf16[64,512]{1,0:T(8,128)(2,1)}, bf16[64,512]{1,0:T(8,128)(2,1)}) custom-call(s32[8,512]{1,0:T(8,128)S(1)} %get-tuple-element.47.refs_0_, bf16[4096,128]{1,0:T(8,128)(2,1)S(1)} %get-tuple-element.51.refs_1_, bf16[128,2048]{1,0:T(8,128)(2,1)S(1)} %join.7.refs_2_, ...), custom_call_target="tpu_custom_call" | custom-call | flops 67108864 | bytes 3825664 | tf_op jit(solution)/shard_map/states/pallas_call | solution.py:95
  (36 shorter events, 8.7 us)
Async XLA Ops:
  5.0 2.2 %collective-permute-start = (bf16[160,2048]{1,0:T(8,128)(2,1)S(1)}, bf16[160,2048]{1,0:T(8,128)(2,1)S(1)}, u32[]{:S(2)}, u32[]{:S(2)}) collective-permute-start(bf16[160,2048]{1,0:T(8,128)(2,1)S(1)} %get-tuple-element.49), channel_id=1, source_target_pairs={{0,2},{2,0},{4,6},{6,4},{8,10},{10,8},{12,14},{14,12},{16,18},{18,... | collective-permute-start | bytes 1966088 | tf_op jit(solution)/shard_map/ppermute | solution.py:44
  7.5 14.3 %collective-permute-start.6 = (bf16[160,1024]{1,0:T(8,128)(2,1)S(1)}, bf16[160,1024]{1,0:T(8,128)(2,1)S(1)}, u32[]{:S(2)}, u32[]{:S(2)}) collective-permute-start(bf16[160,1024]{1,0:T(8,128)(2,1)S(1)} %get-tuple-element.50.refs_0_), channel_id=1, source_target_pairs={{0,4},{2,6},{4,0},{6,2},{8,12},{10,14},{12,8},{14,10},{16,20},{18,... | collective-permute-start | bytes 983048 | tf_op jit(solution)/shard_map/ppermute | solution.py:44
  10.9 4.4 %collective-permute-start.1 = (bf16[8,4096]{1,0:T(8,128)(2,1)S(1)}, bf16[8,4096]{1,0:T(8,128)(2,1)S(1)}, u32[]{:S(2)}, u32[]{:S(2)}) collective-permute-start(bf16[8,4096]{1,0:T(8,128)(2,1)S(1)} %resident_hidden.1.refs_0_), channel_id=1, source_target_pairs={{0,8},{2,10},{4,12},{6,14},{8,0},{10,2},{12,4},{14,6},{16,24},{18,... | collective-permute-start | bytes 196616 | tf_op jit(solution)/shard_map/ppermute | solution.py:44
  12.5 7.3 %collective-permute-start.2 = (bf16[8,4096]{1,0:T(8,128)(2,1)S(1)}, bf16[8,4096]{1,0:T(8,128)(2,1)S(1)}, u32[]{:S(2)}, u32[]{:S(2)}) collective-permute-start(bf16[8,4096]{1,0:T(8,128)(2,1)S(1)} %resident_hidden.1.refs_0_), channel_id=1, source_target_pairs={{0,16},{2,18},{4,20},{6,22},{8,24},{10,26},{12,28},{14,30},{16,0},... | collective-permute-start | bytes 196616 | tf_op jit(solution)/shard_map/ppermute | solution.py:44
  15.1 6.1 %collective-permute-start.3 = (bf16[8,4096]{1,0:T(8,128)(2,1)S(1)}, bf16[8,4096]{1,0:T(8,128)(2,1)S(1)}, u32[]{:S(2)}, u32[]{:S(2)}) collective-permute-start(bf16[8,4096]{1,0:T(8,128)(2,1)S(1)} %resident_hidden.1.refs_0_), channel_id=1, source_target_pairs={{0,24},{2,26},{4,28},{6,30},{8,16},{10,18},{12,20},{14,22},{16,8},... | collective-permute-start | bytes 196616 | tf_op jit(solution)/shard_map/ppermute | solution.py:44
  21.2 15.3 %collective-permute-start.4 = (bf16[32,4096]{1,0:T(8,128)(2,1)S(1)}, bf16[32,4096]{1,0:T(8,128)(2,1)S(1)}, u32[]{:S(2)}, u32[]{:S(2)}) collective-permute-start(bf16[32,4096]{1,0:T(8,128)(2,1)S(1)} %join.4.refs_0_), channel_id=1, source_target_pairs={{0,4},{2,6},{4,0},{6,2},{8,12},{10,14},{12,8},{14,10},{16,20},{18,... | collective-permute-start | bytes 786440 | tf_op jit(solution)/shard_map/ppermute | solution.py:44
  22.0 9.7 %collective-permute-start.7 = (bf16[160,256]{1,0:T(8,128)(2,1)S(1)}, bf16[160,256]{1,0:T(8,128)(2,1)S(1)}, u32[]{:S(2)}, u32[]{:S(2)}) collective-permute-start(bf16[160,256]{1,0:T(8,128)(2,1)S(1)} %get-tuple-element.67), channel_id=1, source_target_pairs={{0,8},{2,10},{4,12},{6,14},{8,0},{10,2},{12,4},{14,6},{16,24},{18,... | collective-permute-start | bytes 245768 | tf_op jit(solution)/shard_map/ppermute | solution.py:44
  22.1 9.7 %collective-permute-start.8 = (bf16[160,256]{1,0:T(8,128)(2,1)S(1)}, bf16[160,256]{1,0:T(8,128)(2,1)S(1)}, u32[]{:S(2)}, u32[]{:S(2)}) collective-permute-start(bf16[160,256]{1,0:T(8,128)(2,1)S(1)} %get-tuple-element.68), channel_id=1, source_target_pairs={{0,16},{2,18},{4,20},{6,22},{8,24},{10,26},{12,28},{14,30},{16,0},... | collective-permute-start | bytes 245768 | tf_op jit(solution)/shard_map/ppermute | solution.py:44
  24.4 7.3 %collective-permute-start.9 = (bf16[160,256]{1,0:T(8,128)(2,1)S(1)}, bf16[160,256]{1,0:T(8,128)(2,1)S(1)}, u32[]{:S(2)}, u32[]{:S(2)}) collective-permute-start(bf16[160,256]{1,0:T(8,128)(2,1)S(1)} %get-tuple-element.57.refs_0_), channel_id=1, source_target_pairs={{0,24},{2,26},{4,28},{6,30},{8,16},{10,18},{12,20},{14,22},{16,8},... | collective-permute-start | bytes 245768 | tf_op jit(solution)/shard_map/ppermute | solution.py:44
  32.1 6.1 %collective-permute-start.10 = (bf16[144,256]{1,0:T(8,128)(2,1)S(1)}, bf16[144,256]{1,0:T(8,128)(2,1)S(1)}, u32[]{:S(2)}, u32[]{:S(2)}) collective-permute-start(bf16[144,256]{1,0:T(8,128)(2,1)S(1)} %get-tuple-element.71), channel_id=1, source_target_pairs={{0,8},{2,10},{4,12},{6,14},{8,0},{10,2},{12,4},{14,6},{16,24},{18,... | collective-permute-start | bytes 221192 | tf_op jit(solution)/shard_map/ppermute | solution.py:44
  32.3 5.9 %collective-permute-start.11 = (bf16[144,256]{1,0:T(8,128)(2,1)S(1)}, bf16[144,256]{1,0:T(8,128)(2,1)S(1)}, u32[]{:S(2)}, u32[]{:S(2)}) collective-permute-start(bf16[144,256]{1,0:T(8,128)(2,1)S(1)} %get-tuple-element.72), channel_id=1, source_target_pairs={{0,16},{2,18},{4,20},{6,22},{8,24},{10,26},{12,28},{14,30},{16,0},... | collective-permute-start | bytes 221192 | tf_op jit(solution)/shard_map/ppermute | solution.py:44
  34.5 6.2 %collective-permute-start.12 = (bf16[144,256]{1,0:T(8,128)(2,1)S(1)}, bf16[144,256]{1,0:T(8,128)(2,1)S(1)}, u32[]{:S(2)}, u32[]{:S(2)}) collective-permute-start(bf16[144,256]{1,0:T(8,128)(2,1)S(1)} %get-tuple-element.69.refs_0_), channel_id=1, source_target_pairs={{0,24},{2,26},{4,28},{6,30},{8,16},{10,18},{12,20},{14,22},{16,8},... | collective-permute-start | bytes 221192 | tf_op jit(solution)/shard_map/ppermute | solution.py:44
  41.0 11.0 %collective-permute-start.16 = (bf16[144,1024]{1,0:T(8,128)(2,1)S(1)}, bf16[144,1024]{1,0:T(8,128)(2,1)S(1)}, u32[]{:S(2)}, u32[]{:S(2)}) collective-permute-start(bf16[144,1024]{1,0:T(8,128)(2,1)S(1)} %get-tuple-element.74.refs_0_), channel_id=1, source_target_pairs={{0,4},{2,6},{4,0},{6,2},{8,12},{10,14},{12,8},{14,10},{16,20},{18,... | collective-permute-start | bytes 884744 | tf_op jit(solution)/shard_map/ppermute | solution.py:44
  42.6 6.0 %collective-permute-start.13 = (bf16[128,256]{1,0:T(8,128)(2,1)S(1)}, bf16[128,256]{1,0:T(8,128)(2,1)S(1)}, u32[]{:S(2)}, u32[]{:S(2)}) collective-permute-start(bf16[128,256]{1,0:T(8,128)(2,1)S(1)} %get-tuple-element.75.refs_0_), channel_id=1, source_target_pairs={{0,8},{2,10},{4,12},{6,14},{8,0},{10,2},{12,4},{14,6},{16,24},{18,... | collective-permute-start | bytes 196616 | tf_op jit(solution)/shard_map/ppermute | solution.py:44
  42.6 6.0 %collective-permute-start.14 = (bf16[128,256]{1,0:T(8,128)(2,1)S(1)}, bf16[128,256]{1,0:T(8,128)(2,1)S(1)}, u32[]{:S(2)}, u32[]{:S(2)}) collective-permute-start(bf16[128,256]{1,0:T(8,128)(2,1)S(1)} %get-tuple-element.75.refs_0_), channel_id=1, source_target_pairs={{0,16},{2,18},{4,20},{6,22},{8,24},{10,26},{12,28},{14,30},{16,0},... | collective-permute-start | bytes 196616 | tf_op jit(solution)/shard_map/ppermute | solution.py:44
  45.9 6.1 %collective-permute-start.15 = (bf16[128,256]{1,0:T(8,128)(2,1)S(1)}, bf16[128,256]{1,0:T(8,128)(2,1)S(1)}, u32[]{:S(2)}, u32[]{:S(2)}) collective-permute-start(bf16[128,256]{1,0:T(8,128)(2,1)S(1)} %get-tuple-element.75.refs_0_), channel_id=1, source_target_pairs={{0,24},{2,26},{4,28},{6,30},{8,16},{10,18},{12,20},{14,22},{16,8},... | collective-permute-start | bytes 196616 | tf_op jit(solution)/shard_map/ppermute | solution.py:44
  52.7 2.8 %collective-permute-start.17 = (bf16[144,2048]{1,0:T(8,128)(2,1)S(1)}, bf16[144,2048]{1,0:T(8,128)(2,1)S(1)}, u32[]{:S(2)}, u32[]{:S(2)}) collective-permute-start(bf16[144,2048]{1,0:T(8,128)(2,1)S(1)} %get-tuple-element.78), channel_id=1, source_target_pairs={{0,2},{2,0},{4,6},{6,4},{8,10},{10,8},{12,14},{14,12},{16,18},{18,... | collective-permute-start | bytes 1769480 | tf_op jit(solution)/shard_map/ppermute | solution.py:44
  52.8 2.7 %collective-permute-start.5 = (bf16[64,4096]{1,0:T(8,128)(2,1)S(1)}, bf16[64,4096]{1,0:T(8,128)(2,1)S(1)}, u32[]{:S(2)}, u32[]{:S(2)}) collective-permute-start(bf16[64,4096]{1,0:T(8,128)(2,1)S(1)} %join.5.refs_1_), channel_id=1, source_target_pairs={{0,2},{2,0},{4,6},{6,4},{8,10},{10,8},{12,14},{14,12},{16,18},{18,... | collective-permute-start | bytes 1572872 | tf_op jit(solution)/shard_map/ppermute | solution.py:44
  53.3 8.3 %collective-permute-start.19 = (bf16[128,1024]{1,0:T(8,128)(2,1)S(1)}, bf16[128,1024]{1,0:T(8,128)(2,1)S(1)}, u32[]{:S(2)}, u32[]{:S(2)}) collective-permute-start(bf16[128,1024]{1,0:T(8,128)(2,1)S(1)} %join.6.refs_1_.refs_2_), channel_id=1, source_target_pairs={{0,4},{2,6},{4,0},{6,2},{8,12},{10,14},{12,8},{14,10},{16,20},{18,... | collective-permute-start | bytes 786440 | tf_op jit(solution)/shard_map/ppermute | solution.py:44
  56.5 5.6 %collective-permute-start.18 = (f32[64,512]{1,0:T(8,128)S(1)}, f32[64,512]{1,0:T(8,128)S(1)}, u32[]{:S(2)}, u32[]{:S(2)}) collective-permute-start(f32[64,512]{1,0:T(8,128)S(1)} %get-tuple-element.84), channel_id=1, source_target_pairs={{0,1},{1,0},{2,3},{3,2},{4,5},{5,4},{6,7},{7,6},{8,9},{9,8},{10,11... | collective-permute-start | bytes 393224 | tf_op jit(solution)/shard_map/ppermute | solution.py:44
  62.1 2.0 %collective-permute-start.20 = (bf16[128,2048]{1,0:T(8,128)(2,1)S(1)}, bf16[128,2048]{1,0:T(8,128)(2,1)S(1)}, u32[]{:S(2)}, u32[]{:S(2)}) collective-permute-start(bf16[128,2048]{1,0:T(8,128)(2,1)S(1)} %join.7.refs_2_), channel_id=1, source_target_pairs={{0,2},{2,0},{4,6},{6,4},{8,10},{10,8},{12,14},{14,12},{16,18},{18,... | collective-permute-start | bytes 1572872 | tf_op jit(solution)/shard_map/ppermute | solution.py:44
